TPU v7x, 512 devices: a whole 4x8x8 slice. The times are simulated.
512 devices in a mesh: dp: 8 (over z), ctx: 64 (over y, x, core).
Axes of the slice: x: 4, y: 8, z: 8, core: 2. Of those that a mesh axis runs over, the one named last changes fastest.
Arguments:
- queries: bfloat16 [8, 8192, 2048], P('dp', 'ctx')
- keys: bfloat16 [8, 8192, 2048], P('dp', 'ctx')
- values: bfloat16 [8, 8192, 2048], P('dp', 'ctx'), may hold values from -6 to 6
- router_logit: float32 [8, 8192], P('dp', 'ctx'), may hold values from -8 to 8
- head_scale: float32 [16], replicated, may hold values from 0.5 to 2
- routed: int32 [8, 1024], P('dp'), may hold values from 0 to 8191, as said below
- grad_out: bfloat16 [8, 8192, 2048], P('dp', 'ctx'), may hold values from -6 to 6
Outputs:
- block_out: bfloat16 [8, 8192, 2048], P('dp', 'ctx')
- d_queries: bfloat16 [8, 8192, 2048], P('dp', 'ctx')
- d_keys: bfloat16 [8, 8192, 2048], P('dp', 'ctx')
- d_values: bfloat16 [8, 8192, 2048], P('dp', 'ctx')
- d_logit: float32 [8, 8192], P('dp', 'ctx')
- d_head_scale: float32 [16], replicated
Inputs may be any that keep to these rules, and one draw needn't show every extreme that they name: Each document's routed positions increase strictly. A shard of 128 positions (positions c * 128 to c * 128 + 127) holds 1 to 40 of them, and in every document some shard holds exactly 40.
All inputs are finite; a program needn't handle non-finite values.
Results may differ from a plain program's by a relative error of at most 0.011.
Values may be sent and summed in bfloat16 or wider, within the bound.
No kernel may reach another device: no remote copies, remote signals or barrier semaphores. Data moves between devices by JAX's collectives and lax.ppermute only.
A program may use at most 128 MiB of HBM per device.

v0:
```python
import math

import jax
import jax.numpy as jnp
from jax import lax
from jax.sharding import PartitionSpec as P


def body(queries, keys, values, router_logit, head_scale, routed, grad_out):
    nctx = lax.axis_size("ctx")
    here = lax.axis_index("ctx")
    tok = queries.shape[1]
    width = queries.shape[2]
    heads = head_scale.shape[0]
    hdim = width // heads
    inv = 1.0 / math.sqrt(hdim)
    coef = head_scale * inv
    places = routed[0]
    total = places.shape[0]
    rows = total // nctx
    per = (rows + 3 * (rows // 2) + nctx - 1) // nctx
    first = here * tok
    before = jnp.sum((places < first).astype(jnp.int32))
    owned = jnp.sum(((places >= first) & (places < first + tok)).astype(jnp.int32))
    slots = jnp.arange(nctx, dtype=jnp.int32)
    turns = jnp.arange(per, dtype=jnp.int32)
    offset = jnp.mod(slots[:, None] - before, nctx) + nctx * turns[None, :]
    filled = offset < owned
    which = jnp.minimum(before + offset, total - 1)
    local = jnp.clip(places[which] - first, 0, tok - 1)
    gate_all = jax.nn.sigmoid(router_logit[0])

    def pick(table):
        return jnp.where(filled[:, :, None], table[local], jnp.zeros((), table.dtype))

    send_grad = (gate_all[local][:, :, None] * grad_out[0][local].astype(jnp.float32)).astype(
        jnp.bfloat16
    )
    send_grad = jnp.where(filled[:, :, None], send_grad, jnp.zeros((), jnp.bfloat16))
    arrived = (
        lax.all_to_all(pick(queries[0]), "ctx", split_axis=0, concat_axis=0, tiled=True),
        lax.all_to_all(pick(keys[0]), "ctx", split_axis=0, concat_axis=0, tiled=True),
        lax.all_to_all(pick(values[0]), "ctx", split_axis=0, concat_axis=0, tiled=True),
        lax.all_to_all(send_grad, "ctx", split_axis=0, concat_axis=0, tiled=True),
    )
    my_rank = here + nctx * jnp.arange(rows, dtype=jnp.int32)
    my_pos = places[my_rank]
    source = my_pos // tok
    source_before = jnp.sum((places[None, :] < (source * tok)[:, None]).astype(jnp.int32), axis=1)
    turn = (my_rank - source_before) // nctx
    q_bal = arrived[0][source, turn]
    k_bal = arrived[1][source, turn]
    v_bal = arrived[2][source, turn]
    d_bal = arrived[3][source, turn]

    def split_heads(block):
        return block.reshape(block.shape[0], heads, hdim)

    def key_places(count):
        index = jnp.arange(count, dtype=jnp.int32)
        return places[index // rows + nctx * (index % rows)]

    gathered = (
        lax.all_gather(k_bal, "ctx", axis=0, tiled=True),
        lax.all_gather(v_bal, "ctx", axis=0, tiled=True),
    )
    all_keys = gathered[0]
    all_values = gathered[1]
    kept = key_places(total)[None, None, :] <= my_pos[None, :, None]
    scores = head_scale[:, None, None] * (
        jnp.einsum(
            "shd,khd->hsk",
            split_heads(q_bal),
            split_heads(all_keys),
            preferred_element_type=jnp.float32,
        )
        * inv
    )
    masked = jnp.where(kept, scores, -jnp.inf)
    top = jnp.max(masked, axis=-1, keepdims=True)
    lse = top + jnp.log(jnp.sum(jnp.exp(masked - top), axis=-1, keepdims=True))
    probs = jnp.where(kept, jnp.exp(masked - lse), 0.0)
    weights = probs.astype(jnp.bfloat16)
    attended = jnp.einsum(
        "hsk,khd->shd", weights, split_heads(all_values), preferred_element_type=jnp.float32
    )
    attended = attended.astype(jnp.bfloat16).reshape(rows, width)
    d_heads = split_heads(d_bal).astype(jnp.float32)
    delta = jnp.sum(d_heads * split_heads(attended).astype(jnp.float32), axis=-1)
    lse_rows = jnp.transpose(lse[:, :, 0], (1, 0))
    stats = (
        lax.all_gather(lse_rows, "ctx", axis=0, tiled=True),
        lax.all_gather(delta, "ctx", axis=0, tiled=True),
    )
    all_rows = (
        lax.all_gather(q_bal, "ctx", axis=0, tiled=True),
        lax.all_gather(d_bal, "ctx", axis=0, tiled=True),
    )
    q_piece = all_rows[0]
    d_piece = all_rows[1]
    count = q_piece.shape[0]
    piece_pos = key_places(count)
    lse_piece = stats[0]
    delta_piece = stats[1]
    kept = my_pos[None, :, None] <= piece_pos[None, None, :]
    raw = (
        jnp.einsum(
            "khd,nhd->hkn",
            split_heads(k_bal),
            split_heads(q_piece),
            preferred_element_type=jnp.float32,
        )
        * inv
    )
    key_probs = jnp.where(
        kept, jnp.exp(head_scale[:, None, None] * raw - lse_piece.T[:, None, :]), 0.0
    )
    d_probs = jnp.einsum(
        "khd,nhd->hkn", split_heads(v_bal), split_heads(d_piece), preferred_element_type=jnp.float32
    )
    d_scores = key_probs * (d_probs - delta_piece.T[:, None, :])
    dv_part = jnp.einsum(
        "hkn,nhd->khd",
        key_probs.astype(jnp.bfloat16),
        split_heads(d_piece),
        preferred_element_type=jnp.float32,
    )
    dk_part = jnp.einsum(
        "hkn,nhd->khd",
        d_scores.astype(jnp.bfloat16),
        split_heads(q_piece),
        preferred_element_type=jnp.float32,
    )
    scale_acc = jnp.sum(d_scores * raw, axis=(1, 2))
    d_probs = jnp.einsum(
        "shd,khd->hsk",
        split_heads(d_bal),
        split_heads(all_values),
        preferred_element_type=jnp.float32,
    )
    d_scores = probs * (d_probs - delta.T[:, :, None])
    dq_acc = jnp.einsum(
        "hsk,khd->shd",
        d_scores.astype(jnp.bfloat16),
        split_heads(all_keys),
        preferred_element_type=jnp.float32,
    )
    coef_heads = coef[None, :, None]
    d_q = (coef_heads * dq_acc).astype(jnp.bfloat16).reshape(rows, width)
    d_k = (coef_heads * dk_part).astype(jnp.bfloat16).reshape(rows, width)
    d_v = dv_part.astype(jnp.bfloat16).reshape(rows, width)
    matched = (source[None, None, :] == slots[:, None, None]) & (
        turn[None, None, :] == turns[None, :, None]
    )
    back_index = jnp.sum(
        jnp.where(matched, jnp.arange(rows, dtype=jnp.int32)[None, None, :], 0), axis=2
    )
    back_hit = jnp.any(matched, axis=2)

    def outgoing(block):
        return jnp.where(back_hit[:, :, None], block[back_index], jnp.zeros((), block.dtype))

    flat_local = local.reshape(nctx * per)
    flat_filled = filled.reshape(nctx * per)
    spread = (
        (jnp.arange(tok, dtype=jnp.int32)[:, None] == flat_local[None, :]) & flat_filled[None, :]
    ).astype(jnp.bfloat16)

    def place_home(block):
        flat = block.reshape(nctx * per, width)
        return jnp.dot(spread, flat, preferred_element_type=jnp.float32).astype(jnp.bfloat16)

    att_back = lax.all_to_all(outgoing(attended), "ctx", split_axis=0, concat_axis=0, tiled=True)
    grads = (
        lax.all_to_all(outgoing(d_q), "ctx", split_axis=0, concat_axis=0, tiled=True),
        lax.all_to_all(outgoing(d_k), "ctx", split_axis=0, concat_axis=0, tiled=True),
        lax.all_to_all(outgoing(d_v), "ctx", split_axis=0, concat_axis=0, tiled=True),
    )
    dq_back, dk_back, dv_back = grads
    att_home = place_home(att_back).astype(jnp.float32)
    block_out = (gate_all[:, None] * att_home).astype(jnp.bfloat16)
    d_logit = (
        gate_all * (1.0 - gate_all) * jnp.sum(grad_out[0].astype(jnp.float32) * att_home, axis=-1)
    )
    d_head_scale = lax.psum(scale_acc, ("dp", "ctx"))
    return (
        block_out[None],
        place_home(dq_back)[None],
        place_home(dk_back)[None],
        place_home(dv_back)[None],
        d_logit[None],
        d_head_scale,
    )


def solution(mesh):
    in_specs = (
        P("dp", "ctx", None),
        P("dp", "ctx", None),
        P("dp", "ctx", None),
        P("dp", "ctx"),
        P(),
        P("dp", None),
        P("dp", "ctx", None),
    )
    out_specs = (
        P("dp", "ctx", None),
        P("dp", "ctx", None),
        P("dp", "ctx", None),
        P("dp", "ctx", None),
        P("dp", "ctx"),
        P(),
    )
    return jax.shard_map(body, mesh=mesh, in_specs=in_specs, out_specs=out_specs, check_vma=False)
```

profile of v0, /device:TPU:1, one launch (start us, length us, event | category | flops | bytes accessed | tf_op | source)
XLA Modules:
  0.0 560.0 jit_solution(13016982971042493739)
XLA Ops:
  17.3 11.6 %all-to-all-start.2 = ((bf16[64,2,1024]{2,1,0:T(2,128)(2,1)}), bf16[64,2,1024]{2,1,0:T(2,128)(2,1)S(1)}, u32[]{:S(2)}, u32[]{:S(2)}) async-start(bf16[64,2,1024]{2,1,0:T(2,128)(2,1)} %reshape.1058), calls=%async_computation.2 | async-start | bytes 524288 | tf_op jit(solution)/shard_map/all_to_all | solution.py:42
  29.9 12.2 %all-to-all-done.2 = bf16[64,2,1024]{2,1,0:T(2,128)(2,1)S(1)} async-done(((bf16[64,2,1024]{2,1,0:T(2,128)(2,1)}), bf16[64,2,1024]{2,1,0:T(2,128)(2,1)S(1)}, u32[]{:S(2)}, u32[]{:S(2)}) %all-to-all-start.2) | async-done | bytes 262176 | tf_op jit(solution)/shard_map/all_to_all | solution.py:42
  44.9 17.7 %all_to_all.40 = bf16[64,2,1024]{2,1,0:T(2,128)(2,1)S(1)} all-to-all(bf16[64,2,1024]{2,1,0:T(2,128)(2,1)S(1)} %reshape.1056), channel_id=1, replica_groups=mesh['dp'=8,'ctx'=64] {'ctx'}, dimensions={0} | all-to-all | bytes 524288 | tf_op jit(solution)/shard_map/all_to_all | solution.py:43
  65.4 17.8 %all_to_all.41 = bf16[64,2,1024]{2,1,0:T(2,128)(2,1)S(1)} all-to-all(bf16[64,2,1024]{2,1,0:T(2,128)(2,1)S(1)} %reshape.1060), channel_id=1, replica_groups=mesh['dp'=8,'ctx'=64] {'ctx'}, dimensions={0} | all-to-all | bytes 524288 | tf_op jit(solution)/shard_map/all_to_all | solution.py:41
  85.0 4.5 gather_fusion.4
  90.5 37.5 %all-gather.7.cloned.1.call-done = bf16[1024,2048]{1,0:T(8,128)(2,1)} async-done(((bf16[16,2048]{1,0:T(8,128)(2,1)}), bf16[1024,2048]{1,0:T(8,128)(2,1)}) %all-gather.7.cloned.1.call-update) | async-done | bytes 4194320 | tf_op jit(solution)/shard_map/all_gather | solution.py:64
  128.0 6.4 %copy.155 = bf16[1024,2048]{0,1:T(8,128)(2,1)} copy(bf16[1024,2048]{1,0:T(8,128)(2,1)} %all-gather.7.cloned.1.call-done) | data formatting | bytes 8388608 | tf_op jit(solution)/shard_map/all_gather | solution.py:64
  134.4 79.5 %all-gather.5.cloned.1.call-done = bf16[1024,2048]{1,0:T(8,128)(2,1)} async-done(((bf16[16,2048]{1,0:T(8,128)(2,1)}), bf16[1024,2048]{1,0:T(8,128)(2,1)}) %all-gather.5.cloned.1.call-update) | async-done | bytes 4194320 | tf_op jit(solution)/shard_map/all_gather | solution.py:65
  213.8 6.4 %copy.150 = bf16[1024,2048]{0,1:T(8,128)(2,1)} copy(bf16[1024,2048]{1,0:T(8,128)(2,1)} %all-gather.5.cloned.1.call-done) | data formatting | bytes 8388608 | tf_op jit(solution)/shard_map/all_gather | solution.py:65
  227.5 6.2 %all-to-all-start.3 = ((bf16[64,2,1024]{2,1,0:T(2,128)(2,1)}), bf16[64,2,1024]{2,1,0:T(2,128)(2,1)S(1)}, u32[]{:S(2)}, u32[]{:S(2)}) async-start(bf16[64,2,1024]{2,1,0:T(2,128)(2,1)} %reshape.1062), calls=%async_computation.3 | async-start | bytes 524288 | tf_op jit(solution)/shard_map/all_to_all | solution.py:173
  234.6 12.1 %all-to-all-done.3 = bf16[64,2,1024]{2,1,0:T(2,128)(2,1)S(1)} async-done(((bf16[64,2,1024]{2,1,0:T(2,128)(2,1)}), bf16[64,2,1024]{2,1,0:T(2,128)(2,1)S(1)}, u32[]{:S(2)}, u32[]{:S(2)}) %all-to-all-start.3) | async-done | bytes 262176 | tf_op jit(solution)/shard_map/all_to_all | solution.py:173
  251.6 18.5 %all_to_all.42 = bf16[64,2,1024]{2,1,0:T(2,128)(2,1)S(1)} all-to-all(bf16[64,2,1024]{2,1,0:T(2,128)(2,1)S(1)} %reshape.1064), channel_id=1, replica_groups=mesh['dp'=8,'ctx'=64] {'ctx'}, dimensions={0} | all-to-all | bytes 524288 | tf_op jit(solution)/shard_map/all_to_all | solution.py:44
  273.7 49.0 %all_gather.21 = f32[1024,16]{1,0:T(8,128)S(1)} all-gather(f32[16,16]{1,0:T(8,128)S(1)} %copy.172), channel_id=1, replica_groups=mesh['dp'=8,'ctx'=64] {'ctx'}, dimensions={0}, use_global_device_ids=true | all-gather | bytes 66560 | tf_op jit(solution)/shard_map/all_gather | solution.py:92
  323.5 6.5 %copy.169 = bf16[1024,2048]{0,1:T(8,128)(2,1)} copy(bf16[1024,2048]{1,0:T(8,128)(2,1)} %all-gather.9.cloned.1.call-done) | data formatting | bytes 8388608 | tf_op jit(solution)/shard_map/all_gather | solution.py:96
  330.0 3.9 fusion.44
  334.0 5.2 fusion.13
  340.2 48.6 %all_gather.23 = f32[1024,16]{1,0:T(8,128)S(1)} all-gather(f32[16,16]{1,0:T(8,128)S(1)} %copy.177), channel_id=1, replica_groups=mesh['dp'=8,'ctx'=64] {'ctx'}, dimensions={0}, use_global_device_ids=true | all-gather | bytes 66560 | tf_op jit(solution)/shard_map/all_gather | solution.py:93
  389.6 6.5 %copy.174 = bf16[1024,2048]{0,1:T(8,128)(2,1)} copy(bf16[1024,2048]{1,0:T(8,128)(2,1)} %all-gather.11.cloned.1.call-done) | data formatting | bytes 8388608 | tf_op jit(solution)/shard_map/all_gather | solution.py:97
  406.7 6.0 %all-to-all-start.7 = ((bf16[64,2,1024]{2,1,0:T(2,128)(2,1)}), bf16[64,2,1024]{2,1,0:T(2,128)(2,1)S(1)}, u32[]{:S(2)}, u32[]{:S(2)}) async-start(bf16[64,2,1024]{2,1,0:T(2,128)(2,1)} %reshape.1070), calls=%async_computation.7 | async-start | bytes 524288 | tf_op jit(solution)/shard_map/all_to_all | solution.py:177
  414.3 11.5 %all-to-all-done.7 = bf16[64,2,1024]{2,1,0:T(2,128)(2,1)S(1)} async-done(((bf16[64,2,1024]{2,1,0:T(2,128)(2,1)}), bf16[64,2,1024]{2,1,0:T(2,128)(2,1)S(1)}, u32[]{:S(2)}, u32[]{:S(2)}) %all-to-all-start.7) | async-done | bytes 262176 | tf_op jit(solution)/shard_map/all_to_all | solution.py:177
  425.8 4.7 all-to-all-start.6
  432.2 11.5 %all-to-all-done.6 = bf16[64,2,1024]{2,1,0:T(2,128)(2,1)S(1)} async-done(((bf16[64,2,1024]{2,1,0:T(2,128)(2,1)}), bf16[64,2,1024]{2,1,0:T(2,128)(2,1)S(1)}, u32[]{:S(2)}, u32[]{:S(2)}) %all-to-all-start.6) | async-done | bytes 262176 | tf_op jit(solution)/shard_map/all_to_all | solution.py:176
  443.7 4.7 all-to-all-start.5
  449.4 100.1 %psum.7 = f32[16]{0:T(128)} all-reduce(f32[16]{0:T(128)S(1)} %get-tuple-element.26), channel_id=1, replica_groups=mesh['dp'=8,'ctx'=64] {'dp','ctx'}, use_global_device_ids=true, to_apply=%region_10.11 | all-reduce | flops 16 | bytes 128 | tf_op jit(solution)/shard_map/psum | solution.py:185
  (155 shorter events, 57.3 us)
Async XLA Ops:
  7.2 7.0 %copy-start.7 = (bf16[1,128,2048]{2,1,0:T(8,128)(2,1)S(1)}, bf16[1,128,2048]{2,1,0:T(8,128)(2,1)}, u32[]{:S(2)}) copy-start(bf16[1,128,2048]{2,1,0:T(8,128)(2,1)} %param.9) | copy-start | bytes 1572868
  12.7 221.2 %copy-start.19 = (s32[1024]{0:T(1024)}, s32[1024]{0:T(1024)S(1)}, u32[]{:S(2)}) copy-start(s32[1024]{0:T(1024)S(1)} %pad_clamp_fusion.1) | copy-start | bytes 12292
  13.5 15.5 %copy-start.1 = (s32[1,1024]{1,0:T(1,128)S(1)}, s32[1,1024]{1,0:T(1,128)}, u32[]{:S(2)}) copy-start(s32[1,1024]{1,0:T(1,128)} %param.12) | copy-start | bytes 12292
  17.3 24.8 %all-to-all-start.2 = ((bf16[64,2,1024]{2,1,0:T(2,128)(2,1)}), bf16[64,2,1024]{2,1,0:T(2,128)(2,1)S(1)}, u32[]{:S(2)}, u32[]{:S(2)}) async-start(bf16[64,2,1024]{2,1,0:T(2,128)(2,1)} %reshape.1058), calls=%async_computation.2 | async-start | bytes 524288 | tf_op jit(solution)/shard_map/all_to_all | solution.py:42
  28.9 99.1 %all-gather.7.cloned.1.call-start = ((), (), s32[]{:S(2)}) async-start(), calls=%async_computation.9 | async-start | bytes 4259840 | tf_op jit(solution)/shard_map/all_gather | solution.py:64
  43.9 169.9 %all-gather.5.cloned.1.call-start = ((), (), s32[]{:S(2)}) async-start(), calls=%async_computation.8 | async-start | bytes 4259840 | tf_op jit(solution)/shard_map/all_gather | solution.py:65
  64.4 25.4 %copy-start.26 = (f32[16]{0:T(128)S(1)}, f32[16]{0:T(128)}, u32[]{:S(2)}) copy-start(f32[16]{0:T(128)} %param.11) | copy-start | bytes 196
  64.4 259.1 %all-gather.9.cloned.1.call-start = ((), (), s32[]{:S(2)}) async-start(), calls=%async_computation.10 | async-start | bytes 4259840 | tf_op jit(solution)/shard_map/all_gather | solution.py:96
  89.7 135.3 %copy-start.20 = (s32[1024]{0:T(1024)}, s32[1024]{0:T(1024)S(1)}, u32[]{:S(2)}) copy-start(s32[1024]{0:T(1024)S(1)} %pad_clamp_fusion) | copy-start | bytes 12292
  89.8 135.9 %copy-start.23 = (pred[64]{0:T(512)(128)(4,1)}, pred[64]{0:T(512)(128)(4,1)S(1)}, u32[]{:S(2)}) copy-start(pred[64]{0:T(512)(128)(4,1)S(1)} %fusion.67) | copy-start | bytes 196
  89.8 130.4 %copy-start.21 = (f32[16]{0:T(128)}, f32[16]{0:T(128)S(1)}, u32[]{:S(2)}) copy-start(f32[16]{0:T(128)S(1)} %broadcast_multiply_fusion) | copy-start | bytes 196
  90.5 133.1 %copy-start.13 = (pred[16,1024]{1,0:T(8,128)(4,1)}, pred[16,1024]{1,0:T(8,128)(4,1)S(1)}, u32[]{:S(2)}) copy-start(pred[16,1024]{1,0:T(8,128)(4,1)S(1)} %get-tuple-element.15) | copy-start | bytes 49156
  134.4 85.9 %copy-start.11 = (bf16[16,2048]{1,0:T(8,128)(2,1)S(1)}, bf16[16,2048]{1,0:T(8,128)(2,1)}, u32[]{:S(2)}) copy-start(bf16[16,2048]{1,0:T(8,128)(2,1)} %gather_fusion.6) | copy-start | bytes 196612
  223.7 10.2 %copy-start.5 = (bf16[1,128,2048]{2,1,0:T(8,128)(2,1)S(1)}, bf16[1,128,2048]{2,1,0:T(8,128)(2,1)}, u32[]{:S(2)}) copy-start(bf16[1,128,2048]{2,1,0:T(8,128)(2,1)} %param.13) | copy-start | bytes 1572868
  225.7 23.4 %copy-start.25 = (f32[1,128]{1,0:T(1,128)S(1)}, f32[1,128]{1,0:T(1,128)}, u32[]{:S(2)}) copy-start(f32[1,128]{1,0:T(1,128)} %param.10) | copy-start | bytes 1540
  227.5 19.3 %all-to-all-start.3 = ((bf16[64,2,1024]{2,1,0:T(2,128)(2,1)}), bf16[64,2,1024]{2,1,0:T(2,128)(2,1)S(1)}, u32[]{:S(2)}, u32[]{:S(2)}) async-start(bf16[64,2,1024]{2,1,0:T(2,128)(2,1)} %reshape.1062), calls=%async_computation.3 | async-start | bytes 524288 | tf_op jit(solution)/shard_map/all_to_all | solution.py:173
  233.6 155.9 %all-gather.11.cloned.1.call-start = ((), (), s32[]{:S(2)}) async-start(), calls=%async_computation.11 | async-start | bytes 4259840 | tf_op jit(solution)/shard_map/all_gather | solution.py:97
  389.6 6.5 %copy-start.8 = (f32[16,16,1024]{2,1,0:T(8,128)S(1)}, f32[16,16,1024]{2,1,0:T(8,128)}, u32[]{:S(2)}) copy-start(f32[16,16,1024]{2,1,0:T(8,128)} %fusion.44) | copy-start | bytes 3145732
  389.6 6.5 %copy-start.15 = (f32[16,1024]{1,0:T(8,128)S(1)}, f32[16,1024]{1,0:T(8,128)}, u32[]{:S(2)}) copy-start(f32[16,1024]{1,0:T(8,128)} %copy.173) | copy-start | bytes 196612
  389.6 6.5 %copy-start.17 = (pred[16,1024]{1,0:T(8,128)(4,1)S(1)}, pred[16,1024]{1,0:T(8,128)(4,1)}, u32[]{:S(2)}) copy-start(pred[16,1024]{1,0:T(8,128)(4,1)} %get-tuple-element.14) | copy-start | bytes 49156
  405.0 144.9 %copy-start.18 = (s32[64]{0:T(128)S(1)}, s32[64]{0:T(128)}, u32[]{:S(2)}) copy-start(s32[64]{0:T(128)} %get-tuple-element.13) | copy-start | bytes 772
  406.7 19.1 %all-to-all-start.7 = ((bf16[64,2,1024]{2,1,0:T(2,128)(2,1)}), bf16[64,2,1024]{2,1,0:T(2,128)(2,1)S(1)}, u32[]{:S(2)}, u32[]{:S(2)}) async-start(bf16[64,2,1024]{2,1,0:T(2,128)(2,1)} %reshape.1070), calls=%async_computation.7 | async-start | bytes 524288 | tf_op jit(solution)/shard_map/all_to_all | solution.py:177
  425.8 17.9 %all-to-all-start.6 = ((bf16[64,2,1024]{2,1,0:T(2,128)(2,1)}), bf16[64,2,1024]{2,1,0:T(2,128)(2,1)S(1)}, u32[]{:S(2)}, u32[]{:S(2)}) async-start(bf16[64,2,1024]{2,1,0:T(2,128)(2,1)} %reshape.1068), calls=%async_computation.6 | async-start | bytes 524288 | tf_op jit(solution)/shard_map/all_to_all | solution.py:176
  443.7 108.4 %all-to-all-start.5 = ((bf16[64,2,1024]{2,1,0:T(2,128)(2,1)}), bf16[64,2,1024]{2,1,0:T(2,128)(2,1)S(1)}, u32[]{:S(2)}, u32[]{:S(2)}) async-start(bf16[64,2,1024]{2,1,0:T(2,128)(2,1)} %reshape.1066), calls=%async_computation.5 | async-start | bytes 524288 | tf_op jit(solution)/shard_map/all_to_all | solution.py:175
  (12 other events, 49.8 us)
Sparse Core Ops, SparseCore 0:
  44.0 83.9 all-gather.6
  131.9 81.8 all-gather.4
  217.7 82.5 all-gather.8
  304.1 82.1 all-gather.10
where the time goes:
time: 561 us; the launch traced here: 560 us
  blocking collectives  252 us (45%)
  waiting for transfers between devices  164 us (29%)
  local copies, waits for them, and re-layouts  58.7 us (10%)
  starting transfers between devices  33.6 us (6%)
  matrix products  23.8 us (4%)
  between operations  14.3 us (3%)
  other arithmetic  13.7 us (2%)
    psum x1, blocking collectives, body(): d_head_scale = lax.psum(scale_acc, ('dp', 'ctx'))  100 us
    all_gather x1, waiting for transfers between devices, body(): lax.all_gather(v_bal, 'ctx', axis=0, tiled=True)  79.5 us
    all_gather x1, blocking collectives, body(): lax.all_gather(lse_rows, 'ctx', axis=0, tiled=True)  49 us
    all_gather x1, blocking collectives, body(): lax.all_gather(delta, 'ctx', axis=0, tiled=True)  48.6 us
    all_gather x1, waiting for transfers between devices, body(): lax.all_gather(k_bal, 'ctx', axis=0, tiled=True)  37.5 us
    all_to_all x1, blocking collectives, body(): lax.all_to_all(send_grad, 'ctx', split_axis=0, concat_axis=0, tiled=True)  18.5 us
    all_to_all x1, blocking collectives, body(): lax.all_to_all(pick(queries[0]), 'ctx', split_axis=0, concat_axis=0, tile...  17.8 us
    all_to_all x1, blocking collectives, body(): lax.all_to_all(pick(values[0]), 'ctx', split_axis=0, concat_axis=0, tiled...  17.7 us
  transfers between devices with their start and end apart: 9, of which 6 were waited for; matrix products, arithmetic and copies ran while one was open for 12% of the time, Pallas kernels for 0%

commit v1 on v0

v1 whole, which is shorter than its diff:
```python
import functools
import math

import jax
import jax.numpy as jnp
from jax import lax
from jax.experimental import pallas as pl
from jax.experimental.pallas import tpu as pltpu
from jax.sharding import PartitionSpec as P

F32 = jnp.float32
BF16 = jnp.bfloat16
VM = pl.BlockSpec(memory_space=pltpu.VMEM)
SM = pl.BlockSpec(memory_space=pltpu.SMEM)
NT = (((1,), (1,)), ((), ()))
PARTS = 4


def eye(n):
    return lax.broadcasted_iota(jnp.int32, (n, n), 0) == lax.broadcasted_iota(jnp.int32, (n, n), 1)


def to_row(col, n):
    return jnp.sum(jnp.where(eye(n), col, 0.0), axis=0, keepdims=True)


def to_col(row, n):
    return jnp.sum(jnp.where(eye(n), row, 0.0), axis=1, keepdims=True)


def slot_column(places, first, tok):
    total = places.shape[1]
    before = jnp.sum((places < first).astype(F32), axis=1, keepdims=True)
    rank = lax.broadcasted_iota(jnp.int32, (1, total), 1).astype(F32) + 1.0 - before
    here = places - first == lax.broadcasted_iota(jnp.int32, (tok, total), 0)
    return jnp.sum(jnp.where(here, rank, 0.0), axis=1, keepdims=True)


def sigmoid(x):
    return 1.0 / (1.0 + jnp.exp(-x))


def pack_kernel(here_ref, places_ref, logit_ref, q_ref, k_ref, v_ref, g_ref, out_ref):
    tok, width = q_ref.shape
    slots, hdim = out_ref.shape[1:]
    row = to_row(slot_column(places_ref[...], here_ref[0] * tok, tok), tok)
    hit = lax.broadcasted_iota(jnp.int32, (slots, tok), 0).astype(F32) + 1.0 == row
    pick = hit.astype(BF16)
    gate = jnp.sum(jnp.where(hit, sigmoid(logit_ref[...]), 0.0), axis=1, keepdims=True)
    for part, ref in enumerate((q_ref, k_ref, v_ref, g_ref)):
        for base in range(0, width, 4 * hdim):
            rows = jnp.dot(pick, ref[:, base : base + 4 * hdim], preferred_element_type=F32)
            if part == 3:
                rows = rows * gate
            rows = rows.astype(BF16)
            for i in range(4):
                head = base // hdim + i
                out_ref[head * PARTS + part] = rows[:, i * hdim : (i + 1) * hdim]


def compact_kernel(before_ref, in_ref, out_ref, buf):
    shards, slots, _ = in_ref.shape
    total = out_ref.shape[0]
    for c in range(shards):
        buf[pl.ds(before_ref[c], slots), :] = in_ref[c].astype(F32)
    out_ref[...] = buf[:total, :].astype(BF16)


def attend_kernel(before_ref, role_ref, scale_ref, x0, x1, x2, x3, out_ref, ds_ref, arr, res):
    shards, slots, hdim = out_ref.shape
    total = x0.shape[0]
    blk = 256
    inv = 1.0 / math.sqrt(hdim)
    role = role_ref[0]
    scale = scale_ref[0]
    coef = scale * inv
    for i, ref in enumerate((x0, x1, x2, x3)):
        arr[role ^ i] = ref[...]
    res[...] = jnp.zeros_like(res)
    q_ref, k_ref, v_ref, g_ref = (arr.at[i] for i in range(PARTS))
    kt = k_ref[...].astype(F32).T.astype(BF16)
    vt = v_ref[...].astype(F32).T.astype(BF16)
    tri = lax.broadcasted_iota(jnp.int32, (blk, blk), 0) <= lax.broadcasted_iota(
        jnp.int32, (blk, blk), 1
    )
    dsc = jnp.zeros((1, blk), F32)
    for lo in range(0, total, blk):
        n = lo + blk
        qi = q_ref[lo:n, :]
        gi = g_ref[lo:n, :]
        raw = lax.dot_general(k_ref[:n, :], qi, NT, preferred_element_type=F32)
        s = raw * coef
        diag = jnp.where(tri, s[lo:, :], -jnp.inf)
        top = jnp.max(diag, axis=0, keepdims=True)
        if lo:
            top = jnp.maximum(top, jnp.max(s[:lo, :], axis=0, keepdims=True))
            s = jnp.concatenate([s[:lo, :], diag], axis=0)
        else:
            s = diag
        e = jnp.exp(s - top)
        p = e * (1.0 / jnp.sum(e, axis=0, keepdims=True))
        pb = p.astype(BF16)
        att = jnp.dot(vt[:, :n], pb, preferred_element_type=F32).astype(BF16)
        git = gi.astype(F32).T
        delta = jnp.sum(git * att.astype(F32), axis=0, keepdims=True)
        dp = lax.dot_general(v_ref[:n, :], gi, NT, preferred_element_type=F32)
        ds = p * (dp - delta)
        dsc = dsc + jnp.sum(ds * raw, axis=0, keepdims=True)
        dsb = ds.astype(BF16)

        @pl.when(role == 0)
        def _():
            res[lo:n, :] = att.astype(F32).T

        @pl.when(role == 1)
        def _():
            res[lo:n, :] = coef * jnp.dot(kt[:, :n], dsb, preferred_element_type=F32).T

        @pl.when(role == 2)
        def _():
            res[:n, :] += coef * jnp.dot(dsb, qi, preferred_element_type=F32)

        @pl.when(role == 3)
        def _():
            res[:n, :] += jnp.dot(pb, gi, preferred_element_type=F32)

    ds_ref[...] = jnp.broadcast_to(jnp.sum(dsc, axis=1, keepdims=True) * inv, ds_ref.shape)
    for c in range(shards):
        out_ref[c] = res[pl.ds(before_ref[c], slots), :].astype(BF16)


def place_kernel(
    here_ref, places_ref, logit_ref, g_ref, in_ref, bo_ref, dq_ref, dk_ref, dv_ref, dl_ref
):
    tok, width = g_ref.shape
    slots, hdim = in_ref.shape[1:]
    col = slot_column(places_ref[...], here_ref[0] * tok, tok)
    hit = lax.broadcasted_iota(jnp.int32, (tok, slots), 1).astype(F32) + 1.0 == col
    spread = hit.astype(BF16)
    gate_row = sigmoid(logit_ref[...])
    gate = to_col(gate_row, tok)
    acc = jnp.zeros((tok, hdim), F32)
    for head in range(width // hdim):
        cols = slice(head * hdim, (head + 1) * hdim)
        att = jnp.dot(spread, in_ref[head * PARTS], preferred_element_type=F32)
        bo_ref[:, cols] = (gate * att).astype(BF16)
        acc = acc + g_ref[:, cols].astype(F32) * att
        for part, ref in ((1, dq_ref), (2, dk_ref), (3, dv_ref)):
            ref[:, cols] = jnp.dot(
                spread, in_ref[head * PARTS + part], preferred_element_type=F32
            ).astype(BF16)
    dot = to_row(jnp.sum(acc, axis=1, keepdims=True), tok)
    dl_ref[...] = gate_row * (1.0 - gate_row) * dot


def body(queries, keys, values, router_logit, head_scale, routed, grad_out):
    nctx = lax.axis_size("ctx")
    here = lax.axis_index("ctx")
    tok, width = queries.shape[1:]
    heads = head_scale.shape[0]
    hdim = width // heads
    total = routed.shape[1]
    rows = total // nctx
    slots = rows + 3 * (rows // 2)
    here_vec = here.astype(jnp.int32)[None]
    role = (here % PARTS).astype(jnp.int32)[None]
    head = here // PARTS
    scale = lax.dynamic_slice_in_dim(head_scale, head, 1)
    starts = jnp.arange(nctx, dtype=jnp.int32) * tok
    before = jnp.sum((routed[0][None, :] < starts[:, None]).astype(jnp.int32), axis=1)
    params = pltpu.CompilerParams(vmem_limit_bytes=48 * 1024 * 1024)

    send = pl.pallas_call(
        pack_kernel,
        out_shape=jax.ShapeDtypeStruct((nctx, slots, hdim), BF16),
        in_specs=[SM] + [VM] * 6,
        out_specs=VM,
        compiler_params=params,
        name="pack",
    )(here_vec, routed, router_logit, queries[0], keys[0], values[0], grad_out[0])
    got = lax.all_to_all(send, "ctx", split_axis=0, concat_axis=0, tiled=True)
    own = pl.pallas_call(
        compact_kernel,
        out_shape=jax.ShapeDtypeStruct((total, hdim), BF16),
        in_specs=[SM, VM],
        out_specs=VM,
        scratch_shapes=[pltpu.VMEM((total + slots, hdim), F32)],
        compiler_params=params,
        name="compact",
    )(before, got)
    side = lax.ppermute(own, "ctx", [(i, i ^ 2) for i in range(nctx)])
    near = lax.ppermute(own, "ctx", [(i, i ^ 1) for i in range(nctx)])
    cross = lax.ppermute(side, "ctx", [(i, i ^ 1) for i in range(nctx)])
    back, dsc = pl.pallas_call(
        attend_kernel,
        out_shape=(
            jax.ShapeDtypeStruct((nctx, slots, hdim), BF16),
            jax.ShapeDtypeStruct((8, 128), F32),
        ),
        in_specs=[SM] * 3 + [VM] * 4,
        out_specs=(VM, VM),
        scratch_shapes=[
            pltpu.VMEM((PARTS, total, hdim), BF16),
            pltpu.VMEM((total + slots, hdim), F32),
        ],
        compiler_params=params,
        name="attend",
    )(before, role, scale, own, near, side, cross)
    home = lax.all_to_all(back, "ctx", split_axis=0, concat_axis=0, tiled=True)
    dsc = lax.psum(dsc, "dp")
    groups = [[PARTS * i + j for i in range(heads)] for j in range(nctx // heads)]
    all_dsc = lax.all_to_all(
        jnp.broadcast_to(dsc[None], (heads,) + dsc.shape),
        "ctx",
        split_axis=0,
        concat_axis=0,
        axis_index_groups=groups,
        tiled=True,
    )
    outs = pl.pallas_call(
        place_kernel,
        out_shape=tuple([jax.ShapeDtypeStruct((tok, width), BF16)] * 4)
        + (jax.ShapeDtypeStruct((1, tok), F32),),
        in_specs=[SM] + [VM] * 4,
        out_specs=(VM,) * 5,
        compiler_params=params,
        name="place",
    )(here_vec, routed, router_logit, grad_out[0], home)
    block_out, d_q, d_k, d_v, d_logit = outs
    return block_out[None], d_q[None], d_k[None], d_v[None], d_logit, all_dsc[:, 0, 0]


def solution(mesh):
    in_specs = (
        P("dp", "ctx", None),
        P("dp", "ctx", None),
        P("dp", "ctx", None),
        P("dp", "ctx"),
        P(),
        P("dp", None),
        P("dp", "ctx", None),
    )
    out_specs = (
        P("dp", "ctx", None),
        P("dp", "ctx", None),
        P("dp", "ctx", None),
        P("dp", "ctx", None),
        P("dp", "ctx"),
        P(),
    )
    return jax.shard_map(body, mesh=mesh, in_specs=in_specs, out_specs=out_specs, check_vma=False)
```

time: 561 us -> 125 us (0.22)
  blocking collectives: 252 us -> 33.1 us
  waiting for transfers between devices: 164 us -> 43.3 us
  local copies, waits for them, and re-layouts: 58.7 us -> 6.79 us
  matrix products: 23.8 us -> 0 us
  between operations: 14.3 us -> 0.75 us
  other arithmetic: 13.7 us -> 0.19 us
  Pallas kernels: 0 us -> 11.1 us
    all_gather x4 -> x0, waiting for transfers between devices: 117 us -> none  [the longest x1 79.5 us: body(): lax.all_gather(v_bal, 'ctx', axis=0, tiled=True)]
    all_gather x2 -> x0, blocking collectives: 97.6 us -> none  [the longest x1 49 us: body(): lax.all_gather(lse_rows, 'ctx', axis=0, tiled=True)]
    psum x1, blocking collectives: 100 us -> 19.7 us  [body(): dsc = lax.psum(dsc, 'dp')]
    all_to_all x3 -> x1, blocking collectives: 53.9 us -> 13.4 us  [body(): lax.all_to_all(jnp.broadcast_to(dsc[None], (heads,) + dsc.shape), 'ctx',...]
    all_gather x4 -> x0, local copies, waits for them, and re-layouts: 25.7 us -> none  [the longest x1 6.49 us: body(): lax.all_gather(d_bal, 'ctx', axis=0, tiled=True)]
    dot_general x11 -> x0, matrix products: 23.8 us -> none  [the longest x1 5.23 us: body(): jnp.einsum('hsk,khd->shd', d_scores.astype(jnp.bfloat16), split_heads(all...]
    gather x16 -> x0, local copies, waits for them, and re-layouts: 19.4 us -> none  [the longest x1 4.53 us: key_places(): return places[index // rows + nctx * (index % rows)]]
    all_to_all x5 -> x2, starting transfers between devices: 33.2 us -> 20.2 us  [the longest x1 11.6 us: body(): got = lax.all_to_all(send, 'ctx', split_axis=0, concat_axis=0, tiled=True)]
  transfers between devices with their start and end apart: 9 -> 5, of which waited for: 6 -> 3; matrix products, arithmetic and copies ran while one was open for 12% -> 1% of each run, Pallas kernels for 0% -> 0%
where the time goes in v1:
time: 125 us
  waiting for transfers between devices  43.3 us (35%)
  blocking collectives  33.1 us (26%)
  starting transfers between devices  29.4 us (24%)
  Pallas kernels  11.1 us (9%)
  local copies, waits for them, and re-layouts  6.79 us (5%)
    all_to_all x1, waiting for transfers between devices, body(): got = lax.all_to_all(send, 'ctx', split_axis=0, concat_axis=0, tiled=True)  20.2 us
    all_to_all x1, waiting for transfers between devices, body(): home = lax.all_to_all(back, 'ctx', split_axis=0, concat_axis=0, tiled=True)  19.8 us
    psum x1, blocking collectives, body(): dsc = lax.psum(dsc, 'dp')  19.7 us
    all_to_all x1, blocking collectives, body(): lax.all_to_all(jnp.broadcast_to(dsc[None], (heads,) + dsc.shape), 'ctx',...  13.4 us
    all_to_all x1, starting transfers between devices, body(): got = lax.all_to_all(send, 'ctx', split_axis=0, concat_axis=0, tiled=True)  11.6 us
    all_to_all x1, starting transfers between devices, body(): home = lax.all_to_all(back, 'ctx', split_axis=0, concat_axis=0, tiled=True)  8.63 us
    pallas_call x1, Pallas kernels, body(): pl.pallas_call(attend_kernel, out_shape=(jax.ShapeDtypeStruct((nctx, slot...  6.73 us
    unnamed x16, local copies, waits for them, and re-layouts  5.49 us
  transfers between devices with their start and end apart: 5, of which 3 were waited for; matrix products, arithmetic and copies ran while one was open for 1% of the time, Pallas kernels for 0%

profile of v1, /device:TPU:1, one launch (start us, length us, event | category | flops | bytes accessed | tf_op | source)
XLA Modules:
  0.0 124.7 jit_solution(3338134729720521098)
XLA Ops:
  0.7 0.7 copy-done.5
  1.3 1.0 copy-done
  2.4 1.0 copy-done.2
  3.4 1.0 copy-done.3
  4.5 1.0 copy-done.4
  5.5 1.5 %pack.1 = bf16[64,40,128]{2,1,0:T(8,128)(2,1)} custom-call(s32[1]{0:T(128)} %bitcast.here_ref, s32[1,1024]{1,0:T(1,128)S(1)} %copy-done.5, f32[1,128]{1,0:T(1,128)S(1)} %copy-done.6, bf16[128,2048]{1,0:T(8,128)(2,1)S(1)} %bitcast.13, bf16[128,2048]{1,0:T(8,128)(2,1)S(1)} %bitcast.14, bf16[128,2048]{1,0:T(8,128)(2,1)S(1)} %bitcast.15, ...), custom_call_target="tpu_custom_call" | custom-call | tf_op jit(solution)/shard_map/pack/pallas_call | solution.py:173
  7.0 11.6 %all-to-all-start = ((bf16[64,40,128]{2,1,0:T(8,128)(2,1)}), bf16[64,40,128]{2,1,0:T(8,128)(2,1)S(1)}, u32[]{:S(2)}, u32[]{:S(2)}) async-start(bf16[64,40,128]{2,1,0:T(8,128)(2,1)} %pack.1), calls=%async_computation | async-start | bytes 1310720 | tf_op jit(solution)/shard_map/all_to_all | solution.py:181
  18.6 0.2 convert_reduce_fusion.before_ref
  18.8 20.2 %all-to-all-done.in_ref = bf16[64,40,128]{2,1,0:T(8,128)(2,1)S(1)} async-done(((bf16[64,40,128]{2,1,0:T(8,128)(2,1)}), bf16[64,40,128]{2,1,0:T(8,128)(2,1)S(1)}, u32[]{:S(2)}, u32[]{:S(2)}) %all-to-all-start) | async-done | bytes 655392 | tf_op jit(solution)/shard_map/all_to_all | solution.py:181
  39.0 0.7 compact.1.x0
  39.6 3.0 %collective-permute-start.1 = (bf16[1024,128]{1,0:T(8,128)(2,1)S(1)}, bf16[1024,128]{1,0:T(8,128)(2,1)S(1)}, u32[]{:S(2)}, u32[]{:S(2)}) collective-permute-start(bf16[1024,128]{1,0:T(8,128)(2,1)S(1)} %compact.1.x0), channel_id=1, source_target_pairs={{0,2},{1,3},{2,0},{3,1},{4,6},{5,7},{6,4},{7,5},{8,10},{9,11},{10,... | collective-permute-start | bytes 786440 | tf_op jit(solution)/shard_map/ppermute | solution.py:191
  42.6 2.9 %collective-permute-start = (bf16[1024,128]{1,0:T(8,128)(2,1)S(1)}, bf16[1024,128]{1,0:T(8,128)(2,1)S(1)}, u32[]{:S(2)}, u32[]{:S(2)}) collective-permute-start(bf16[1024,128]{1,0:T(8,128)(2,1)S(1)} %compact.1.x0), channel_id=1, source_target_pairs={{0,1},{1,0},{2,3},{3,2},{4,5},{5,4},{6,7},{7,6},{8,9},{9,8},{10,11... | collective-permute-start | bytes 786440 | tf_op jit(solution)/shard_map/ppermute | solution.py:192
  45.5 3.3 %collective-permute-done.1.x2 = bf16[1024,128]{1,0:T(8,128)(2,1)S(1)} collective-permute-done((bf16[1024,128]{1,0:T(8,128)(2,1)S(1)}, bf16[1024,128]{1,0:T(8,128)(2,1)S(1)}, u32[]{:S(2)}, u32[]{:S(2)}) %collective-permute-start.1) | collective-permute-done | bytes 262176 | tf_op jit(solution)/shard_map/ppermute | solution.py:191
  48.8 3.3 %collective-permute-start.2 = (bf16[1024,128]{1,0:T(8,128)(2,1)S(1)}, bf16[1024,128]{1,0:T(8,128)(2,1)S(1)}, u32[]{:S(2)}, u32[]{:S(2)}) collective-permute-start(bf16[1024,128]{1,0:T(8,128)(2,1)S(1)} %collective-permute-done.1.x2), channel_id=1, source_target_pairs={{0,1},{1,0},{2,3},{3,2},{4,5},{5,4},{6,7},{7,6},{8,9},{9,8},{10,11... | collective-permute-start | bytes 786440 | tf_op jit(solution)/shard_map/ppermute | solution.py:193
  52.2 0.0 copy-start.7
  52.2 0.6 copy-done.7
  52.8 0.6 dynamic_slice.3.scale_ref
  53.4 6.7 %attend.1 = (bf16[64,40,128]{2,1,0:T(8,128)(2,1)}, f32[8,128]{1,0:T(8,128)S(1)}) custom-call(s32[64]{0:T(128)S(1)} %convert_reduce_fusion.before_ref, s32[1]{0:T(128)} %bitcast.3.role_ref, f32[1]{0:T(128)} %dynamic_slice.3.scale_ref, bf16[1024,128]{1,0:T(8,128)(2,1)S(1)} %compact.1.x0, bf16[1024,128]{1,0:T(8,128)(2,1)S(1)} %collective-permute-done.x1, ...), custom_call_target="tpu_custom_call" | custom-call | tf_op jit(solution)/shard_map/attend/pallas_call | solution.py:194
  60.2 19.7 %psum.7 = f32[8,128]{1,0:T(8,128)S(1)} all-reduce(f32[8,128]{1,0:T(8,128)S(1)} %get-tuple-element.19), channel_id=1, replica_groups=mesh['dp'=8,'ctx'=64] {'dp'}, use_global_device_ids=true, to_apply=%region_1.2 | all-reduce | flops 1024 | bytes 8192 | tf_op jit(solution)/shard_map/psum | solution.py:210
  79.9 13.4 %all_to_all.15 = f32[16,8,128]{2,1,0:T(8,128)S(1)} all-to-all(f32[16,8,128]{2,1,0:T(8,128)S(1)} %broadcast_in_dim.31), channel_id=1, replica_groups={{0,4,8,12,16,20,24,28,32,36,40,44,48,52,56,60},{1,5,9,13,17,21,25,29,33..., dimensions={0} | all-to-all | bytes 131072 | tf_op jit(solution)/shard_map/all_to_all | solution.py:212
  93.3 8.6 %all-to-all-start.1 = ((bf16[64,40,128]{2,1,0:T(8,128)(2,1)}), bf16[64,40,128]{2,1,0:T(8,128)(2,1)S(1)}, u32[]{:S(2)}, u32[]{:S(2)}) async-start(bf16[64,40,128]{2,1,0:T(8,128)(2,1)} %get-tuple-element.13), calls=%async_computation.1 | async-start | bytes 1310720 | tf_op jit(solution)/shard_map/all_to_all | solution.py:209
  101.9 0.7 slice_reduce_fusion
  102.6 19.8 %all-to-all-done.1.in_ref = bf16[64,40,128]{2,1,0:T(8,128)(2,1)S(1)} async-done(((bf16[64,40,128]{2,1,0:T(8,128)(2,1)}), bf16[64,40,128]{2,1,0:T(8,128)(2,1)S(1)}, u32[]{:S(2)}, u32[]{:S(2)}) %all-to-all-start.1) | async-done | bytes 655392 | tf_op jit(solution)/shard_map/all_to_all | solution.py:209
  122.4 2.3 %place.1 = (bf16[128,2048]{1,0:T(8,128)(2,1)}, bf16[128,2048]{1,0:T(8,128)(2,1)}, bf16[128,2048]{1,0:T(8,128)(2,1)}, bf16[128,2048]{1,0:T(8,128)(2,1)}, f32[1,128]{1,0:T(1,128)}) custom-call(s32[1]{0:T(128)} %bitcast.here_ref, s32[1,1024]{1,0:T(1,128)S(1)} %copy-done.5, f32[1,128]{1,0:T(1,128)S(1)} %copy-done.6, bf16[128,2048]{1,0:T(8,128)(2,1)S(1)} %bitcast.12, ...), custom_call_target="tpu_custom_call" | custom-call | tf_op jit(solution)/shard_map/place/pallas_call | solution.py:220
  (13 shorter events, 0.0 us)
Async XLA Ops:
  0.6 0.7 copy-start.5
  0.6 0.7 copy-start.6
  1.3 1.0 copy-start
  2.4 1.0 copy-start.2
  3.4 1.0 copy-start.3
  4.5 1.0 copy-start.4
  7.0 32.0 %all-to-all-start = ((bf16[64,40,128]{2,1,0:T(8,128)(2,1)}), bf16[64,40,128]{2,1,0:T(8,128)(2,1)S(1)}, u32[]{:S(2)}, u32[]{:S(2)}) async-start(bf16[64,40,128]{2,1,0:T(8,128)(2,1)} %pack.1), calls=%async_computation | async-start | bytes 1310720 | tf_op jit(solution)/shard_map/all_to_all | solution.py:181
  39.6 9.2 %collective-permute-start.1 = (bf16[1024,128]{1,0:T(8,128)(2,1)S(1)}, bf16[1024,128]{1,0:T(8,128)(2,1)S(1)}, u32[]{:S(2)}, u32[]{:S(2)}) collective-permute-start(bf16[1024,128]{1,0:T(8,128)(2,1)S(1)} %compact.1.x0), channel_id=1, source_target_pairs={{0,2},{1,3},{2,0},{3,1},{4,6},{5,7},{6,4},{7,5},{8,10},{9,11},{10,... | collective-permute-start | bytes 786440 | tf_op jit(solution)/shard_map/ppermute | solution.py:191
  42.6 10.8 %collective-permute-start = (bf16[1024,128]{1,0:T(8,128)(2,1)S(1)}, bf16[1024,128]{1,0:T(8,128)(2,1)S(1)}, u32[]{:S(2)}, u32[]{:S(2)}) collective-permute-start(bf16[1024,128]{1,0:T(8,128)(2,1)S(1)} %compact.1.x0), channel_id=1, source_target_pairs={{0,1},{1,0},{2,3},{3,2},{4,5},{5,4},{6,7},{7,6},{8,9},{9,8},{10,11... | collective-permute-start | bytes 786440 | tf_op jit(solution)/shard_map/ppermute | solution.py:192
  48.8 4.6 %collective-permute-start.2 = (bf16[1024,128]{1,0:T(8,128)(2,1)S(1)}, bf16[1024,128]{1,0:T(8,128)(2,1)S(1)}, u32[]{:S(2)}, u32[]{:S(2)}) collective-permute-start(bf16[1024,128]{1,0:T(8,128)(2,1)S(1)} %collective-permute-done.1.x2), channel_id=1, source_target_pairs={{0,1},{1,0},{2,3},{3,2},{4,5},{5,4},{6,7},{7,6},{8,9},{9,8},{10,11... | collective-permute-start | bytes 786440 | tf_op jit(solution)/shard_map/ppermute | solution.py:193
  52.2 0.7 copy-start.7
  93.3 29.1 %copy-start.1 = (bf16[1,128,2048]{2,1,0:T(8,128)(2,1)S(1)}, bf16[1,128,2048]{2,1,0:T(8,128)(2,1)}, u32[]{:S(2)}) copy-start(bf16[1,128,2048]{2,1,0:T(8,128)(2,1)} %param.13) | copy-start | bytes 1572868
  93.3 29.1 %all-to-all-start.1 = ((bf16[64,40,128]{2,1,0:T(8,128)(2,1)}), bf16[64,40,128]{2,1,0:T(8,128)(2,1)S(1)}, u32[]{:S(2)}, u32[]{:S(2)}) async-start(bf16[64,40,128]{2,1,0:T(8,128)(2,1)} %get-tuple-element.13), calls=%async_computation.1 | async-start | bytes 1310720 | tf_op jit(solution)/shard_map/all_to_all | solution.py:209

commit v2 on v1

--- a/solution.py
+++ b/solution.py
@@ -12,6 +12,7 @@
 BF16 = jnp.bfloat16
 VM = pl.BlockSpec(memory_space=pltpu.VMEM)
 SM = pl.BlockSpec(memory_space=pltpu.SMEM)
+HB = pl.BlockSpec(memory_space=pltpu.HBM)
 NT = (((1,), (1,)), ((), ()))
 PARTS = 4
 
@@ -40,16 +41,23 @@
     return 1.0 / (1.0 + jnp.exp(-x))
 
 
-def pack_kernel(here_ref, places_ref, logit_ref, q_ref, k_ref, v_ref, g_ref, out_ref):
+def pack_kernel(here_ref, places_ref, logit_ref, q_ref, k_ref, v_ref, g_ref, out_ref, buf, sems):
     tok, width = q_ref.shape
     slots, hdim = out_ref.shape[1:]
+    copies = [
+        pltpu.make_async_copy(ref, buf.at[part], sems.at[part])
+        for part, ref in enumerate((q_ref, k_ref, v_ref, g_ref))
+    ]
+    for copy in copies:
+        copy.start()
     row = to_row(slot_column(places_ref[...], here_ref[0] * tok, tok), tok)
     hit = lax.broadcasted_iota(jnp.int32, (slots, tok), 0).astype(F32) + 1.0 == row
     pick = hit.astype(BF16)
     gate = jnp.sum(jnp.where(hit, sigmoid(logit_ref[...]), 0.0), axis=1, keepdims=True)
-    for part, ref in enumerate((q_ref, k_ref, v_ref, g_ref)):
+    for part, copy in enumerate(copies):
+        copy.wait()
         for base in range(0, width, 4 * hdim):
-            rows = jnp.dot(pick, ref[:, base : base + 4 * hdim], preferred_element_type=F32)
+            rows = jnp.dot(pick, buf[part, :, base : base + 4 * hdim], preferred_element_type=F32)
             if part == 3:
                 rows = rows * gate
             rows = rows.astype(BF16)
@@ -66,65 +74,109 @@
     out_ref[...] = buf[:total, :].astype(BF16)
 
 
-def attend_kernel(before_ref, role_ref, scale_ref, x0, x1, x2, x3, out_ref, ds_ref, arr, res):
+def fold(x, op):
+    return op(x.reshape(x.shape[0] // 8, 8, x.shape[1]), axis=0)
+
+
+def attend_kernel(
+    before_ref, role_ref, head_ref, scale_ref, x0, x1, x2, x3, out_ref, ds_ref, arr, res, pbuf, dbuf, abuf, rbuf, gbuf
+):
     shards, slots, hdim = out_ref.shape
     total = x0.shape[0]
     blk = 256
+    strip = 32
     inv = 1.0 / math.sqrt(hdim)
     role = role_ref[0]
     scale = scale_ref[0]
     coef = scale * inv
+    coef2 = coef * math.log2(math.e)
     for i, ref in enumerate((x0, x1, x2, x3)):
         arr[role ^ i] = ref[...]
-    res[...] = jnp.zeros_like(res)
     q_ref, k_ref, v_ref, g_ref = (arr.at[i] for i in range(PARTS))
-    kt = k_ref[...].astype(F32).T.astype(BF16)
+    blocks = range(0, total, blk)
+
+    def scores(lo):
+        n = lo + blk
+        raw = lax.dot_general(k_ref[:n, :], q_ref[lo:n, :], NT, preferred_element_type=F32)
+        rbuf[:n, lo:n] = raw
+
+    def products(lo):
+        n = lo + blk
+        gbuf[:n, lo:n] = lax.dot_general(
+            v_ref[:n, :], g_ref[lo:n, :], NT, preferred_element_type=F32
+        )
+
+    def strips(lo):
+        return [(a, slice(a, a + strip)) for a in range(0, lo + blk, strip)]
+
+    def masked(x, a, lo):
+        if a + strip <= lo:
+            return x
+        row = lax.broadcasted_iota(jnp.int32, (strip, blk), 0) + (a - lo)
+        return jnp.where(row <= lax.broadcasted_iota(jnp.int32, (strip, blk), 1), x, -jnp.inf)
+
+    scores(0)
+    products(0)
     vt = v_ref[...].astype(F32).T.astype(BF16)
-    tri = lax.broadcasted_iota(jnp.int32, (blk, blk), 0) <= lax.broadcasted_iota(
-        jnp.int32, (blk, blk), 1
-    )
-    dsc = jnp.zeros((1, blk), F32)
-    for lo in range(0, total, blk):
+    dsc = jnp.zeros((8, blk), F32)
+    for lo in blocks:
         n = lo + blk
-        qi = q_ref[lo:n, :]
-        gi = g_ref[lo:n, :]
-        raw = lax.dot_general(k_ref[:n, :], qi, NT, preferred_element_type=F32)
-        s = raw * coef
-        diag = jnp.where(tri, s[lo:, :], -jnp.inf)
-        top = jnp.max(diag, axis=0, keepdims=True)
-        if lo:
-            top = jnp.maximum(top, jnp.max(s[:lo, :], axis=0, keepdims=True))
-            s = jnp.concatenate([s[:lo, :], diag], axis=0)
-        else:
-            s = diag
-        e = jnp.exp(s - top)
-        p = e * (1.0 / jnp.sum(e, axis=0, keepdims=True))
-        pb = p.astype(BF16)
-        att = jnp.dot(vt[:, :n], pb, preferred_element_type=F32).astype(BF16)
-        git = gi.astype(F32).T
+        cols = slice(lo, n)
+        if n < total:
+            scores(n)
+        top = jnp.full((8, blk), -jnp.inf, F32)
+        for a, rows in strips(lo):
+            top = jnp.maximum(top, fold(masked(rbuf[rows, cols], a, lo), jnp.max))
+        top = jnp.max(top, axis=0, keepdims=True) * coef2
+        acc = jnp.zeros((8, blk), F32)
+        for a, rows in strips(lo):
+            acc = acc + fold(jnp.exp2(masked(rbuf[rows, cols], a, lo) * coef2 - top), jnp.sum)
+        lse = top + jnp.log2(jnp.sum(acc, axis=0, keepdims=True))
+        for a, rows in strips(lo):
+            p = jnp.exp2(masked(rbuf[rows, cols], a, lo) * coef2 - lse)
+            pbuf[rows, cols] = p.astype(BF16)
+        att = jnp.dot(vt[:, :n], pbuf[:n, cols], preferred_element_type=F32).astype(BF16)
+        abuf[:, cols] = att
+        if n < total:
+            products(n)
+        git = g_ref[lo:n, :].astype(F32).T
         delta = jnp.sum(git * att.astype(F32), axis=0, keepdims=True)
-        dp = lax.dot_general(v_ref[:n, :], gi, NT, preferred_element_type=F32)
-        ds = p * (dp - delta)
-        dsc = dsc + jnp.sum(ds * raw, axis=0, keepdims=True)
-        dsb = ds.astype(BF16)
-
-        @pl.when(role == 0)
-        def _():
-            res[lo:n, :] = att.astype(F32).T
-
-        @pl.when(role == 1)
-        def _():
-            res[lo:n, :] = coef * jnp.dot(kt[:, :n], dsb, preferred_element_type=F32).T
-
-        @pl.when(role == 2)
-        def _():
-            res[:n, :] += coef * jnp.dot(dsb, qi, preferred_element_type=F32)
-
-        @pl.when(role == 3)
-        def _():
-            res[:n, :] += jnp.dot(pb, gi, preferred_element_type=F32)
-
-    ds_ref[...] = jnp.broadcast_to(jnp.sum(dsc, axis=1, keepdims=True) * inv, ds_ref.shape)
+        for a, rows in strips(lo):
+            raw = rbuf[rows, cols]
+            ds = jnp.exp2(masked(raw, a, lo) * coef2 - lse) * (gbuf[rows, cols] - delta)
+            dsc = dsc + fold(ds * raw, jnp.sum)
+            dbuf[rows, cols] = ds.astype(BF16)
+    mine = lax.broadcasted_iota(jnp.int32, ds_ref.shape, 1) == head_ref[0]
+    dsum = jnp.sum(jnp.sum(dsc, axis=0, keepdims=True), axis=1, keepdims=True)
+    ds_ref[...] = jnp.where(mine, dsum * inv, 0.0)
+
+    @pl.when(role == 0)
+    def _():
+        res[:total, :] = abuf[...].astype(F32).T
+
+    @pl.when(role == 1)
+    def _():
+        kt = k_ref[...].astype(F32).T.astype(BF16)
+        for lo in blocks:
+            n = lo + blk
+            dq = jnp.dot(kt[:, :n], dbuf[:n, lo:n], preferred_element_type=F32)
+            res[lo:n, :] = (coef * dq).T
+
+    @pl.when(role == 2)
+    def _():
+        for lo in blocks:
+            res[lo : lo + blk, :] = coef * jnp.dot(
+                dbuf[lo : lo + blk, lo:], q_ref[lo:, :], preferred_element_type=F32
+            )
+
+    @pl.when(role == 3)
+    def _():
+        for lo in blocks:
+            res[lo : lo + blk, :] = jnp.dot(
+                pbuf[lo : lo + blk, lo:], g_ref[lo:, :], preferred_element_type=F32
+            )
+
+    res[total:, :] = jnp.zeros((slots, hdim), F32)
     for c in range(shards):
         out_ref[c] = res[pl.ds(before_ref[c], slots), :].astype(BF16)
 
@@ -164,7 +216,7 @@
     slots = rows + 3 * (rows // 2)
     here_vec = here.astype(jnp.int32)[None]
     role = (here % PARTS).astype(jnp.int32)[None]
-    head = here // PARTS
+    head = (here // PARTS).astype(jnp.int32)
     scale = lax.dynamic_slice_in_dim(head_scale, head, 1)
     starts = jnp.arange(nctx, dtype=jnp.int32) * tok
     before = jnp.sum((routed[0][None, :] < starts[:, None]).astype(jnp.int32), axis=1)
@@ -173,9 +225,10 @@
     send = pl.pallas_call(
         pack_kernel,
         out_shape=jax.ShapeDtypeStruct((nctx, slots, hdim), BF16),
-        in_specs=[SM] + [VM] * 6,
+        in_specs=[SM] + [VM] * 2 + [HB] * 4,
         out_specs=VM,
-        compiler_params=params,
+        scratch_shapes=[pltpu.VMEM((PARTS, tok, width), BF16), pltpu.SemaphoreType.DMA((PARTS,))],
+        compiler_params=pltpu.CompilerParams(vmem_limit_bytes=60 * 1024 * 1024),
         name="pack",
     )(here_vec, routed, router_logit, queries[0], keys[0], values[0], grad_out[0])
     got = lax.all_to_all(send, "ctx", split_axis=0, concat_axis=0, tiled=True)
@@ -195,21 +248,27 @@
         attend_kernel,
         out_shape=(
             jax.ShapeDtypeStruct((nctx, slots, hdim), BF16),
-            jax.ShapeDtypeStruct((8, 128), F32),
+            jax.ShapeDtypeStruct((1, 128), F32),
         ),
-        in_specs=[SM] * 3 + [VM] * 4,
+        in_specs=[SM] * 4 + [VM] * 4,
         out_specs=(VM, VM),
         scratch_shapes=[
             pltpu.VMEM((PARTS, total, hdim), BF16),
             pltpu.VMEM((total + slots, hdim), F32),
+            pltpu.VMEM((total, total), BF16),
+            pltpu.VMEM((total, total), BF16),
+            pltpu.VMEM((hdim, total), BF16),
+            pltpu.VMEM((total, total), F32),
+            pltpu.VMEM((total, total), F32),
         ],
         compiler_params=params,
         name="attend",
-    )(before, role, scale, own, near, side, cross)
+    )(before, role, head[None], scale, own, near, side, cross)
     home = lax.all_to_all(back, "ctx", split_axis=0, concat_axis=0, tiled=True)
     dsc = lax.psum(dsc, "dp")
+    home, dsc = lax.optimization_barrier((home, dsc))
     groups = [[PARTS * i + j for i in range(heads)] for j in range(nctx // heads)]
-    all_dsc = lax.all_to_all(
+    dsc = lax.all_to_all(
         jnp.broadcast_to(dsc[None], (heads,) + dsc.shape),
         "ctx",
         split_axis=0,
@@ -227,7 +286,7 @@
         name="place",
     )(here_vec, routed, router_logit, grad_out[0], home)
     block_out, d_q, d_k, d_v, d_logit = outs
-    return block_out[None], d_q[None], d_k[None], d_v[None], d_logit, all_dsc[:, 0, 0]
+    return block_out[None], d_q[None], d_k[None], d_v[None], d_logit, jnp.sum(dsc[:, 0, :heads], axis=0)
 
 
 def solution(mesh):

time: 125 us -> 103 us (0.82)
  the two profiles are of different devices: /device:TPU:1 before, /device:TPU:2 now
where the time goes in v2:
time: 103 us
  waiting for transfers between devices  33.7 us (33%)
  starting transfers between devices  31.1 us (30%)
  blocking collectives  23.2 us (23%)
  Pallas kernels  11.4 us (11%)
  local copies, waits for them, and re-layouts  1.85 us (2%)
    psum x1, blocking collectives, body(): dsc = lax.psum(dsc, 'dp')  23.2 us
    all_to_all x1, waiting for transfers between devices, body(): got = lax.all_to_all(send, 'ctx', split_axis=0, concat_axis=0, tiled=True)  20.2 us
    all_to_all x1, starting transfers between devices, body(): got = lax.all_to_all(send, 'ctx', split_axis=0, concat_axis=0, tiled=True)  10.7 us
    all_to_all x1, starting transfers between devices, body(): lax.all_to_all(jnp.broadcast_to(dsc[None], (heads,) + dsc.shape), 'ctx',...  8.53 us
    all_to_all x1, waiting for transfers between devices, body(): lax.all_to_all(jnp.broadcast_to(dsc[None], (heads,) + dsc.shape), 'ctx',...  7.72 us
    all_to_all x1, starting transfers between devices, body(): home = lax.all_to_all(back, 'ctx', split_axis=0, concat_axis=0, tiled=True)  5.63 us
    ppermute x1, waiting for transfers between devices, body(): side = lax.ppermute(own, 'ctx', [(i, i ^ 2) for i in range(nctx)])  5.54 us
    pallas_call x1, Pallas kernels, body(): pl.pallas_call(attend_kernel, out_shape=(jax.ShapeDtypeStruct((nctx, slot...  5 us
  transfers between devices with their start and end apart: 6, of which 4 were waited for; matrix products, arithmetic and copies ran while one was open for 1% of the time, Pallas kernels for 2%

profile of v2, /device:TPU:2, one launch (start us, length us, event | category | flops | bytes accessed | tf_op | source)
XLA Modules:
  0.0 102.7 jit_solution(11776293763258238179)
XLA Ops:
  0.6 3.5 %pack.1 = bf16[64,40,128]{2,1,0:T(8,128)(2,1)} custom-call(s32[1]{0:T(128)} %bitcast.here_ref, s32[1,1024]{1,0:T(1,128)} %places_ref.3, f32[1,128]{1,0:T(1,128)} %logit_ref.3, bf16[128,2048]{1,0:T(8,128)(2,1)} %bitcast.18, bf16[128,2048]{1,0:T(8,128)(2,1)} %bitcast.19, bf16[128,2048]{1,0:T(8,128)(2,1)} %bitcast.20, bf16[128,2048]{1,0:T(8,128)(2,1)} %bitcast.15), custom_call_target="tpu_custom_call" | custom-call | tf_op jit(solution)/shard_map/pack/pallas_call | solution.py:225
  4.1 0.0 copy-start.1
  4.1 10.7 %all-to-all-start = ((bf16[64,40,128]{2,1,0:T(8,128)(2,1)}), bf16[64,40,128]{2,1,0:T(8,128)(2,1)S(1)}, u32[]{:S(2)}, u32[]{:S(2)}) async-start(bf16[64,40,128]{2,1,0:T(8,128)(2,1)} %pack.1), calls=%async_computation | async-start | bytes 1310720 | tf_op jit(solution)/shard_map/all_to_all | solution.py:234
  14.8 0.2 convert_reduce_fusion.before_ref
  15.0 20.2 %all-to-all-done.in_ref = bf16[64,40,128]{2,1,0:T(8,128)(2,1)S(1)} async-done(((bf16[64,40,128]{2,1,0:T(8,128)(2,1)}), bf16[64,40,128]{2,1,0:T(8,128)(2,1)S(1)}, u32[]{:S(2)}, u32[]{:S(2)}) %all-to-all-start) | async-done | bytes 655392 | tf_op jit(solution)/shard_map/all_to_all | solution.py:234
  35.2 0.7 compact.1.x0
  35.8 2.5 %collective-permute-start.1 = (bf16[1024,128]{1,0:T(8,128)(2,1)S(1)}, bf16[1024,128]{1,0:T(8,128)(2,1)S(1)}, u32[]{:S(2)}, u32[]{:S(2)}) collective-permute-start(bf16[1024,128]{1,0:T(8,128)(2,1)S(1)} %compact.1.x0), channel_id=1, source_target_pairs={{0,2},{1,3},{2,0},{3,1},{4,6},{5,7},{6,4},{7,5},{8,10},{9,11},{10,... | collective-permute-start | bytes 786440 | tf_op jit(solution)/shard_map/ppermute | solution.py:244
  38.3 1.9 %collective-permute-start = (bf16[1024,128]{1,0:T(8,128)(2,1)S(1)}, bf16[1024,128]{1,0:T(8,128)(2,1)S(1)}, u32[]{:S(2)}, u32[]{:S(2)}) collective-permute-start(bf16[1024,128]{1,0:T(8,128)(2,1)S(1)} %compact.1.x0), channel_id=1, source_target_pairs={{0,1},{1,0},{2,3},{3,2},{4,5},{5,4},{6,7},{7,6},{8,9},{9,8},{10,11... | collective-permute-start | bytes 786440 | tf_op jit(solution)/shard_map/ppermute | solution.py:245
  40.2 5.5 %collective-permute-done.1.x2 = bf16[1024,128]{1,0:T(8,128)(2,1)S(1)} collective-permute-done((bf16[1024,128]{1,0:T(8,128)(2,1)S(1)}, bf16[1024,128]{1,0:T(8,128)(2,1)S(1)}, u32[]{:S(2)}, u32[]{:S(2)}) %collective-permute-start.1) | collective-permute-done | bytes 262176 | tf_op jit(solution)/shard_map/ppermute | solution.py:244
  45.8 1.9 %collective-permute-start.2 = (bf16[1024,128]{1,0:T(8,128)(2,1)S(1)}, bf16[1024,128]{1,0:T(8,128)(2,1)S(1)}, u32[]{:S(2)}, u32[]{:S(2)}) collective-permute-start(bf16[1024,128]{1,0:T(8,128)(2,1)S(1)} %collective-permute-done.1.x2), channel_id=1, source_target_pairs={{0,1},{1,0},{2,3},{3,2},{4,5},{5,4},{6,7},{7,6},{8,9},{9,8},{10,11... | collective-permute-start | bytes 786440 | tf_op jit(solution)/shard_map/ppermute | solution.py:246
  47.7 0.0 copy-start.3
  47.7 0.6 copy-done.3
  48.4 0.6 dynamic_slice.3.scale_ref
  49.0 0.0 collective-permute-done.x1
  49.0 0.2 collective-permute-done.2.x3
  49.2 5.0 %attend.1 = (bf16[64,40,128]{2,1,0:T(8,128)(2,1)}, f32[1,128]{1,0:T(1,128)S(1)}) custom-call(s32[64]{0:T(128)S(1)} %convert_reduce_fusion.before_ref, s32[1]{0:T(128)} %bitcast.3.role_ref, s32[1]{0:T(128)} %bitcast.4.head_ref, f32[1]{0:T(128)} %dynamic_slice.3.scale_ref, bf16[1024,128]{1,0:T(8,128)(2,1)S(1)} %compact.1.x0, ...), custom_call_target="tpu_custom_call" | custom-call | tf_op jit(solution)/shard_map/attend/pallas_call | solution.py:247
  54.2 5.6 %all-to-all-start.1 = ((bf16[64,40,128]{2,1,0:T(8,128)(2,1)}), bf16[64,40,128]{2,1,0:T(8,128)(2,1)S(1)}, u32[]{:S(2)}, u32[]{:S(2)}) async-start(bf16[64,40,128]{2,1,0:T(8,128)(2,1)} %get-tuple-element.15), calls=%async_computation.1 | async-start | bytes 1310720 | tf_op jit(solution)/shard_map/all_to_all | solution.py:267
  59.8 23.2 %psum.7 = f32[1,128]{1,0:T(1,128)S(1)} all-reduce(f32[1,128]{1,0:T(1,128)S(1)} %get-tuple-element.16), channel_id=1, replica_groups=mesh['dp'=8,'ctx'=64] {'dp'}, use_global_device_ids=true, to_apply=%region_1.2 | all-reduce | flops 128 | bytes 1024 | tf_op jit(solution)/shard_map/psum | solution.py:268
  83.0 0.0 all-to-all-done.1.in_ref
  83.0 0.6 broadcast_in_dim.38
  83.6 8.5 %all-to-all-start.2 = ((f32[16,1,128]{2,1,0:T(1,128)}), f32[16,1,128]{2,1,0:T(1,128)S(1)}, u32[]{:S(2)}, u32[]{:S(2)}) async-start(f32[16,1,128]{2,1,0:T(1,128)} %broadcast_in_dim.38), calls=%async_computation.2 | async-start | bytes 16384 | tf_op jit(solution)/shard_map/all_to_all | solution.py:271
  92.2 2.3 %place.1 = (bf16[128,2048]{1,0:T(8,128)(2,1)}, bf16[128,2048]{1,0:T(8,128)(2,1)}, bf16[128,2048]{1,0:T(8,128)(2,1)}, bf16[128,2048]{1,0:T(8,128)(2,1)}, f32[1,128]{1,0:T(1,128)}) custom-call(s32[1]{0:T(128)} %bitcast.here_ref, s32[1,1024]{1,0:T(1,128)S(1)} %copy-done.1, f32[1,128]{1,0:T(1,128)S(1)} %copy-done.2, bf16[128,2048]{1,0:T(8,128)(2,1)S(1)} %bitcast.16, ...), custom_call_target="tpu_custom_call" | custom-call | tf_op jit(solution)/shard_map/place/pallas_call | solution.py:279
  94.5 7.7 %all-to-all-done.2 = f32[16,1,128]{2,1,0:T(1,128)S(1)} async-done(((f32[16,1,128]{2,1,0:T(1,128)}), f32[16,1,128]{2,1,0:T(1,128)S(1)}, u32[]{:S(2)}, u32[]{:S(2)}) %all-to-all-start.2) | async-done | bytes 8224 | tf_op jit(solution)/shard_map/all_to_all | solution.py:271
  102.2 0.5 reduce_sum.19
  (6 shorter events, 0.0 us)
Async XLA Ops:
  4.1 10.7 %copy-start.1 = (s32[1,1024]{1,0:T(1,128)S(1)}, s32[1,1024]{1,0:T(1,128)}, u32[]{:S(2)}) copy-start(s32[1,1024]{1,0:T(1,128)} %places_ref.3) | copy-start | bytes 12292
  4.1 31.0 %all-to-all-start = ((bf16[64,40,128]{2,1,0:T(8,128)(2,1)}), bf16[64,40,128]{2,1,0:T(8,128)(2,1)S(1)}, u32[]{:S(2)}, u32[]{:S(2)}) async-start(bf16[64,40,128]{2,1,0:T(8,128)(2,1)} %pack.1), calls=%async_computation | async-start | bytes 1310720 | tf_op jit(solution)/shard_map/all_to_all | solution.py:234
  35.8 9.9 %collective-permute-start.1 = (bf16[1024,128]{1,0:T(8,128)(2,1)S(1)}, bf16[1024,128]{1,0:T(8,128)(2,1)S(1)}, u32[]{:S(2)}, u32[]{:S(2)}) collective-permute-start(bf16[1024,128]{1,0:T(8,128)(2,1)S(1)} %compact.1.x0), channel_id=1, source_target_pairs={{0,2},{1,3},{2,0},{3,1},{4,6},{5,7},{6,4},{7,5},{8,10},{9,11},{10,... | collective-permute-start | bytes 786440 | tf_op jit(solution)/shard_map/ppermute | solution.py:244
  38.3 10.7 %collective-permute-start = (bf16[1024,128]{1,0:T(8,128)(2,1)S(1)}, bf16[1024,128]{1,0:T(8,128)(2,1)S(1)}, u32[]{:S(2)}, u32[]{:S(2)}) collective-permute-start(bf16[1024,128]{1,0:T(8,128)(2,1)S(1)} %compact.1.x0), channel_id=1, source_target_pairs={{0,1},{1,0},{2,3},{3,2},{4,5},{5,4},{6,7},{7,6},{8,9},{9,8},{10,11... | collective-permute-start | bytes 786440 | tf_op jit(solution)/shard_map/ppermute | solution.py:245
  45.8 3.4 %collective-permute-start.2 = (bf16[1024,128]{1,0:T(8,128)(2,1)S(1)}, bf16[1024,128]{1,0:T(8,128)(2,1)S(1)}, u32[]{:S(2)}, u32[]{:S(2)}) collective-permute-start(bf16[1024,128]{1,0:T(8,128)(2,1)S(1)} %collective-permute-done.1.x2), channel_id=1, source_target_pairs={{0,1},{1,0},{2,3},{3,2},{4,5},{5,4},{6,7},{7,6},{8,9},{9,8},{10,11... | collective-permute-start | bytes 786440 | tf_op jit(solution)/shard_map/ppermute | solution.py:246
  47.7 0.7 copy-start.3
  54.2 38.0 %copy-start = (bf16[1,128,2048]{2,1,0:T(8,128)(2,1)S(1)}, bf16[1,128,2048]{2,1,0:T(8,128)(2,1)}, u32[]{:S(2)}) copy-start(bf16[1,128,2048]{2,1,0:T(8,128)(2,1)} %param.13) | copy-start | bytes 1572868
  54.2 28.8 %all-to-all-start.1 = ((bf16[64,40,128]{2,1,0:T(8,128)(2,1)}), bf16[64,40,128]{2,1,0:T(8,128)(2,1)S(1)}, u32[]{:S(2)}, u32[]{:S(2)}) async-start(bf16[64,40,128]{2,1,0:T(8,128)(2,1)} %get-tuple-element.15), calls=%async_computation.1 | async-start | bytes 1310720 | tf_op jit(solution)/shard_map/all_to_all | solution.py:267
  83.6 8.5 %copy-start.2 = (f32[1,128]{1,0:T(1,128)S(1)}, f32[1,128]{1,0:T(1,128)}, u32[]{:S(2)}) copy-start(f32[1,128]{1,0:T(1,128)} %logit_ref.3) | copy-start | bytes 1540
  83.6 18.5 %all-to-all-start.2 = ((f32[16,1,128]{2,1,0:T(1,128)}), f32[16,1,128]{2,1,0:T(1,128)S(1)}, u32[]{:S(2)}, u32[]{:S(2)}) async-start(f32[16,1,128]{2,1,0:T(1,128)} %broadcast_in_dim.38), calls=%async_computation.2 | async-start | bytes 16384 | tf_op jit(solution)/shard_map/all_to_all | solution.py:271

commit v3 on v2

--- a/solution.py
+++ b/solution.py
@@ -41,19 +41,28 @@
     return 1.0 / (1.0 + jnp.exp(-x))
 
 
-def pack_kernel(here_ref, places_ref, logit_ref, q_ref, k_ref, v_ref, g_ref, out_ref, buf, sems):
-    tok, width = q_ref.shape
-    slots, hdim = out_ref.shape[1:]
+def pack_kernel(
+    here_ref, places_hbm, logit_hbm, q_hbm, k_hbm, v_hbm, g_hbm, out_hbm, places, logit, buf, out, sems, out_sems
+):
+    tok, width = q_hbm.shape
+    heads, _, slots, hdim = out.shape
+    small = [
+        pltpu.make_async_copy(src, dst, sems.at[PARTS + i])
+        for i, (src, dst) in enumerate(((places_hbm, places), (logit_hbm, logit)))
+    ]
     copies = [
         pltpu.make_async_copy(ref, buf.at[part], sems.at[part])
-        for part, ref in enumerate((q_ref, k_ref, v_ref, g_ref))
+        for part, ref in enumerate((q_hbm, k_hbm, v_hbm, g_hbm))
     ]
-    for copy in copies:
+    for copy in small + copies:
         copy.start()
-    row = to_row(slot_column(places_ref[...], here_ref[0] * tok, tok), tok)
+    for copy in small:
+        copy.wait()
+    row = to_row(slot_column(places[...], here_ref[0] * tok, tok), tok)
     hit = lax.broadcasted_iota(jnp.int32, (slots, tok), 0).astype(F32) + 1.0 == row
     pick = hit.astype(BF16)
-    gate = jnp.sum(jnp.where(hit, sigmoid(logit_ref[...]), 0.0), axis=1, keepdims=True)
+    gate = jnp.sum(jnp.where(hit, sigmoid(logit[...]), 0.0), axis=1, keepdims=True)
+    sends = []
     for part, copy in enumerate(copies):
         copy.wait()
         for base in range(0, width, 4 * hdim):
@@ -62,8 +71,12 @@
                 rows = rows * gate
             rows = rows.astype(BF16)
             for i in range(4):
-                head = base // hdim + i
-                out_ref[head * PARTS + part] = rows[:, i * hdim : (i + 1) * hdim]
+                out[base // hdim + i, part] = rows[:, i * hdim : (i + 1) * hdim]
+        send = pltpu.make_async_copy(out.at[:, part], out_hbm.at[:, part], out_sems.at[part])
+        send.start()
+        sends.append(send)
+    for send in sends:
+        send.wait()
 
 
 def compact_kernel(before_ref, in_ref, out_ref, buf):
@@ -79,16 +92,16 @@
 
 
 def attend_kernel(
-    before_ref, role_ref, head_ref, scale_ref, x0, x1, x2, x3, out_ref, ds_ref, arr, res, pbuf, dbuf, abuf, rbuf, gbuf
+    before_ref, here_ref, scale_ref, x0, x1, x2, x3, out_ref, ds_ref, arr, res, pbuf, dbuf, abuf, rbuf, gbuf
 ):
     shards, slots, hdim = out_ref.shape
     total = x0.shape[0]
     blk = 256
     strip = 32
     inv = 1.0 / math.sqrt(hdim)
-    role = role_ref[0]
-    scale = scale_ref[0]
-    coef = scale * inv
+    role = lax.rem(here_ref[0], PARTS)
+    head = lax.div(here_ref[0], PARTS)
+    coef = scale_ref[head] * inv
     coef2 = coef * math.log2(math.e)
     for i, ref in enumerate((x0, x1, x2, x3)):
         arr[role ^ i] = ref[...]
@@ -115,15 +128,8 @@
         row = lax.broadcasted_iota(jnp.int32, (strip, blk), 0) + (a - lo)
         return jnp.where(row <= lax.broadcasted_iota(jnp.int32, (strip, blk), 1), x, -jnp.inf)
 
-    scores(0)
-    products(0)
-    vt = v_ref[...].astype(F32).T.astype(BF16)
-    dsc = jnp.zeros((8, blk), F32)
-    for lo in blocks:
-        n = lo + blk
-        cols = slice(lo, n)
-        if n < total:
-            scores(n)
+    def softmax(lo):
+        cols = slice(lo, lo + blk)
         top = jnp.full((8, blk), -jnp.inf, F32)
         for a, rows in strips(lo):
             top = jnp.maximum(top, fold(masked(rbuf[rows, cols], a, lo), jnp.max))
@@ -135,18 +141,36 @@
         for a, rows in strips(lo):
             p = jnp.exp2(masked(rbuf[rows, cols], a, lo) * coef2 - lse)
             pbuf[rows, cols] = p.astype(BF16)
-        att = jnp.dot(vt[:, :n], pbuf[:n, cols], preferred_element_type=F32).astype(BF16)
-        abuf[:, cols] = att
-        if n < total:
-            products(n)
+        return lse
+
+    def attended(lo):
+        n = lo + blk
+        att = jnp.dot(vt[:, :n], pbuf[:n, lo:n], preferred_element_type=F32).astype(BF16)
+        abuf[:, lo:n] = att
         git = g_ref[lo:n, :].astype(F32).T
-        delta = jnp.sum(git * att.astype(F32), axis=0, keepdims=True)
+        return jnp.sum(git * att.astype(F32), axis=0, keepdims=True)
+
+    def backward(lo, lse, delta, dsc):
+        cols = slice(lo, lo + blk)
         for a, rows in strips(lo):
             raw = rbuf[rows, cols]
             ds = jnp.exp2(masked(raw, a, lo) * coef2 - lse) * (gbuf[rows, cols] - delta)
             dsc = dsc + fold(ds * raw, jnp.sum)
             dbuf[rows, cols] = ds.astype(BF16)
-    mine = lax.broadcasted_iota(jnp.int32, ds_ref.shape, 1) == head_ref[0]
+        return dsc
+
+    vt = v_ref[...].astype(F32).T.astype(BF16)
+    dsc = jnp.zeros((8, blk), F32)
+    for lo in blocks:
+        scores(lo)
+    lses = []
+    for lo in blocks:
+        lses.append(softmax(lo))
+        products(lo)
+    deltas = [attended(lo) for lo in blocks]
+    for lo, lse, delta in zip(blocks, lses, deltas):
+        dsc = backward(lo, lse, delta, dsc)
+    mine = lax.broadcasted_iota(jnp.int32, ds_ref.shape, 1) == head
     dsum = jnp.sum(jnp.sum(dsc, axis=0, keepdims=True), axis=1, keepdims=True)
     ds_ref[...] = jnp.where(mine, dsum * inv, 0.0)
 
@@ -191,16 +215,20 @@
     spread = hit.astype(BF16)
     gate_row = sigmoid(logit_ref[...])
     gate = to_col(gate_row, tok)
-    acc = jnp.zeros((tok, hdim), F32)
-    for head in range(width // hdim):
-        cols = slice(head * hdim, (head + 1) * hdim)
-        att = jnp.dot(spread, in_ref[head * PARTS], preferred_element_type=F32)
+    acc = jnp.zeros((tok, 2 * hdim), F32)
+    for head in range(0, width // hdim, 2):
+        cols = slice(head * hdim, (head + 2) * hdim)
+
+        def home(part):
+            pair = [in_ref[(head + i) * PARTS + part] for i in range(2)]
+            return jnp.dot(spread, jnp.concatenate(pair, axis=1), preferred_element_type=F32)
+
+        att = home(0)
         bo_ref[:, cols] = (gate * att).astype(BF16)
         acc = acc + g_ref[:, cols].astype(F32) * att
-        for part, ref in ((1, dq_ref), (2, dk_ref), (3, dv_ref)):
-            ref[:, cols] = jnp.dot(
-                spread, in_ref[head * PARTS + part], preferred_element_type=F32
-            ).astype(BF16)
+        dq_ref[:, cols] = home(1).astype(BF16)
+        dk_ref[:, cols] = home(2).astype(BF16)
+        dv_ref[:, cols] = home(3).astype(BF16)
     dot = to_row(jnp.sum(acc, axis=1, keepdims=True), tok)
     dl_ref[...] = gate_row * (1.0 - gate_row) * dot
 
@@ -215,22 +243,27 @@
     rows = total // nctx
     slots = rows + 3 * (rows // 2)
     here_vec = here.astype(jnp.int32)[None]
-    role = (here % PARTS).astype(jnp.int32)[None]
-    head = (here // PARTS).astype(jnp.int32)
-    scale = lax.dynamic_slice_in_dim(head_scale, head, 1)
     starts = jnp.arange(nctx, dtype=jnp.int32) * tok
     before = jnp.sum((routed[0][None, :] < starts[:, None]).astype(jnp.int32), axis=1)
     params = pltpu.CompilerParams(vmem_limit_bytes=48 * 1024 * 1024)
 
     send = pl.pallas_call(
         pack_kernel,
-        out_shape=jax.ShapeDtypeStruct((nctx, slots, hdim), BF16),
-        in_specs=[SM] + [VM] * 2 + [HB] * 4,
-        out_specs=VM,
-        scratch_shapes=[pltpu.VMEM((PARTS, tok, width), BF16), pltpu.SemaphoreType.DMA((PARTS,))],
+        out_shape=jax.ShapeDtypeStruct((heads, PARTS, slots, hdim), BF16),
+        in_specs=[SM] + [HB] * 6,
+        out_specs=HB,
+        scratch_shapes=[
+            pltpu.VMEM((1, total), jnp.int32),
+            pltpu.VMEM((1, tok), F32),
+            pltpu.VMEM((PARTS, tok, width), BF16),
+            pltpu.VMEM((heads, PARTS, slots, hdim), BF16),
+            pltpu.SemaphoreType.DMA((PARTS + 2,)),
+            pltpu.SemaphoreType.DMA((PARTS,)),
+        ],
         compiler_params=pltpu.CompilerParams(vmem_limit_bytes=60 * 1024 * 1024),
         name="pack",
     )(here_vec, routed, router_logit, queries[0], keys[0], values[0], grad_out[0])
+    send = send.reshape(nctx, slots, hdim)
     got = lax.all_to_all(send, "ctx", split_axis=0, concat_axis=0, tiled=True)
     own = pl.pallas_call(
         compact_kernel,
@@ -250,7 +283,7 @@
             jax.ShapeDtypeStruct((nctx, slots, hdim), BF16),
             jax.ShapeDtypeStruct((1, 128), F32),
         ),
-        in_specs=[SM] * 4 + [VM] * 4,
+        in_specs=[SM] * 3 + [VM] * 4,
         out_specs=(VM, VM),
         scratch_shapes=[
             pltpu.VMEM((PARTS, total, hdim), BF16),
@@ -263,10 +296,7 @@
         ],
         compiler_params=params,
         name="attend",
-    )(before, role, head[None], scale, own, near, side, cross)
-    home = lax.all_to_all(back, "ctx", split_axis=0, concat_axis=0, tiled=True)
-    dsc = lax.psum(dsc, "dp")
-    home, dsc = lax.optimization_barrier((home, dsc))
+    )(before, here_vec, head_scale, own, near, side, cross)
     groups = [[PARTS * i + j for i in range(heads)] for j in range(nctx // heads)]
     dsc = lax.all_to_all(
         jnp.broadcast_to(dsc[None], (heads,) + dsc.shape),
@@ -276,6 +306,10 @@
         axis_index_groups=groups,
         tiled=True,
     )
+    back, dsc = lax.optimization_barrier((back, dsc))
+    home = lax.all_to_all(back, "ctx", split_axis=0, concat_axis=0, tiled=True)
+    dsc = lax.psum(jnp.sum(dsc, axis=0)[:, :heads], "dp")
+    home, dsc = lax.optimization_barrier((home, dsc))
     outs = pl.pallas_call(
         place_kernel,
         out_shape=tuple([jax.ShapeDtypeStruct((tok, width), BF16)] * 4)
@@ -286,7 +320,7 @@
         name="place",
     )(here_vec, routed, router_logit, grad_out[0], home)
     block_out, d_q, d_k, d_v, d_logit = outs
-    return block_out[None], d_q[None], d_k[None], d_v[None], d_logit, jnp.sum(dsc[:, 0, :heads], axis=0)
+    return block_out[None], d_q[None], d_k[None], d_v[None], d_logit, dsc[0]
 
 
 def solution(mesh):

time: 103 us -> 97.9 us (0.950)
  blocking collectives: 23.2 us -> 37.3 us
  starting transfers between devices: 31.1 us -> 22.2 us
  waiting for transfers between devices: 33.7 us -> 27.2 us
  local copies, waits for them, and re-layouts: 1.85 us -> 0.03 us
  Pallas kernels: 11.4 us -> 9.8 us
    all_to_all x0 -> x1, blocking collectives: none -> 13.6 us  [body(): lax.all_to_all(jnp.broadcast_to(dsc[None], (heads,) + dsc.shape), 'ctx',...]
    all_to_all x1 -> x0, starting transfers between devices: 8.53 us -> none  [body(): lax.all_to_all(jnp.broadcast_to(dsc[None], (heads,) + dsc.shape), 'ctx',...]
    all_to_all x1 -> x0, waiting for transfers between devices: 7.72 us -> none  [body(): lax.all_to_all(jnp.broadcast_to(dsc[None], (heads,) + dsc.shape), 'ctx',...]
    ppermute x1, waiting for transfers between devices: 0.23 us -> 1.49 us  [body(): cross = lax.ppermute(side, 'ctx', [(i, i ^ 1) for i in range(nctx)])]
  transfers between devices with their start and end apart: 6 -> 5, of which waited for: 4 -> 3; matrix products, arithmetic and copies ran while one was open for 1% -> 0% of each run, Pallas kernels for 2% -> 0%
where the time goes in v3:
time: 97.9 us; the launch traced here: 97.4 us
  blocking collectives  37.3 us (38%)
  waiting for transfers between devices  27.2 us (28%)
  starting transfers between devices  22.2 us (23%)
  Pallas kernels  9.8 us (10%)
    psum x1, blocking collectives, body(): dsc = lax.psum(jnp.sum(dsc, axis=0)[:, :heads], 'dp')  23.7 us
    all_to_all x1, waiting for transfers between devices, body(): got = lax.all_to_all(send, 'ctx', split_axis=0, concat_axis=0, tiled=True)  20.1 us
    all_to_all x1, blocking collectives, body(): lax.all_to_all(jnp.broadcast_to(dsc[None], (heads,) + dsc.shape), 'ctx',...  13.6 us
    all_to_all x1, starting transfers between devices, body(): got = lax.all_to_all(send, 'ctx', split_axis=0, concat_axis=0, tiled=True)  10.7 us
    ppermute x1, waiting for transfers between devices, body(): side = lax.ppermute(own, 'ctx', [(i, i ^ 2) for i in range(nctx)])  5.54 us
    all_to_all x1, starting transfers between devices, body(): home = lax.all_to_all(back, 'ctx', split_axis=0, concat_axis=0, tiled=True)  5.21 us
    pallas_call x1, Pallas kernels, body(): pl.pallas_call(attend_kernel, out_shape=(jax.ShapeDtypeStruct((nctx, slot...  4.25 us
    pallas_call x1, Pallas kernels, body(): pl.pallas_call(pack_kernel, out_shape=jax.ShapeDtypeStruct((heads, PARTS,...  2.72 us
  transfers between devices with their start and end apart: 5, of which 3 were waited for; matrix products, arithmetic and copies ran while one was open for 0% of the time, Pallas kernels for 0%

profile of v3, /device:TPU:2, one launch (start us, length us, event | category | flops | bytes accessed | tf_op | source)
XLA Modules:
  0.0 97.4 jit_solution(7451636892733647709)
XLA Ops:
  0.6 2.7 %pack.1 = bf16[16,4,40,128]{3,2,1,0:T(8,128)(2,1)} custom-call(s32[1]{0:T(128)} %bitcast.here_ref, s32[1,1024]{1,0:T(1,128)} %places_ref.1, f32[1,128]{1,0:T(1,128)} %logit_ref.1, bf16[128,2048]{1,0:T(8,128)(2,1)} %bitcast.20, bf16[128,2048]{1,0:T(8,128)(2,1)} %bitcast.21, bf16[128,2048]{1,0:T(8,128)(2,1)} %bitcast.22, bf16[128,2048]{1,0:T(8,128)(2,1)} %bitcast.15), custom_call_target="tpu_custom_call" | custom-call | tf_op jit(solution)/shard_map/pack/pallas_call | solution.py:250
  3.4 0.0 copy-start.1
  3.4 10.7 %all-to-all-start = ((bf16[64,40,128]{2,1,0:T(8,128)(2,1)}), bf16[64,40,128]{2,1,0:T(8,128)(2,1)S(1)}, u32[]{:S(2)}, u32[]{:S(2)}) async-start(bf16[64,40,128]{2,1,0:T(8,128)(2,1)} %bitcast.19), calls=%async_computation | async-start | bytes 1310720 | tf_op jit(solution)/shard_map/all_to_all | solution.py:267
  14.1 0.0 copy-done.1
  14.1 0.2 convert_reduce_fusion.before_ref
  14.3 0.0 copy-start.3
  14.3 20.1 %all-to-all-done.in_ref = bf16[64,40,128]{2,1,0:T(8,128)(2,1)S(1)} async-done(((bf16[64,40,128]{2,1,0:T(8,128)(2,1)}), bf16[64,40,128]{2,1,0:T(8,128)(2,1)S(1)}, u32[]{:S(2)}, u32[]{:S(2)}) %all-to-all-start) | async-done | bytes 655392 | tf_op jit(solution)/shard_map/all_to_all | solution.py:267
  34.4 0.7 compact.1.x0
  35.1 2.5 %collective-permute-start.1 = (bf16[1024,128]{1,0:T(8,128)(2,1)S(1)}, bf16[1024,128]{1,0:T(8,128)(2,1)S(1)}, u32[]{:S(2)}, u32[]{:S(2)}) collective-permute-start(bf16[1024,128]{1,0:T(8,128)(2,1)S(1)} %compact.1.x0), channel_id=1, source_target_pairs={{0,2},{1,3},{2,0},{3,1},{4,6},{5,7},{6,4},{7,5},{8,10},{9,11},{10,... | collective-permute-start | bytes 786440 | tf_op jit(solution)/shard_map/ppermute | solution.py:277
  37.6 1.9 %collective-permute-start = (bf16[1024,128]{1,0:T(8,128)(2,1)S(1)}, bf16[1024,128]{1,0:T(8,128)(2,1)S(1)}, u32[]{:S(2)}, u32[]{:S(2)}) collective-permute-start(bf16[1024,128]{1,0:T(8,128)(2,1)S(1)} %compact.1.x0), channel_id=1, source_target_pairs={{0,1},{1,0},{2,3},{3,2},{4,5},{5,4},{6,7},{7,6},{8,9},{9,8},{10,11... | collective-permute-start | bytes 786440 | tf_op jit(solution)/shard_map/ppermute | solution.py:278
  39.5 5.5 %collective-permute-done.1.x2 = bf16[1024,128]{1,0:T(8,128)(2,1)S(1)} collective-permute-done((bf16[1024,128]{1,0:T(8,128)(2,1)S(1)}, bf16[1024,128]{1,0:T(8,128)(2,1)S(1)}, u32[]{:S(2)}, u32[]{:S(2)}) %collective-permute-start.1) | collective-permute-done | bytes 262176 | tf_op jit(solution)/shard_map/ppermute | solution.py:277
  45.0 1.9 %collective-permute-start.2 = (bf16[1024,128]{1,0:T(8,128)(2,1)S(1)}, bf16[1024,128]{1,0:T(8,128)(2,1)S(1)}, u32[]{:S(2)}, u32[]{:S(2)}) collective-permute-start(bf16[1024,128]{1,0:T(8,128)(2,1)S(1)} %collective-permute-done.1.x2), channel_id=1, source_target_pairs={{0,1},{1,0},{2,3},{3,2},{4,5},{5,4},{6,7},{7,6},{8,9},{9,8},{10,11... | collective-permute-start | bytes 786440 | tf_op jit(solution)/shard_map/ppermute | solution.py:279
  46.9 0.0 collective-permute-done.x1
  47.0 1.5 %collective-permute-done.2.x3 = bf16[1024,128]{1,0:T(8,128)(2,1)S(1)} collective-permute-done((bf16[1024,128]{1,0:T(8,128)(2,1)S(1)}, bf16[1024,128]{1,0:T(8,128)(2,1)S(1)}, u32[]{:S(2)}, u32[]{:S(2)}) %collective-permute-start.2) | collective-permute-done | bytes 262176 | tf_op jit(solution)/shard_map/ppermute | solution.py:279
  48.4 0.0 copy-done.3
  48.4 4.3 %attend.1 = (bf16[64,40,128]{2,1,0:T(8,128)(2,1)}, f32[1,128]{1,0:T(1,128)S(1)}) custom-call(s32[64]{0:T(128)S(1)} %convert_reduce_fusion.before_ref, s32[1]{0:T(128)} %bitcast.here_ref, f32[16]{0:T(128)S(1)} %copy-done.3, bf16[1024,128]{1,0:T(8,128)(2,1)S(1)} %compact.1.x0, bf16[1024,128]{1,0:T(8,128)(2,1)S(1)} %collective-permute-done.x1, ...), custom_call_target="tpu_custom_call" | custom-call | tf_op jit(solution)/shard_map/attend/pallas_call | solution.py:280
  52.7 13.6 %all_to_all.15 = f32[16,1,128]{2,1,0:T(1,128)S(1)} all-to-all(f32[16,1,128]{2,1,0:T(1,128)S(1)} %broadcast_in_dim.26), channel_id=1, replica_groups={{0,4,8,12,16,20,24,28,32,36,40,44,48,52,56,60},{1,5,9,13,17,21,25,29,33..., dimensions={0} | all-to-all | bytes 16384 | tf_op jit(solution)/shard_map/all_to_all | solution.py:301
  66.3 0.0 copy-start
  66.3 5.2 %all-to-all-start.2 = ((bf16[64,40,128]{2,1,0:T(8,128)(2,1)}), bf16[64,40,128]{2,1,0:T(8,128)(2,1)S(1)}, u32[]{:S(2)}, u32[]{:S(2)}) async-start(bf16[64,40,128]{2,1,0:T(8,128)(2,1)} %get-tuple-element.19), calls=%async_computation.2 | async-start | bytes 1310720 | tf_op jit(solution)/shard_map/all_to_all | solution.py:310
  71.6 23.7 %psum.7 = f32[1,16]{1,0:T(1,128)} all-reduce(f32[1,16]{1,0:T(1,128)S(1)} %bitcast.23), channel_id=1, replica_groups=mesh['dp'=8,'ctx'=64] {'dp'}, use_global_device_ids=true, to_apply=%region_2.0 | all-reduce | flops 16 | bytes 128 | tf_op jit(solution)/shard_map/psum | solution.py:311
  95.3 0.0 all-to-all-done.2.in_ref
  95.3 0.0 copy-done
  95.3 0.0 copy-done.2
  95.3 2.2 %place.1 = (bf16[128,2048]{1,0:T(8,128)(2,1)}, bf16[128,2048]{1,0:T(8,128)(2,1)}, bf16[128,2048]{1,0:T(8,128)(2,1)}, bf16[128,2048]{1,0:T(8,128)(2,1)}, f32[1,128]{1,0:T(1,128)}) custom-call(s32[1]{0:T(128)} %bitcast.here_ref, s32[1,1024]{1,0:T(1,128)S(1)} %copy-done.1, f32[1,128]{1,0:T(1,128)S(1)} %copy-done.2, bf16[128,2048]{1,0:T(8,128)(2,1)S(1)} %bitcast.16, ...), custom_call_target="tpu_custom_call" | custom-call | tf_op jit(solution)/shard_map/place/pallas_call | solution.py:313
  (4 shorter events, 0.0 us)
Async XLA Ops:
  3.4 10.7 %copy-start.1 = (s32[1,1024]{1,0:T(1,128)S(1)}, s32[1,1024]{1,0:T(1,128)}, u32[]{:S(2)}) copy-start(s32[1,1024]{1,0:T(1,128)} %places_ref.1) | copy-start | bytes 12292
  3.4 31.0 %all-to-all-start = ((bf16[64,40,128]{2,1,0:T(8,128)(2,1)}), bf16[64,40,128]{2,1,0:T(8,128)(2,1)S(1)}, u32[]{:S(2)}, u32[]{:S(2)}) async-start(bf16[64,40,128]{2,1,0:T(8,128)(2,1)} %bitcast.19), calls=%async_computation | async-start | bytes 1310720 | tf_op jit(solution)/shard_map/all_to_all | solution.py:267
  14.3 34.2 %copy-start.3 = (f32[16]{0:T(128)S(1)}, f32[16]{0:T(128)}, u32[]{:S(2)}) copy-start(f32[16]{0:T(128)} %scale_ref.1) | copy-start | bytes 196
  35.1 9.9 %collective-permute-start.1 = (bf16[1024,128]{1,0:T(8,128)(2,1)S(1)}, bf16[1024,128]{1,0:T(8,128)(2,1)S(1)}, u32[]{:S(2)}, u32[]{:S(2)}) collective-permute-start(bf16[1024,128]{1,0:T(8,128)(2,1)S(1)} %compact.1.x0), channel_id=1, source_target_pairs={{0,2},{1,3},{2,0},{3,1},{4,6},{5,7},{6,4},{7,5},{8,10},{9,11},{10,... | collective-permute-start | bytes 786440 | tf_op jit(solution)/shard_map/ppermute | solution.py:277
  37.6 9.4 %collective-permute-start = (bf16[1024,128]{1,0:T(8,128)(2,1)S(1)}, bf16[1024,128]{1,0:T(8,128)(2,1)S(1)}, u32[]{:S(2)}, u32[]{:S(2)}) collective-permute-start(bf16[1024,128]{1,0:T(8,128)(2,1)S(1)} %compact.1.x0), channel_id=1, source_target_pairs={{0,1},{1,0},{2,3},{3,2},{4,5},{5,4},{6,7},{7,6},{8,9},{9,8},{10,11... | collective-permute-start | bytes 786440 | tf_op jit(solution)/shard_map/ppermute | solution.py:278
  45.0 3.4 %collective-permute-start.2 = (bf16[1024,128]{1,0:T(8,128)(2,1)S(1)}, bf16[1024,128]{1,0:T(8,128)(2,1)S(1)}, u32[]{:S(2)}, u32[]{:S(2)}) collective-permute-start(bf16[1024,128]{1,0:T(8,128)(2,1)S(1)} %collective-permute-done.1.x2), channel_id=1, source_target_pairs={{0,1},{1,0},{2,3},{3,2},{4,5},{5,4},{6,7},{7,6},{8,9},{9,8},{10,11... | collective-permute-start | bytes 786440 | tf_op jit(solution)/shard_map/ppermute | solution.py:279
  66.3 29.0 %copy-start = (bf16[1,128,2048]{2,1,0:T(8,128)(2,1)S(1)}, bf16[1,128,2048]{2,1,0:T(8,128)(2,1)}, u32[]{:S(2)}) copy-start(bf16[1,128,2048]{2,1,0:T(8,128)(2,1)} %param.13) | copy-start | bytes 1572868
  66.3 29.0 %all-to-all-start.2 = ((bf16[64,40,128]{2,1,0:T(8,128)(2,1)}), bf16[64,40,128]{2,1,0:T(8,128)(2,1)S(1)}, u32[]{:S(2)}, u32[]{:S(2)}) async-start(bf16[64,40,128]{2,1,0:T(8,128)(2,1)} %get-tuple-element.19), calls=%async_computation.2 | async-start | bytes 1310720 | tf_op jit(solution)/shard_map/all_to_all | solution.py:310
  71.6 23.7 %copy-start.2 = (f32[1,128]{1,0:T(1,128)S(1)}, f32[1,128]{1,0:T(1,128)}, u32[]{:S(2)}) copy-start(f32[1,128]{1,0:T(1,128)} %logit_ref.1) | copy-start | bytes 1540

commit v4 on v3

--- a/solution.py
+++ b/solution.py
@@ -15,6 +15,9 @@
 HB = pl.BlockSpec(memory_space=pltpu.HBM)
 NT = (((1,), (1,)), ((), ()))
 PARTS = 4
+FAR = -3e38
+BLK = 256
+STRIP = 32
 
 
 def eye(n):
@@ -91,113 +94,136 @@
     return op(x.reshape(x.shape[0] // 8, 8, x.shape[1]), axis=0)
 
 
-def attend_kernel(
-    before_ref, here_ref, scale_ref, x0, x1, x2, x3, out_ref, ds_ref, arr, res, pbuf, dbuf, abuf, rbuf, gbuf
+def strips(lo):
+    return [slice(a, a + STRIP) for a in range(0, lo + BLK, STRIP)]
+
+
+def sort_arrays(here_ref, arr, refs):
+    role = lax.rem(here_ref[0], PARTS)
+    for i, ref in enumerate(refs):
+        arr[role ^ i] = ref[...]
+    return role, lax.div(here_ref[0], PARTS), [arr.at[i] for i in range(PARTS)]
+
+
+def raw_scores(k_ref, q_ref, rbuf, lo):
+    n = lo + BLK
+    raw = lax.dot_general(k_ref[:n, :], q_ref[lo:n, :], NT, preferred_element_type=F32)
+    tri = lax.broadcasted_iota(jnp.int32, (BLK, BLK), 0) <= lax.broadcasted_iota(
+        jnp.int32, (BLK, BLK), 1
+    )
+    if lo:
+        rbuf[:lo, lo:n] = raw[:lo, :]
+    rbuf[lo:n, lo:n] = jnp.where(tri, raw[lo:, :], FAR)
+
+
+def products(v_ref, g_ref, gbuf, lo):
+    n = lo + BLK
+    gbuf[:n, lo:n] = lax.dot_general(v_ref[:n, :], g_ref[lo:n, :], NT, preferred_element_type=F32)
+
+
+def stats_kernel(
+    here_ref, scale_ref, x0, x1, x2, x3, ds_ref, att_ref, lse_ref, delta_ref, arr, pbuf, rbuf, gbuf
+):
+    total, hdim = x0.shape
+    inv = 1.0 / math.sqrt(hdim)
+    _, head, (q_ref, k_ref, v_ref, g_ref) = sort_arrays(here_ref, arr, (x0, x1, x2, x3))
+    coef2 = scale_ref[head] * (inv * math.log2(math.e))
+    blocks = range(0, total, BLK)
+    for lo in blocks:
+        raw_scores(k_ref, q_ref, rbuf, lo)
+    vt = v_ref[...].astype(F32).T.astype(BF16)
+    lses = []
+    for lo in blocks:
+        cols = slice(lo, lo + BLK)
+        top = jnp.full((8, BLK), -jnp.inf, F32)
+        for rows in strips(lo):
+            top = jnp.maximum(top, fold(rbuf[rows, cols], jnp.max))
+        top = jnp.max(top, axis=0, keepdims=True) * coef2
+        acc = jnp.zeros((8, BLK), F32)
+        for rows in strips(lo):
+            acc = acc + fold(jnp.exp2(rbuf[rows, cols] * coef2 - top), jnp.sum)
+        lse = top + jnp.log2(jnp.sum(acc, axis=0, keepdims=True))
+        for rows in strips(lo):
+            pbuf[rows, cols] = jnp.exp2(rbuf[rows, cols] * coef2 - lse).astype(BF16)
+        lse_ref[:, cols] = lse
+        lses.append(lse)
+        products(v_ref, g_ref, gbuf, lo)
+    deltas = []
+    for lo in blocks:
+        n = lo + BLK
+        att = jnp.dot(vt[:, :n], pbuf[:n, lo:n], preferred_element_type=F32).astype(BF16)
+        att_ref[:, lo:n] = att
+        git = g_ref[lo:n, :].astype(F32).T
+        delta = jnp.sum(git * att.astype(F32), axis=0, keepdims=True)
+        delta_ref[:, lo:n] = delta
+        deltas.append(delta)
+    dsc = jnp.zeros((8, BLK), F32)
+    for lo, lse, delta in zip(blocks, lses, deltas):
+        cols = slice(lo, lo + BLK)
+        for rows in strips(lo):
+            raw = rbuf[rows, cols]
+            ds = jnp.exp2(raw * coef2 - lse) * (gbuf[rows, cols] - delta)
+            dsc = dsc + fold(ds * raw, jnp.sum)
+    mine = lax.broadcasted_iota(jnp.int32, ds_ref.shape, 2) == head
+    dsum = jnp.sum(jnp.sum(dsc, axis=0, keepdims=True), axis=1, keepdims=True) * inv
+    ds_ref[...] = jnp.where(mine, dsum.reshape(1, 1, 1), 0.0)
+
+
+def grads_kernel(
+    before_ref, here_ref, scale_ref, x0, x1, x2, x3, att_ref, lse_ref, delta_ref, out_ref, arr, res, wbuf, rbuf, gbuf
 ):
     shards, slots, hdim = out_ref.shape
     total = x0.shape[0]
-    blk = 256
-    strip = 32
     inv = 1.0 / math.sqrt(hdim)
-    role = lax.rem(here_ref[0], PARTS)
-    head = lax.div(here_ref[0], PARTS)
+    role, head, (q_ref, k_ref, v_ref, g_ref) = sort_arrays(here_ref, arr, (x0, x1, x2, x3))
     coef = scale_ref[head] * inv
     coef2 = coef * math.log2(math.e)
-    for i, ref in enumerate((x0, x1, x2, x3)):
-        arr[role ^ i] = ref[...]
-    q_ref, k_ref, v_ref, g_ref = (arr.at[i] for i in range(PARTS))
-    blocks = range(0, total, blk)
-
-    def scores(lo):
-        n = lo + blk
-        raw = lax.dot_general(k_ref[:n, :], q_ref[lo:n, :], NT, preferred_element_type=F32)
-        rbuf[:n, lo:n] = raw
-
-    def products(lo):
-        n = lo + blk
-        gbuf[:n, lo:n] = lax.dot_general(
-            v_ref[:n, :], g_ref[lo:n, :], NT, preferred_element_type=F32
-        )
-
-    def strips(lo):
-        return [(a, slice(a, a + strip)) for a in range(0, lo + blk, strip)]
-
-    def masked(x, a, lo):
-        if a + strip <= lo:
-            return x
-        row = lax.broadcasted_iota(jnp.int32, (strip, blk), 0) + (a - lo)
-        return jnp.where(row <= lax.broadcasted_iota(jnp.int32, (strip, blk), 1), x, -jnp.inf)
-
-    def softmax(lo):
-        cols = slice(lo, lo + blk)
-        top = jnp.full((8, blk), -jnp.inf, F32)
-        for a, rows in strips(lo):
-            top = jnp.maximum(top, fold(masked(rbuf[rows, cols], a, lo), jnp.max))
-        top = jnp.max(top, axis=0, keepdims=True) * coef2
-        acc = jnp.zeros((8, blk), F32)
-        for a, rows in strips(lo):
-            acc = acc + fold(jnp.exp2(masked(rbuf[rows, cols], a, lo) * coef2 - top), jnp.sum)
-        lse = top + jnp.log2(jnp.sum(acc, axis=0, keepdims=True))
-        for a, rows in strips(lo):
-            p = jnp.exp2(masked(rbuf[rows, cols], a, lo) * coef2 - lse)
-            pbuf[rows, cols] = p.astype(BF16)
-        return lse
-
-    def attended(lo):
-        n = lo + blk
-        att = jnp.dot(vt[:, :n], pbuf[:n, lo:n], preferred_element_type=F32).astype(BF16)
-        abuf[:, lo:n] = att
-        git = g_ref[lo:n, :].astype(F32).T
-        return jnp.sum(git * att.astype(F32), axis=0, keepdims=True)
-
-    def backward(lo, lse, delta, dsc):
-        cols = slice(lo, lo + blk)
-        for a, rows in strips(lo):
-            raw = rbuf[rows, cols]
-            ds = jnp.exp2(masked(raw, a, lo) * coef2 - lse) * (gbuf[rows, cols] - delta)
-            dsc = dsc + fold(ds * raw, jnp.sum)
-            dbuf[rows, cols] = ds.astype(BF16)
-        return dsc
-
-    vt = v_ref[...].astype(F32).T.astype(BF16)
-    dsc = jnp.zeros((8, blk), F32)
-    for lo in blocks:
-        scores(lo)
-    lses = []
-    for lo in blocks:
-        lses.append(softmax(lo))
-        products(lo)
-    deltas = [attended(lo) for lo in blocks]
-    for lo, lse, delta in zip(blocks, lses, deltas):
-        dsc = backward(lo, lse, delta, dsc)
-    mine = lax.broadcasted_iota(jnp.int32, ds_ref.shape, 1) == head
-    dsum = jnp.sum(jnp.sum(dsc, axis=0, keepdims=True), axis=1, keepdims=True)
-    ds_ref[...] = jnp.where(mine, dsum * inv, 0.0)
+    blocks = range(0, total, BLK)
 
     @pl.when(role == 0)
     def _():
-        res[:total, :] = abuf[...].astype(F32).T
+        res[:total, :] = att_ref[...].astype(F32).T
+
+    @pl.when(role == 3)
+    def _():
+        for lo in blocks:
+            raw_scores(k_ref, q_ref, rbuf, lo)
+        for lo in blocks:
+            cols = slice(lo, lo + BLK)
+            lse = lse_ref[:, cols]
+            for rows in strips(lo):
+                wbuf[rows, cols] = jnp.exp2(rbuf[rows, cols] * coef2 - lse).astype(BF16)
+        for lo in blocks:
+            res[lo : lo + BLK, :] = jnp.dot(
+                wbuf[lo : lo + BLK, lo:], g_ref[lo:, :], preferred_element_type=F32
+            )
+
+    @pl.when((role == 1) | (role == 2))
+    def _():
+        for lo in blocks:
+            raw_scores(k_ref, q_ref, rbuf, lo)
+            products(v_ref, g_ref, gbuf, lo)
+        for lo in blocks:
+            cols = slice(lo, lo + BLK)
+            lse = lse_ref[:, cols]
+            delta = delta_ref[:, cols]
+            for rows in strips(lo):
+                p = jnp.exp2(rbuf[rows, cols] * coef2 - lse)
+                wbuf[rows, cols] = (p * (gbuf[rows, cols] - delta)).astype(BF16)
 
     @pl.when(role == 1)
     def _():
         kt = k_ref[...].astype(F32).T.astype(BF16)
         for lo in blocks:
-            n = lo + blk
-            dq = jnp.dot(kt[:, :n], dbuf[:n, lo:n], preferred_element_type=F32)
+            n = lo + BLK
+            dq = jnp.dot(kt[:, :n], wbuf[:n, lo:n], preferred_element_type=F32)
             res[lo:n, :] = (coef * dq).T
 
     @pl.when(role == 2)
     def _():
         for lo in blocks:
-            res[lo : lo + blk, :] = coef * jnp.dot(
-                dbuf[lo : lo + blk, lo:], q_ref[lo:, :], preferred_element_type=F32
-            )
-
-    @pl.when(role == 3)
-    def _():
-        for lo in blocks:
-            res[lo : lo + blk, :] = jnp.dot(
-                pbuf[lo : lo + blk, lo:], g_ref[lo:, :], preferred_element_type=F32
+            res[lo : lo + BLK, :] = coef * jnp.dot(
+                wbuf[lo : lo + BLK, lo:], q_ref[lo:, :], preferred_element_type=F32
             )
 
     res[total:, :] = jnp.zeros((slots, hdim), F32)
@@ -245,7 +271,7 @@
     here_vec = here.astype(jnp.int32)[None]
     starts = jnp.arange(nctx, dtype=jnp.int32) * tok
     before = jnp.sum((routed[0][None, :] < starts[:, None]).astype(jnp.int32), axis=1)
-    params = pltpu.CompilerParams(vmem_limit_bytes=48 * 1024 * 1024)
+    params = pltpu.CompilerParams(vmem_limit_bytes=24 * 1024 * 1024)
 
     send = pl.pallas_call(
         pack_kernel,
@@ -277,29 +303,39 @@
     side = lax.ppermute(own, "ctx", [(i, i ^ 2) for i in range(nctx)])
     near = lax.ppermute(own, "ctx", [(i, i ^ 1) for i in range(nctx)])
     cross = lax.ppermute(side, "ctx", [(i, i ^ 1) for i in range(nctx)])
-    back, dsc = pl.pallas_call(
-        attend_kernel,
+    arrays = (own, near, side, cross)
+    table = [
+        pltpu.VMEM((PARTS, total, hdim), BF16),
+        pltpu.VMEM((total, total), BF16),
+        pltpu.VMEM((total, total), F32),
+        pltpu.VMEM((total, total), F32),
+    ]
+    dsc, att, lse, delta = pl.pallas_call(
+        stats_kernel,
         out_shape=(
-            jax.ShapeDtypeStruct((nctx, slots, hdim), BF16),
-            jax.ShapeDtypeStruct((1, 128), F32),
+            jax.ShapeDtypeStruct((heads, 1, 128), F32),
+            jax.ShapeDtypeStruct((hdim, total), BF16),
+            jax.ShapeDtypeStruct((1, total), F32),
+            jax.ShapeDtypeStruct((1, total), F32),
         ),
-        in_specs=[SM] * 3 + [VM] * 4,
-        out_specs=(VM, VM),
-        scratch_shapes=[
-            pltpu.VMEM((PARTS, total, hdim), BF16),
-            pltpu.VMEM((total + slots, hdim), F32),
-            pltpu.VMEM((total, total), BF16),
-            pltpu.VMEM((total, total), BF16),
-            pltpu.VMEM((hdim, total), BF16),
-            pltpu.VMEM((total, total), F32),
-            pltpu.VMEM((total, total), F32),
-        ],
+        in_specs=[SM] * 2 + [VM] * 4,
+        out_specs=(VM,) * 4,
+        scratch_shapes=table,
         compiler_params=params,
-        name="attend",
-    )(before, here_vec, head_scale, own, near, side, cross)
+        name="stats",
+    )(here_vec, head_scale, *arrays)
+    back = pl.pallas_call(
+        grads_kernel,
+        out_shape=jax.ShapeDtypeStruct((nctx, slots, hdim), BF16),
+        in_specs=[SM] * 3 + [VM] * 7,
+        out_specs=VM,
+        scratch_shapes=[table[0], pltpu.VMEM((total + slots, hdim), F32)] + table[1:],
+        compiler_params=params,
+        name="grads",
+    )(before, here_vec, head_scale, *arrays, att, lse, delta)
     groups = [[PARTS * i + j for i in range(heads)] for j in range(nctx // heads)]
     dsc = lax.all_to_all(
-        jnp.broadcast_to(dsc[None], (heads,) + dsc.shape),
+        dsc,
         "ctx",
         split_axis=0,
         concat_axis=0,

time: 97.9 us -> 97.3 us (level)
  blocking collectives: 37.3 us -> 23.7 us
  waiting for transfers between devices: 27.2 us -> 34.2 us
  starting transfers between devices: 22.2 us -> 26.2 us
  Pallas kernels: 9.8 us -> 11.7 us
    all_to_all x1 -> x0, blocking collectives: 13.6 us -> none  [body(): lax.all_to_all(jnp.broadcast_to(dsc[None], (heads,) + dsc.shape), 'ctx',...]
    all_to_all x0 -> x1, waiting for transfers between devices: none -> 7.04 us  [body(): lax.all_to_all(dsc, 'ctx', split_axis=0, concat_axis=0, axis_index_groups...]
    all_to_all x0 -> x1, starting transfers between devices: none -> 3.82 us  [body(): lax.all_to_all(dsc, 'ctx', split_axis=0, concat_axis=0, axis_index_groups...]
    pallas_call x1 -> x2, Pallas kernels: 4.25 us -> 6.13 us  [the longest x1 3.24 us: body(): pl.pallas_call(stats_kernel, out_shape=(jax.ShapeDtypeStruct((heads, 1, 1...]
  transfers between devices with their start and end apart: 5 -> 6, of which waited for: 3 -> 4; matrix products, arithmetic and copies ran while one was open for 0% -> 0% of each run, Pallas kernels for 0% -> 3%
where the time goes in v4:
time: 97.3 us; the launch traced here: 96.8 us
  waiting for transfers between devices  34.2 us (35%)
  starting transfers between devices  26.2 us (27%)
  blocking collectives  23.7 us (24%)
  Pallas kernels  11.7 us (12%)
    psum x1, blocking collectives, body(): dsc = lax.psum(jnp.sum(dsc, axis=0)[:, :heads], 'dp')  23.7 us
    all_to_all x1, waiting for transfers between devices, body(): got = lax.all_to_all(send, 'ctx', split_axis=0, concat_axis=0, tiled=True)  20.1 us
    all_to_all x1, starting transfers between devices, body(): got = lax.all_to_all(send, 'ctx', split_axis=0, concat_axis=0, tiled=True)  10.7 us
    all_to_all x1, waiting for transfers between devices, body(): lax.all_to_all(dsc, 'ctx', split_axis=0, concat_axis=0, axis_index_groups...  7.04 us
    ppermute x1, waiting for transfers between devices, body(): side = lax.ppermute(own, 'ctx', [(i, i ^ 2) for i in range(nctx)])  5.54 us
    all_to_all x1, starting transfers between devices, body(): home = lax.all_to_all(back, 'ctx', split_axis=0, concat_axis=0, tiled=True)  5.43 us
    all_to_all x1, starting transfers between devices, body(): lax.all_to_all(dsc, 'ctx', split_axis=0, concat_axis=0, axis_index_groups...  3.82 us
    pallas_call x1, Pallas kernels, body(): pl.pallas_call(stats_kernel, out_shape=(jax.ShapeDtypeStruct((heads, 1, 1...  3.24 us
  transfers between devices with their start and end apart: 6, of which 4 were waited for; matrix products, arithmetic and copies ran while one was open for 0% of the time, Pallas kernels for 3%

profile of v4, /device:TPU:2, one launch (start us, length us, event | category | flops | bytes accessed | tf_op | source)
XLA Modules:
  0.0 96.8 jit_solution(16352724498823539956)
XLA Ops:
  0.6 2.7 %pack.1 = bf16[16,4,40,128]{3,2,1,0:T(8,128)(2,1)} custom-call(s32[1]{0:T(128)} %bitcast.here_ref, s32[1,1024]{1,0:T(1,128)} %places_ref.1, f32[1,128]{1,0:T(1,128)} %logit_ref.1, bf16[128,2048]{1,0:T(8,128)(2,1)} %bitcast.18, bf16[128,2048]{1,0:T(8,128)(2,1)} %bitcast.19, bf16[128,2048]{1,0:T(8,128)(2,1)} %bitcast.20, bf16[128,2048]{1,0:T(8,128)(2,1)} %bitcast.14), custom_call_target="tpu_custom_call" | custom-call | tf_op jit(solution)/shard_map/pack/pallas_call | solution.py:276
  3.3 0.0 copy-start.1
  3.4 10.7 %all-to-all-start = ((bf16[64,40,128]{2,1,0:T(8,128)(2,1)}), bf16[64,40,128]{2,1,0:T(8,128)(2,1)S(1)}, u32[]{:S(2)}, u32[]{:S(2)}) async-start(bf16[64,40,128]{2,1,0:T(8,128)(2,1)} %bitcast.17), calls=%async_computation | async-start | bytes 1310720 | tf_op jit(solution)/shard_map/all_to_all | solution.py:293
  14.0 0.0 copy-done.1
  14.0 0.2 convert_reduce_fusion.before_ref
  14.2 0.0 copy-start.3
  14.2 20.1 %all-to-all-done.in_ref = bf16[64,40,128]{2,1,0:T(8,128)(2,1)S(1)} async-done(((bf16[64,40,128]{2,1,0:T(8,128)(2,1)}), bf16[64,40,128]{2,1,0:T(8,128)(2,1)S(1)}, u32[]{:S(2)}, u32[]{:S(2)}) %all-to-all-start) | async-done | bytes 655392 | tf_op jit(solution)/shard_map/all_to_all | solution.py:293
  34.4 0.7 compact.1.x0
  35.1 2.5 %collective-permute-start.1 = (bf16[1024,128]{1,0:T(8,128)(2,1)S(1)}, bf16[1024,128]{1,0:T(8,128)(2,1)S(1)}, u32[]{:S(2)}, u32[]{:S(2)}) collective-permute-start(bf16[1024,128]{1,0:T(8,128)(2,1)S(1)} %compact.1.x0), channel_id=1, source_target_pairs={{0,2},{1,3},{2,0},{3,1},{4,6},{5,7},{6,4},{7,5},{8,10},{9,11},{10,... | collective-permute-start | bytes 786440 | tf_op jit(solution)/shard_map/ppermute | solution.py:303
  37.5 1.9 %collective-permute-start = (bf16[1024,128]{1,0:T(8,128)(2,1)S(1)}, bf16[1024,128]{1,0:T(8,128)(2,1)S(1)}, u32[]{:S(2)}, u32[]{:S(2)}) collective-permute-start(bf16[1024,128]{1,0:T(8,128)(2,1)S(1)} %compact.1.x0), channel_id=1, source_target_pairs={{0,1},{1,0},{2,3},{3,2},{4,5},{5,4},{6,7},{7,6},{8,9},{9,8},{10,11... | collective-permute-start | bytes 786440 | tf_op jit(solution)/shard_map/ppermute | solution.py:304
  39.5 5.5 %collective-permute-done.1.x2 = bf16[1024,128]{1,0:T(8,128)(2,1)S(1)} collective-permute-done((bf16[1024,128]{1,0:T(8,128)(2,1)S(1)}, bf16[1024,128]{1,0:T(8,128)(2,1)S(1)}, u32[]{:S(2)}, u32[]{:S(2)}) %collective-permute-start.1) | collective-permute-done | bytes 262176 | tf_op jit(solution)/shard_map/ppermute | solution.py:303
  45.0 1.9 %collective-permute-start.2 = (bf16[1024,128]{1,0:T(8,128)(2,1)S(1)}, bf16[1024,128]{1,0:T(8,128)(2,1)S(1)}, u32[]{:S(2)}, u32[]{:S(2)}) collective-permute-start(bf16[1024,128]{1,0:T(8,128)(2,1)S(1)} %collective-permute-done.1.x2), channel_id=1, source_target_pairs={{0,1},{1,0},{2,3},{3,2},{4,5},{5,4},{6,7},{7,6},{8,9},{9,8},{10,11... | collective-permute-start | bytes 786440 | tf_op jit(solution)/shard_map/ppermute | solution.py:305
  46.9 0.0 collective-permute-done.x1
  46.9 1.5 %collective-permute-done.2.x3 = bf16[1024,128]{1,0:T(8,128)(2,1)S(1)} collective-permute-done((bf16[1024,128]{1,0:T(8,128)(2,1)S(1)}, bf16[1024,128]{1,0:T(8,128)(2,1)S(1)}, u32[]{:S(2)}, u32[]{:S(2)}) %collective-permute-start.2) | collective-permute-done | bytes 262176 | tf_op jit(solution)/shard_map/ppermute | solution.py:305
  48.4 0.0 copy-done.3
  48.4 3.2 %stats.1 = (f32[16,1,128]{2,1,0:T(1,128)}, bf16[128,1024]{1,0:T(8,128)(2,1)S(1)}, f32[1,1024]{1,0:T(1,128)S(1)}, f32[1,1024]{1,0:T(1,128)S(1)}) custom-call(s32[1]{0:T(128)} %bitcast.here_ref, f32[16]{0:T(128)S(1)} %copy-done.3, bf16[1024,128]{1,0:T(8,128)(2,1)S(1)} %compact.1.x0, bf16[1024,128]{1,0:T(8,128)(2,1)S(1)} %collective-permute-done.x1, ...), custom_call_target="tpu_custom_call" | custom-call | tf_op jit(solution)/shard_map/stats/pallas_call | solution.py:313
  51.7 3.8 %all-to-all-start.1 = ((f32[16,1,128]{2,1,0:T(1,128)}), f32[16,1,128]{2,1,0:T(1,128)S(1)}, u32[]{:S(2)}, u32[]{:S(2)}) async-start(f32[16,1,128]{2,1,0:T(1,128)} %get-tuple-element.22), calls=%async_computation.1 | async-start | bytes 16384 | tf_op jit(solution)/shard_map/all_to_all | solution.py:337
  55.5 2.9 %grads.1 = bf16[64,40,128]{2,1,0:T(8,128)(2,1)} custom-call(s32[64]{0:T(128)S(1)} %convert_reduce_fusion.before_ref, s32[1]{0:T(128)} %bitcast.here_ref, f32[16]{0:T(128)S(1)} %copy-done.3, bf16[1024,128]{1,0:T(8,128)(2,1)S(1)} %compact.1.x0, bf16[1024,128]{1,0:T(8,128)(2,1)S(1)} %collective-permute-done.x1, ...), custom_call_target="tpu_custom_call" | custom-call | tf_op jit(solution)/shard_map/grads/pallas_call | solution.py:327
  58.4 7.0 %all-to-all-done.1 = f32[16,1,128]{2,1,0:T(1,128)S(1)} async-done(((f32[16,1,128]{2,1,0:T(1,128)}), f32[16,1,128]{2,1,0:T(1,128)S(1)}, u32[]{:S(2)}, u32[]{:S(2)}) %all-to-all-start.1) | async-done | bytes 8224 | tf_op jit(solution)/shard_map/all_to_all | solution.py:337
  65.4 5.4 %all-to-all-start.2 = ((bf16[64,40,128]{2,1,0:T(8,128)(2,1)}), bf16[64,40,128]{2,1,0:T(8,128)(2,1)S(1)}, u32[]{:S(2)}, u32[]{:S(2)}) async-start(bf16[64,40,128]{2,1,0:T(8,128)(2,1)} %grads.1), calls=%async_computation.2 | async-start | bytes 1310720 | tf_op jit(solution)/shard_map/all_to_all | solution.py:346
  70.9 23.7 %psum.7 = f32[1,16]{1,0:T(1,128)} all-reduce(f32[1,16]{1,0:T(1,128)S(1)} %bitcast.21), channel_id=1, replica_groups=mesh['dp'=8,'ctx'=64] {'dp'}, use_global_device_ids=true, to_apply=%region_2.0 | all-reduce | flops 16 | bytes 128 | tf_op jit(solution)/shard_map/psum | solution.py:347
  94.6 0.0 all-to-all-done.2.in_ref
  94.6 0.0 copy-done
  94.6 2.2 %place.1 = (bf16[128,2048]{1,0:T(8,128)(2,1)}, bf16[128,2048]{1,0:T(8,128)(2,1)}, bf16[128,2048]{1,0:T(8,128)(2,1)}, bf16[128,2048]{1,0:T(8,128)(2,1)}, f32[1,128]{1,0:T(1,128)}) custom-call(s32[1]{0:T(128)} %bitcast.here_ref, s32[1,1024]{1,0:T(1,128)S(1)} %copy-done.1, f32[1,128]{1,0:T(1,128)S(1)} %copy-done.2, bf16[128,2048]{1,0:T(8,128)(2,1)S(1)} %bitcast.15, ...), custom_call_target="tpu_custom_call" | custom-call | tf_op jit(solution)/shard_map/place/pallas_call | solution.py:349
  (5 shorter events, 0.0 us)
Async XLA Ops:
  3.3 10.7 %copy-start.1 = (s32[1,1024]{1,0:T(1,128)S(1)}, s32[1,1024]{1,0:T(1,128)}, u32[]{:S(2)}) copy-start(s32[1,1024]{1,0:T(1,128)} %places_ref.1) | copy-start | bytes 12292
  3.4 31.0 %all-to-all-start = ((bf16[64,40,128]{2,1,0:T(8,128)(2,1)}), bf16[64,40,128]{2,1,0:T(8,128)(2,1)S(1)}, u32[]{:S(2)}, u32[]{:S(2)}) async-start(bf16[64,40,128]{2,1,0:T(8,128)(2,1)} %bitcast.17), calls=%async_computation | async-start | bytes 1310720 | tf_op jit(solution)/shard_map/all_to_all | solution.py:293
  14.2 34.2 %copy-start.3 = (f32[16]{0:T(128)S(1)}, f32[16]{0:T(128)}, u32[]{:S(2)}) copy-start(f32[16]{0:T(128)} %scale_ref.3) | copy-start | bytes 196
  35.1 9.9 %collective-permute-start.1 = (bf16[1024,128]{1,0:T(8,128)(2,1)S(1)}, bf16[1024,128]{1,0:T(8,128)(2,1)S(1)}, u32[]{:S(2)}, u32[]{:S(2)}) collective-permute-start(bf16[1024,128]{1,0:T(8,128)(2,1)S(1)} %compact.1.x0), channel_id=1, source_target_pairs={{0,2},{1,3},{2,0},{3,1},{4,6},{5,7},{6,4},{7,5},{8,10},{9,11},{10,... | collective-permute-start | bytes 786440 | tf_op jit(solution)/shard_map/ppermute | solution.py:303
  37.5 9.4 %collective-permute-start = (bf16[1024,128]{1,0:T(8,128)(2,1)S(1)}, bf16[1024,128]{1,0:T(8,128)(2,1)S(1)}, u32[]{:S(2)}, u32[]{:S(2)}) collective-permute-start(bf16[1024,128]{1,0:T(8,128)(2,1)S(1)} %compact.1.x0), channel_id=1, source_target_pairs={{0,1},{1,0},{2,3},{3,2},{4,5},{5,4},{6,7},{7,6},{8,9},{9,8},{10,11... | collective-permute-start | bytes 786440 | tf_op jit(solution)/shard_map/ppermute | solution.py:304
  45.0 3.4 %collective-permute-start.2 = (bf16[1024,128]{1,0:T(8,128)(2,1)S(1)}, bf16[1024,128]{1,0:T(8,128)(2,1)S(1)}, u32[]{:S(2)}, u32[]{:S(2)}) collective-permute-start(bf16[1024,128]{1,0:T(8,128)(2,1)S(1)} %collective-permute-done.1.x2), channel_id=1, source_target_pairs={{0,1},{1,0},{2,3},{3,2},{4,5},{5,4},{6,7},{7,6},{8,9},{9,8},{10,11... | collective-permute-start | bytes 786440 | tf_op jit(solution)/shard_map/ppermute | solution.py:305
  51.7 13.8 %all-to-all-start.1 = ((f32[16,1,128]{2,1,0:T(1,128)}), f32[16,1,128]{2,1,0:T(1,128)S(1)}, u32[]{:S(2)}, u32[]{:S(2)}) async-start(f32[16,1,128]{2,1,0:T(1,128)} %get-tuple-element.22), calls=%async_computation.1 | async-start | bytes 16384 | tf_op jit(solution)/shard_map/all_to_all | solution.py:337
  58.4 36.2 %copy-start = (bf16[1,128,2048]{2,1,0:T(8,128)(2,1)S(1)}, bf16[1,128,2048]{2,1,0:T(8,128)(2,1)}, u32[]{:S(2)}) copy-start(bf16[1,128,2048]{2,1,0:T(8,128)(2,1)} %param.13) | copy-start | bytes 1572868
  65.4 29.2 %all-to-all-start.2 = ((bf16[64,40,128]{2,1,0:T(8,128)(2,1)}), bf16[64,40,128]{2,1,0:T(8,128)(2,1)S(1)}, u32[]{:S(2)}, u32[]{:S(2)}) async-start(bf16[64,40,128]{2,1,0:T(8,128)(2,1)} %grads.1), calls=%async_computation.2 | async-start | bytes 1310720 | tf_op jit(solution)/shard_map/all_to_all | solution.py:346
  70.9 23.7 %copy-start.2 = (f32[1,128]{1,0:T(1,128)S(1)}, f32[1,128]{1,0:T(1,128)}, u32[]{:S(2)}) copy-start(f32[1,128]{1,0:T(1,128)} %logit_ref.1) | copy-start | bytes 1540

commit v5 on v4

--- a/solution.py
+++ b/solution.py
@@ -98,13 +98,6 @@
     return [slice(a, a + STRIP) for a in range(0, lo + BLK, STRIP)]
 
 
-def sort_arrays(here_ref, arr, refs):
-    role = lax.rem(here_ref[0], PARTS)
-    for i, ref in enumerate(refs):
-        arr[role ^ i] = ref[...]
-    return role, lax.div(here_ref[0], PARTS), [arr.at[i] for i in range(PARTS)]
-
-
 def raw_scores(k_ref, q_ref, rbuf, lo):
     n = lo + BLK
     raw = lax.dot_general(k_ref[:n, :], q_ref[lo:n, :], NT, preferred_element_type=F32)
@@ -121,14 +114,9 @@
     gbuf[:n, lo:n] = lax.dot_general(v_ref[:n, :], g_ref[lo:n, :], NT, preferred_element_type=F32)
 
 
-def stats_kernel(
-    here_ref, scale_ref, x0, x1, x2, x3, ds_ref, att_ref, lse_ref, delta_ref, arr, pbuf, rbuf, gbuf
-):
-    total, hdim = x0.shape
-    inv = 1.0 / math.sqrt(hdim)
-    _, head, (q_ref, k_ref, v_ref, g_ref) = sort_arrays(here_ref, arr, (x0, x1, x2, x3))
-    coef2 = scale_ref[head] * (inv * math.log2(math.e))
-    blocks = range(0, total, BLK)
+def forward(refs, rbuf, pbuf, gbuf, coef2, att_ref, lse_ref, delta_ref):
+    q_ref, k_ref, v_ref, g_ref = refs
+    blocks = range(0, q_ref.shape[0], BLK)
     for lo in blocks:
         raw_scores(k_ref, q_ref, rbuf, lo)
     vt = v_ref[...].astype(F32).T.astype(BF16)
@@ -157,73 +145,101 @@
         delta = jnp.sum(git * att.astype(F32), axis=0, keepdims=True)
         delta_ref[:, lo:n] = delta
         deltas.append(delta)
-    dsc = jnp.zeros((8, BLK), F32)
-    for lo, lse, delta in zip(blocks, lses, deltas):
-        cols = slice(lo, lo + BLK)
-        for rows in strips(lo):
-            raw = rbuf[rows, cols]
-            ds = jnp.exp2(raw * coef2 - lse) * (gbuf[rows, cols] - delta)
-            dsc = dsc + fold(ds * raw, jnp.sum)
-    mine = lax.broadcasted_iota(jnp.int32, ds_ref.shape, 2) == head
-    dsum = jnp.sum(jnp.sum(dsc, axis=0, keepdims=True), axis=1, keepdims=True) * inv
-    ds_ref[...] = jnp.where(mine, dsum.reshape(1, 1, 1), 0.0)
+    return lses, deltas
+
+
+def stats_kernel(
+    here_ref, scale_ref, x0, x1, x2, x3, ds_ref, att_ref, lse_ref, delta_ref, rest_ref, arr, pbuf, rbuf, gbuf
+):
+    total, hdim = x0.shape
+    inv = 1.0 / math.sqrt(hdim)
+    ds_ref[...] = jnp.zeros_like(ds_ref)
+
+    @pl.when(lax.rem(here_ref[0], 2) == 0)
+    def _():
+        role = lax.rem(here_ref[0], PARTS)
+        head = lax.div(here_ref[0], PARTS)
+        for i, ref in enumerate((x0, x1, x2, x3)):
+            arr[role ^ i] = ref[...]
+        rest_ref[0] = x2[...]
+        rest_ref[1] = x3[...]
+        coef2 = scale_ref[head] * (inv * math.log2(math.e))
+        refs = [arr.at[i] for i in range(PARTS)]
+        lses, deltas = forward(refs, rbuf, pbuf, gbuf, coef2, att_ref, lse_ref, delta_ref)
+        dsc = jnp.zeros((8, BLK), F32)
+        for lo, lse, delta in zip(range(0, total, BLK), lses, deltas):
+            cols = slice(lo, lo + BLK)
+            for rows in strips(lo):
+                raw = rbuf[rows, cols]
+                ds = jnp.exp2(raw * coef2 - lse) * (gbuf[rows, cols] - delta)
+                dsc = dsc + fold(ds * raw, jnp.sum)
+        mine = lax.broadcasted_iota(jnp.int32, ds_ref.shape, 2) == head
+        dsum = jnp.sum(jnp.sum(dsc, axis=0, keepdims=True), axis=1, keepdims=True) * inv
+        ds_ref[...] = jnp.where(mine, dsum.reshape(1, 1, 1), 0.0)
 
 
 def grads_kernel(
-    before_ref, here_ref, scale_ref, x0, x1, x2, x3, att_ref, lse_ref, delta_ref, out_ref, arr, res, wbuf, rbuf, gbuf
+    before_ref, here_ref, scale_ref, x0, x1, x2, x3, got, att_ref, lse_ref, delta_ref, out_ref,
+    arr, res, pbuf, rbuf, gbuf, wbuf, att_own, lse_own, delta_own,
 ):
     shards, slots, hdim = out_ref.shape
     total = x0.shape[0]
     inv = 1.0 / math.sqrt(hdim)
-    role, head, (q_ref, k_ref, v_ref, g_ref) = sort_arrays(here_ref, arr, (x0, x1, x2, x3))
-    coef = scale_ref[head] * inv
+    role = lax.rem(here_ref[0], PARTS)
+    coef = scale_ref[lax.div(here_ref[0], PARTS)] * inv
     coef2 = coef * math.log2(math.e)
     blocks = range(0, total, BLK)
-
-    @pl.when(role == 0)
-    def _():
-        res[:total, :] = att_ref[...].astype(F32).T
-
-    @pl.when(role == 3)
-    def _():
-        for lo in blocks:
-            raw_scores(k_ref, q_ref, rbuf, lo)
+    refs = [arr.at[i] for i in range(PARTS)]
+    q_ref, k_ref, v_ref, g_ref = refs
+    arr[role] = x0[...]
+    arr[role ^ 1] = x1[...]
+
+    def fill(lse_of, delta_of):
         for lo in blocks:
             cols = slice(lo, lo + BLK)
-            lse = lse_ref[:, cols]
+            lse = lse_of[:, cols]
+            delta = delta_of[:, cols]
             for rows in strips(lo):
-                wbuf[rows, cols] = jnp.exp2(rbuf[rows, cols] * coef2 - lse).astype(BF16)
-        for lo in blocks:
-            res[lo : lo + BLK, :] = jnp.dot(
-                wbuf[lo : lo + BLK, lo:], g_ref[lo:, :], preferred_element_type=F32
-            )
-
-    @pl.when((role == 1) | (role == 2))
-    def _():
+                p = jnp.exp2(rbuf[rows, cols] * coef2 - lse)
+                wbuf[rows, cols] = (p * (gbuf[rows, cols] - delta)).astype(BF16)
+
+    @pl.when(role == 0)
+    def _():
+        res[:total, :] = att_ref[...].astype(F32).T
+
+    @pl.when(role == 2)
+    def _():
+        arr[role ^ 2] = x2[...]
+        arr[role ^ 3] = x3[...]
         for lo in blocks:
             raw_scores(k_ref, q_ref, rbuf, lo)
             products(v_ref, g_ref, gbuf, lo)
+        fill(lse_ref, delta_ref)
         for lo in blocks:
-            cols = slice(lo, lo + BLK)
-            lse = lse_ref[:, cols]
-            delta = delta_ref[:, cols]
-            for rows in strips(lo):
-                p = jnp.exp2(rbuf[rows, cols] * coef2 - lse)
-                wbuf[rows, cols] = (p * (gbuf[rows, cols] - delta)).astype(BF16)
+            res[lo : lo + BLK, :] = coef * jnp.dot(
+                wbuf[lo : lo + BLK, lo:], q_ref[lo:, :], preferred_element_type=F32
+            )
+
+    @pl.when(lax.rem(role, 2) == 1)
+    def _():
+        arr[role ^ 2] = got[1]
+        arr[role ^ 3] = got[0]
+        forward(refs, rbuf, pbuf, gbuf, coef2, att_own, lse_own, delta_own)
 
     @pl.when(role == 1)
     def _():
+        fill(lse_own, delta_own)
         kt = k_ref[...].astype(F32).T.astype(BF16)
         for lo in blocks:
             n = lo + BLK
             dq = jnp.dot(kt[:, :n], wbuf[:n, lo:n], preferred_element_type=F32)
             res[lo:n, :] = (coef * dq).T
 
-    @pl.when(role == 2)
+    @pl.when(role == 3)
     def _():
         for lo in blocks:
-            res[lo : lo + BLK, :] = coef * jnp.dot(
-                wbuf[lo : lo + BLK, lo:], q_ref[lo:, :], preferred_element_type=F32
+            res[lo : lo + BLK, :] = jnp.dot(
+                pbuf[lo : lo + BLK, lo:], g_ref[lo:, :], preferred_element_type=F32
             )
 
     res[total:, :] = jnp.zeros((slots, hdim), F32)
@@ -300,9 +316,11 @@
         compiler_params=params,
         name="compact",
     )(before, got)
-    side = lax.ppermute(own, "ctx", [(i, i ^ 2) for i in range(nctx)])
+    odd = list(range(1, nctx, 2))
+    even = list(range(0, nctx, 2))
+    side = lax.ppermute(own, "ctx", [(i, i ^ 2) for i in even])
+    cross = lax.ppermute(own, "ctx", [(i, i ^ 3) for i in odd])
     near = lax.ppermute(own, "ctx", [(i, i ^ 1) for i in range(nctx)])
-    cross = lax.ppermute(side, "ctx", [(i, i ^ 1) for i in range(nctx)])
     arrays = (own, near, side, cross)
     table = [
         pltpu.VMEM((PARTS, total, hdim), BF16),
@@ -310,30 +328,39 @@
         pltpu.VMEM((total, total), F32),
         pltpu.VMEM((total, total), F32),
     ]
-    dsc, att, lse, delta = pl.pallas_call(
+    dsc, att, lse, delta, rest = pl.pallas_call(
         stats_kernel,
         out_shape=(
-            jax.ShapeDtypeStruct((heads, 1, 128), F32),
+            jax.ShapeDtypeStruct((nctx // 2, 1, 128), F32),
             jax.ShapeDtypeStruct((hdim, total), BF16),
             jax.ShapeDtypeStruct((1, total), F32),
             jax.ShapeDtypeStruct((1, total), F32),
+            jax.ShapeDtypeStruct((2, total, hdim), BF16),
         ),
         in_specs=[SM] * 2 + [VM] * 4,
-        out_specs=(VM,) * 4,
+        out_specs=(VM,) * 5,
         scratch_shapes=table,
         compiler_params=params,
         name="stats",
     )(here_vec, head_scale, *arrays)
+    got_rest = lax.ppermute(rest, "ctx", [(i, i ^ 1) for i in even])
     back = pl.pallas_call(
         grads_kernel,
         out_shape=jax.ShapeDtypeStruct((nctx, slots, hdim), BF16),
-        in_specs=[SM] * 3 + [VM] * 7,
+        in_specs=[SM] * 3 + [VM] * 8,
         out_specs=VM,
-        scratch_shapes=[table[0], pltpu.VMEM((total + slots, hdim), F32)] + table[1:],
+        scratch_shapes=[table[0], pltpu.VMEM((total + slots, hdim), F32)]
+        + table[1:]
+        + [
+            table[1],
+            pltpu.VMEM((hdim, total), BF16),
+            pltpu.VMEM((1, total), F32),
+            pltpu.VMEM((1, total), F32),
+        ],
         compiler_params=params,
         name="grads",
-    )(before, here_vec, head_scale, *arrays, att, lse, delta)
-    groups = [[PARTS * i + j for i in range(heads)] for j in range(nctx // heads)]
+    )(before, here_vec, head_scale, *arrays, got_rest, att, lse, delta)
+    groups = [[i for i in range(nctx) if i // 2 % 2 == j] for j in range(2)]
     dsc = lax.all_to_all(
         dsc,
         "ctx",

time: 97.3 us -> 95.8 us (0.985)
  waiting for transfers between devices: 34.2 us -> 31.9 us
  starting transfers between devices: 26.2 us -> 27.2 us
    ppermute x2 -> x3, waiting for transfers between devices: 7.03 us -> 4.81 us  [the longest x1 2.86 us: body(): cross = lax.ppermute(own, 'ctx', [(i, i ^ 3) for i in odd])]
    ppermute x2 -> x3, starting transfers between devices: 4.37 us -> 5.06 us  [the longest x1 2.46 us: body(): side = lax.ppermute(own, 'ctx', [(i, i ^ 2) for i in even])]
  transfers between devices with their start and end apart: 6 -> 7, of which waited for: 4 -> 4; matrix products, arithmetic and copies ran while one was open for 0% -> 0% of each run, Pallas kernels for 3% -> 3%
where the time goes in v5:
time: 95.8 us; the launch traced here: 95.3 us
  waiting for transfers between devices  31.9 us (33%)
  starting transfers between devices  27.2 us (28%)
  blocking collectives  23.7 us (25%)
  Pallas kernels  11.6 us (12%)
    psum x1, blocking collectives, body(): dsc = lax.psum(jnp.sum(dsc, axis=0)[:, :heads], 'dp')  23.7 us
    all_to_all x1, waiting for transfers between devices, body(): got = lax.all_to_all(send, 'ctx', split_axis=0, concat_axis=0, tiled=True)  20.1 us
    all_to_all x1, starting transfers between devices, body(): got = lax.all_to_all(send, 'ctx', split_axis=0, concat_axis=0, tiled=True)  10.7 us
    all_to_all x1, waiting for transfers between devices, body(): lax.all_to_all(dsc, 'ctx', split_axis=0, concat_axis=0, axis_index_groups...  6.89 us
    all_to_all x1, starting transfers between devices, body(): home = lax.all_to_all(back, 'ctx', split_axis=0, concat_axis=0, tiled=True)  5.04 us
    all_to_all x1, starting transfers between devices, body(): lax.all_to_all(dsc, 'ctx', split_axis=0, concat_axis=0, axis_index_groups...  4.53 us
    pallas_call x1, Pallas kernels, body(): pl.pallas_call(stats_kernel, out_shape=(jax.ShapeDtypeStruct((nctx // 2,...  3.29 us
    ppermute x1, waiting for transfers between devices, body(): cross = lax.ppermute(own, 'ctx', [(i, i ^ 3) for i in odd])  2.86 us
  transfers between devices with their start and end apart: 7, of which 4 were waited for; matrix products, arithmetic and copies ran while one was open for 0% of the time, Pallas kernels for 3%

profile of v5, /device:TPU:2, one launch (start us, length us, event | category | flops | bytes accessed | tf_op | source)
XLA Modules:
  0.0 95.3 jit_solution(11835015129059715775)
XLA Ops:
  0.6 2.7 %pack.1 = bf16[16,4,40,128]{3,2,1,0:T(8,128)(2,1)} custom-call(s32[1]{0:T(128)} %bitcast.here_ref, s32[1,1024]{1,0:T(1,128)} %places_ref.1, f32[1,128]{1,0:T(1,128)} %logit_ref.1, bf16[128,2048]{1,0:T(8,128)(2,1)} %bitcast.18, bf16[128,2048]{1,0:T(8,128)(2,1)} %bitcast.19, bf16[128,2048]{1,0:T(8,128)(2,1)} %bitcast.20, bf16[128,2048]{1,0:T(8,128)(2,1)} %bitcast.14), custom_call_target="tpu_custom_call" | custom-call | tf_op jit(solution)/shard_map/pack/pallas_call | solution.py:292
  3.3 0.0 copy-start.1
  3.3 10.7 %all-to-all-start = ((bf16[64,40,128]{2,1,0:T(8,128)(2,1)}), bf16[64,40,128]{2,1,0:T(8,128)(2,1)S(1)}, u32[]{:S(2)}, u32[]{:S(2)}) async-start(bf16[64,40,128]{2,1,0:T(8,128)(2,1)} %bitcast.17), calls=%async_computation | async-start | bytes 1310720 | tf_op jit(solution)/shard_map/all_to_all | solution.py:309
  14.0 0.2 convert_reduce_fusion.before_ref
  14.2 0.0 copy-start.2
  14.2 20.1 %all-to-all-done.in_ref = bf16[64,40,128]{2,1,0:T(8,128)(2,1)S(1)} async-done(((bf16[64,40,128]{2,1,0:T(8,128)(2,1)}), bf16[64,40,128]{2,1,0:T(8,128)(2,1)S(1)}, u32[]{:S(2)}, u32[]{:S(2)}) %all-to-all-start) | async-done | bytes 655392 | tf_op jit(solution)/shard_map/all_to_all | solution.py:309
  34.4 0.7 compact.1.x0
  35.1 1.3 %collective-permute-start.2 = (bf16[1024,128]{1,0:T(8,128)(2,1)S(1)}, bf16[1024,128]{1,0:T(8,128)(2,1)S(1)}, u32[]{:S(2)}, u32[]{:S(2)}) collective-permute-start(bf16[1024,128]{1,0:T(8,128)(2,1)S(1)} %compact.1.x0), channel_id=1, source_target_pairs={{1,2},{3,0},{5,6},{7,4},{9,10},{11,8},{13,14},{15,12},{17,18},{19,... | collective-permute-start | bytes 786440 | tf_op jit(solution)/shard_map/ppermute | solution.py:322
  36.4 2.5 %collective-permute-start.1 = (bf16[1024,128]{1,0:T(8,128)(2,1)S(1)}, bf16[1024,128]{1,0:T(8,128)(2,1)S(1)}, u32[]{:S(2)}, u32[]{:S(2)}) collective-permute-start(bf16[1024,128]{1,0:T(8,128)(2,1)S(1)} %compact.1.x0), channel_id=1, source_target_pairs={{0,2},{2,0},{4,6},{6,4},{8,10},{10,8},{12,14},{14,12},{16,18},{18,... | collective-permute-start | bytes 786440 | tf_op jit(solution)/shard_map/ppermute | solution.py:321
  38.8 1.9 %collective-permute-start = (bf16[1024,128]{1,0:T(8,128)(2,1)S(1)}, bf16[1024,128]{1,0:T(8,128)(2,1)S(1)}, u32[]{:S(2)}, u32[]{:S(2)}) collective-permute-start(bf16[1024,128]{1,0:T(8,128)(2,1)S(1)} %compact.1.x0), channel_id=1, source_target_pairs={{0,1},{1,0},{2,3},{3,2},{4,5},{5,4},{6,7},{7,6},{8,9},{9,8},{10,11... | collective-permute-start | bytes 786440 | tf_op jit(solution)/shard_map/ppermute | solution.py:323
  40.8 2.9 %collective-permute-done.2.x3 = bf16[1024,128]{1,0:T(8,128)(2,1)S(1)} collective-permute-done((bf16[1024,128]{1,0:T(8,128)(2,1)S(1)}, bf16[1024,128]{1,0:T(8,128)(2,1)S(1)}, u32[]{:S(2)}, u32[]{:S(2)}) %collective-permute-start.2) | collective-permute-done | bytes 262176 | tf_op jit(solution)/shard_map/ppermute | solution.py:322
  43.6 1.9 %collective-permute-done.1.x2 = bf16[1024,128]{1,0:T(8,128)(2,1)S(1)} collective-permute-done((bf16[1024,128]{1,0:T(8,128)(2,1)S(1)}, bf16[1024,128]{1,0:T(8,128)(2,1)S(1)}, u32[]{:S(2)}, u32[]{:S(2)}) %collective-permute-start.1) | collective-permute-done | bytes 262176 | tf_op jit(solution)/shard_map/ppermute | solution.py:321
  45.6 0.0 collective-permute-done.x1
  45.6 3.3 %stats.1 = (f32[32,1,128]{2,1,0:T(1,128)}, bf16[128,1024]{1,0:T(8,128)(2,1)S(1)}, f32[1,1024]{1,0:T(1,128)S(1)}, f32[1,1024]{1,0:T(1,128)S(1)}, bf16[2,1024,128]{2,1,0:T(8,128)(2,1)S(1)}) custom-call(s32[1]{0:T(128)} %bitcast.here_ref, f32[16]{0:T(128)S(1)} %copy-done.2, bf16[1024,128]{1,0:T(8,128)(2,1)S(1)} %compact.1.x0, ...), custom_call_target="tpu_custom_call" | custom-call | tf_op jit(solution)/shard_map/stats/pallas_call | solution.py:331
  48.9 1.3 %collective-permute-start.3 = (bf16[2,1024,128]{2,1,0:T(8,128)(2,1)S(1)}, bf16[2,1024,128]{2,1,0:T(8,128)(2,1)S(1)}, u32[]{:S(2)}, u32[]{:S(2)}) collective-permute-start(bf16[2,1024,128]{2,1,0:T(8,128)(2,1)S(1)} %get-tuple-element.20), channel_id=1, source_target_pairs={{0,1},{2,3},{4,5},{6,7},{8,9},{10,11},{12,13},{14,15},{16,17},{18,... | collective-permute-start | bytes 1572872 | tf_op jit(solution)/shard_map/ppermute | solution.py:346
  50.2 4.5 %all-to-all-start.1 = ((f32[32,1,128]{2,1,0:T(1,128)}), f32[32,1,128]{2,1,0:T(1,128)S(1)}, u32[]{:S(2)}, u32[]{:S(2)}) async-start(f32[32,1,128]{2,1,0:T(1,128)} %get-tuple-element.24), calls=%async_computation.1 | async-start | bytes 32768 | tf_op jit(solution)/shard_map/all_to_all | solution.py:364
  54.7 0.0 collective-permute-done.3.got
  54.7 2.8 %grads.1 = bf16[64,40,128]{2,1,0:T(8,128)(2,1)} custom-call(s32[64]{0:T(128)S(1)} %convert_reduce_fusion.before_ref, s32[1]{0:T(128)} %bitcast.here_ref, f32[16]{0:T(128)S(1)} %copy-done.2, bf16[1024,128]{1,0:T(8,128)(2,1)S(1)} %compact.1.x0, bf16[1024,128]{1,0:T(8,128)(2,1)S(1)} %collective-permute-done.x1, ...), custom_call_target="tpu_custom_call" | custom-call | tf_op jit(solution)/shard_map/grads/pallas_call | solution.py:347
  57.5 6.9 %all-to-all-done.1 = f32[32,1,128]{2,1,0:T(1,128)S(1)} async-done(((f32[32,1,128]{2,1,0:T(1,128)}), f32[32,1,128]{2,1,0:T(1,128)S(1)}, u32[]{:S(2)}, u32[]{:S(2)}) %all-to-all-start.1) | async-done | bytes 16416 | tf_op jit(solution)/shard_map/all_to_all | solution.py:364
  64.4 5.0 %all-to-all-start.2 = ((bf16[64,40,128]{2,1,0:T(8,128)(2,1)}), bf16[64,40,128]{2,1,0:T(8,128)(2,1)S(1)}, u32[]{:S(2)}, u32[]{:S(2)}) async-start(bf16[64,40,128]{2,1,0:T(8,128)(2,1)} %grads.1), calls=%async_computation.2 | async-start | bytes 1310720 | tf_op jit(solution)/shard_map/all_to_all | solution.py:373
  69.4 0.1 reduce_sum.21
  69.5 23.7 %psum.7 = f32[1,16]{1,0:T(1,128)} all-reduce(f32[1,16]{1,0:T(1,128)S(1)} %bitcast.21), channel_id=1, replica_groups=mesh['dp'=8,'ctx'=64] {'dp'}, use_global_device_ids=true, to_apply=%region_2.0 | all-reduce | flops 16 | bytes 128 | tf_op jit(solution)/shard_map/psum | solution.py:374
  93.2 0.0 all-to-all-done.2.in_ref
  93.2 2.2 %place.1 = (bf16[128,2048]{1,0:T(8,128)(2,1)}, bf16[128,2048]{1,0:T(8,128)(2,1)}, bf16[128,2048]{1,0:T(8,128)(2,1)}, bf16[128,2048]{1,0:T(8,128)(2,1)}, f32[1,128]{1,0:T(1,128)}) custom-call(s32[1]{0:T(128)} %bitcast.here_ref, s32[1,1024]{1,0:T(1,128)S(1)} %copy-done.1, f32[1,128]{1,0:T(1,128)S(1)} %copy-done.3, bf16[128,2048]{1,0:T(8,128)(2,1)S(1)} %bitcast.15, ...), custom_call_target="tpu_custom_call" | custom-call | tf_op jit(solution)/shard_map/place/pallas_call | solution.py:376
  (7 shorter events, 0.0 us)
Async XLA Ops:
  3.3 10.7 %copy-start.1 = (s32[1,1024]{1,0:T(1,128)S(1)}, s32[1,1024]{1,0:T(1,128)}, u32[]{:S(2)}) copy-start(s32[1,1024]{1,0:T(1,128)} %places_ref.1) | copy-start | bytes 12292
  3.3 31.0 %all-to-all-start = ((bf16[64,40,128]{2,1,0:T(8,128)(2,1)}), bf16[64,40,128]{2,1,0:T(8,128)(2,1)S(1)}, u32[]{:S(2)}, u32[]{:S(2)}) async-start(bf16[64,40,128]{2,1,0:T(8,128)(2,1)} %bitcast.17), calls=%async_computation | async-start | bytes 1310720 | tf_op jit(solution)/shard_map/all_to_all | solution.py:309
  14.2 31.3 %copy-start.2 = (f32[16]{0:T(128)S(1)}, f32[16]{0:T(128)}, u32[]{:S(2)}) copy-start(f32[16]{0:T(128)} %scale_ref.3) | copy-start | bytes 196
  35.1 8.6 %collective-permute-start.2 = (bf16[1024,128]{1,0:T(8,128)(2,1)S(1)}, bf16[1024,128]{1,0:T(8,128)(2,1)S(1)}, u32[]{:S(2)}, u32[]{:S(2)}) collective-permute-start(bf16[1024,128]{1,0:T(8,128)(2,1)S(1)} %compact.1.x0), channel_id=1, source_target_pairs={{1,2},{3,0},{5,6},{7,4},{9,10},{11,8},{13,14},{15,12},{17,18},{19,... | collective-permute-start | bytes 786440 | tf_op jit(solution)/shard_map/ppermute | solution.py:322
  36.4 9.2 %collective-permute-start.1 = (bf16[1024,128]{1,0:T(8,128)(2,1)S(1)}, bf16[1024,128]{1,0:T(8,128)(2,1)S(1)}, u32[]{:S(2)}, u32[]{:S(2)}) collective-permute-start(bf16[1024,128]{1,0:T(8,128)(2,1)S(1)} %compact.1.x0), channel_id=1, source_target_pairs={{0,2},{2,0},{4,6},{6,4},{8,10},{10,8},{12,14},{14,12},{16,18},{18,... | collective-permute-start | bytes 786440 | tf_op jit(solution)/shard_map/ppermute | solution.py:321
  38.8 6.7 %collective-permute-start = (bf16[1024,128]{1,0:T(8,128)(2,1)S(1)}, bf16[1024,128]{1,0:T(8,128)(2,1)S(1)}, u32[]{:S(2)}, u32[]{:S(2)}) collective-permute-start(bf16[1024,128]{1,0:T(8,128)(2,1)S(1)} %compact.1.x0), channel_id=1, source_target_pairs={{0,1},{1,0},{2,3},{3,2},{4,5},{5,4},{6,7},{7,6},{8,9},{9,8},{10,11... | collective-permute-start | bytes 786440 | tf_op jit(solution)/shard_map/ppermute | solution.py:323
  48.9 5.9 %collective-permute-start.3 = (bf16[2,1024,128]{2,1,0:T(8,128)(2,1)S(1)}, bf16[2,1024,128]{2,1,0:T(8,128)(2,1)S(1)}, u32[]{:S(2)}, u32[]{:S(2)}) collective-permute-start(bf16[2,1024,128]{2,1,0:T(8,128)(2,1)S(1)} %get-tuple-element.20), channel_id=1, source_target_pairs={{0,1},{2,3},{4,5},{6,7},{8,9},{10,11},{12,13},{14,15},{16,17},{18,... | collective-permute-start | bytes 1572872 | tf_op jit(solution)/shard_map/ppermute | solution.py:346
  50.2 14.2 %all-to-all-start.1 = ((f32[32,1,128]{2,1,0:T(1,128)}), f32[32,1,128]{2,1,0:T(1,128)S(1)}, u32[]{:S(2)}, u32[]{:S(2)}) async-start(f32[32,1,128]{2,1,0:T(1,128)} %get-tuple-element.24), calls=%async_computation.1 | async-start | bytes 32768 | tf_op jit(solution)/shard_map/all_to_all | solution.py:364
  57.5 35.7 %copy-start = (bf16[1,128,2048]{2,1,0:T(8,128)(2,1)S(1)}, bf16[1,128,2048]{2,1,0:T(8,128)(2,1)}, u32[]{:S(2)}) copy-start(bf16[1,128,2048]{2,1,0:T(8,128)(2,1)} %param.13) | copy-start | bytes 1572868
  64.4 28.8 %all-to-all-start.2 = ((bf16[64,40,128]{2,1,0:T(8,128)(2,1)}), bf16[64,40,128]{2,1,0:T(8,128)(2,1)S(1)}, u32[]{:S(2)}, u32[]{:S(2)}) async-start(bf16[64,40,128]{2,1,0:T(8,128)(2,1)} %grads.1), calls=%async_computation.2 | async-start | bytes 1310720 | tf_op jit(solution)/shard_map/all_to_all | solution.py:373
  69.5 23.7 %copy-start.3 = (f32[1,128]{1,0:T(1,128)S(1)}, f32[1,128]{1,0:T(1,128)}, u32[]{:S(2)}) copy-start(f32[1,128]{1,0:T(1,128)} %logit_ref.1) | copy-start | bytes 1540

commit v6 on v5

--- a/solution.py
+++ b/solution.py
@@ -45,10 +45,10 @@
 
 
 def pack_kernel(
-    here_ref, places_hbm, logit_hbm, q_hbm, k_hbm, v_hbm, g_hbm, out_hbm, places, logit, buf, out, sems, out_sems
+    here_ref, places_hbm, logit_hbm, q_hbm, k_hbm, v_hbm, g_hbm, out_ref, places, logit, buf, sems
 ):
     tok, width = q_hbm.shape
-    heads, _, slots, hdim = out.shape
+    slots, hdim = out_ref.shape[1:]
     small = [
         pltpu.make_async_copy(src, dst, sems.at[PARTS + i])
         for i, (src, dst) in enumerate(((places_hbm, places), (logit_hbm, logit)))
@@ -65,7 +65,6 @@
     hit = lax.broadcasted_iota(jnp.int32, (slots, tok), 0).astype(F32) + 1.0 == row
     pick = hit.astype(BF16)
     gate = jnp.sum(jnp.where(hit, sigmoid(logit[...]), 0.0), axis=1, keepdims=True)
-    sends = []
     for part, copy in enumerate(copies):
         copy.wait()
         for base in range(0, width, 4 * hdim):
@@ -74,12 +73,8 @@
                 rows = rows * gate
             rows = rows.astype(BF16)
             for i in range(4):
-                out[base // hdim + i, part] = rows[:, i * hdim : (i + 1) * hdim]
-        send = pltpu.make_async_copy(out.at[:, part], out_hbm.at[:, part], out_sems.at[part])
-        send.start()
-        sends.append(send)
-    for send in sends:
-        send.wait()
+                head = base // hdim + i
+                out_ref[head * PARTS + part] = rows[:, i * hdim : (i + 1) * hdim]
 
 
 def compact_kernel(before_ref, in_ref, out_ref, buf):
@@ -291,21 +286,18 @@
 
     send = pl.pallas_call(
         pack_kernel,
-        out_shape=jax.ShapeDtypeStruct((heads, PARTS, slots, hdim), BF16),
+        out_shape=jax.ShapeDtypeStruct((nctx, slots, hdim), BF16),
         in_specs=[SM] + [HB] * 6,
-        out_specs=HB,
+        out_specs=VM,
         scratch_shapes=[
             pltpu.VMEM((1, total), jnp.int32),
             pltpu.VMEM((1, tok), F32),
             pltpu.VMEM((PARTS, tok, width), BF16),
-            pltpu.VMEM((heads, PARTS, slots, hdim), BF16),
             pltpu.SemaphoreType.DMA((PARTS + 2,)),
-            pltpu.SemaphoreType.DMA((PARTS,)),
         ],
         compiler_params=pltpu.CompilerParams(vmem_limit_bytes=60 * 1024 * 1024),
         name="pack",
     )(here_vec, routed, router_logit, queries[0], keys[0], values[0], grad_out[0])
-    send = send.reshape(nctx, slots, hdim)
     got = lax.all_to_all(send, "ctx", split_axis=0, concat_axis=0, tiled=True)
     own = pl.pallas_call(
         compact_kernel,

time: 95.8 us -> 96 us (level)
  no operation moved by 1% of the time
where the time goes in v6:
time: 96 us; the launch traced here: 95.5 us
  waiting for transfers between devices  31.9 us (33%)
  starting transfers between devices  27.2 us (28%)
  blocking collectives  23.7 us (25%)
  Pallas kernels  11.7 us (12%)
    psum x1, blocking collectives, body(): dsc = lax.psum(jnp.sum(dsc, axis=0)[:, :heads], 'dp')  23.7 us
    all_to_all x1, waiting for transfers between devices, body(): got = lax.all_to_all(send, 'ctx', split_axis=0, concat_axis=0, tiled=True)  20.1 us
    all_to_all x1, starting transfers between devices, body(): got = lax.all_to_all(send, 'ctx', split_axis=0, concat_axis=0, tiled=True)  10.7 us
    all_to_all x1, waiting for transfers between devices, body(): lax.all_to_all(dsc, 'ctx', split_axis=0, concat_axis=0, axis_index_groups...  6.89 us
    all_to_all x1, starting transfers between devices, body(): home = lax.all_to_all(back, 'ctx', split_axis=0, concat_axis=0, tiled=True)  5.04 us
    all_to_all x1, starting transfers between devices, body(): lax.all_to_all(dsc, 'ctx', split_axis=0, concat_axis=0, axis_index_groups...  4.53 us
    pallas_call x1, Pallas kernels, body(): pl.pallas_call(stats_kernel, out_shape=(jax.ShapeDtypeStruct((nctx // 2,...  3.29 us
    ppermute x1, waiting for transfers between devices, body(): cross = lax.ppermute(own, 'ctx', [(i, i ^ 3) for i in odd])  2.86 us
  transfers between devices with their start and end apart: 7, of which 4 were waited for; matrix products, arithmetic and copies ran while one was open for 0% of the time, Pallas kernels for 3%

profile of v6, /device:TPU:2, one launch (start us, length us, event | category | flops | bytes accessed | tf_op | source)
XLA Modules:
  0.0 95.5 jit_solution(15809817309902911296)
XLA Ops:
  0.6 2.8 %pack.1 = bf16[64,40,128]{2,1,0:T(8,128)(2,1)} custom-call(s32[1]{0:T(128)} %bitcast.here_ref, s32[1,1024]{1,0:T(1,128)} %places_ref.1, f32[1,128]{1,0:T(1,128)} %logit_ref.1, bf16[128,2048]{1,0:T(8,128)(2,1)} %bitcast.16, bf16[128,2048]{1,0:T(8,128)(2,1)} %bitcast.17, bf16[128,2048]{1,0:T(8,128)(2,1)} %bitcast.18, bf16[128,2048]{1,0:T(8,128)(2,1)} %bitcast.13), custom_call_target="tpu_custom_call" | custom-call | tf_op jit(solution)/shard_map/pack/pallas_call | solution.py:287
  3.5 0.0 copy-start.1
  3.5 10.7 %all-to-all-start = ((bf16[64,40,128]{2,1,0:T(8,128)(2,1)}), bf16[64,40,128]{2,1,0:T(8,128)(2,1)S(1)}, u32[]{:S(2)}, u32[]{:S(2)}) async-start(bf16[64,40,128]{2,1,0:T(8,128)(2,1)} %pack.1), calls=%async_computation | async-start | bytes 1310720 | tf_op jit(solution)/shard_map/all_to_all | solution.py:301
  14.2 0.2 convert_reduce_fusion.before_ref
  14.4 0.0 copy-start.2
  14.4 20.1 %all-to-all-done.in_ref = bf16[64,40,128]{2,1,0:T(8,128)(2,1)S(1)} async-done(((bf16[64,40,128]{2,1,0:T(8,128)(2,1)}), bf16[64,40,128]{2,1,0:T(8,128)(2,1)S(1)}, u32[]{:S(2)}, u32[]{:S(2)}) %all-to-all-start) | async-done | bytes 655392 | tf_op jit(solution)/shard_map/all_to_all | solution.py:301
  34.5 0.7 compact.1.x0
  35.2 1.3 %collective-permute-start.2 = (bf16[1024,128]{1,0:T(8,128)(2,1)S(1)}, bf16[1024,128]{1,0:T(8,128)(2,1)S(1)}, u32[]{:S(2)}, u32[]{:S(2)}) collective-permute-start(bf16[1024,128]{1,0:T(8,128)(2,1)S(1)} %compact.1.x0), channel_id=1, source_target_pairs={{1,2},{3,0},{5,6},{7,4},{9,10},{11,8},{13,14},{15,12},{17,18},{19,... | collective-permute-start | bytes 786440 | tf_op jit(solution)/shard_map/ppermute | solution.py:314
  36.5 2.5 %collective-permute-start.1 = (bf16[1024,128]{1,0:T(8,128)(2,1)S(1)}, bf16[1024,128]{1,0:T(8,128)(2,1)S(1)}, u32[]{:S(2)}, u32[]{:S(2)}) collective-permute-start(bf16[1024,128]{1,0:T(8,128)(2,1)S(1)} %compact.1.x0), channel_id=1, source_target_pairs={{0,2},{2,0},{4,6},{6,4},{8,10},{10,8},{12,14},{14,12},{16,18},{18,... | collective-permute-start | bytes 786440 | tf_op jit(solution)/shard_map/ppermute | solution.py:313
  39.0 1.9 %collective-permute-start = (bf16[1024,128]{1,0:T(8,128)(2,1)S(1)}, bf16[1024,128]{1,0:T(8,128)(2,1)S(1)}, u32[]{:S(2)}, u32[]{:S(2)}) collective-permute-start(bf16[1024,128]{1,0:T(8,128)(2,1)S(1)} %compact.1.x0), channel_id=1, source_target_pairs={{0,1},{1,0},{2,3},{3,2},{4,5},{5,4},{6,7},{7,6},{8,9},{9,8},{10,11... | collective-permute-start | bytes 786440 | tf_op jit(solution)/shard_map/ppermute | solution.py:315
  40.9 2.9 %collective-permute-done.2.x3 = bf16[1024,128]{1,0:T(8,128)(2,1)S(1)} collective-permute-done((bf16[1024,128]{1,0:T(8,128)(2,1)S(1)}, bf16[1024,128]{1,0:T(8,128)(2,1)S(1)}, u32[]{:S(2)}, u32[]{:S(2)}) %collective-permute-start.2) | collective-permute-done | bytes 262176 | tf_op jit(solution)/shard_map/ppermute | solution.py:314
  43.8 1.9 %collective-permute-done.1.x2 = bf16[1024,128]{1,0:T(8,128)(2,1)S(1)} collective-permute-done((bf16[1024,128]{1,0:T(8,128)(2,1)S(1)}, bf16[1024,128]{1,0:T(8,128)(2,1)S(1)}, u32[]{:S(2)}, u32[]{:S(2)}) %collective-permute-start.1) | collective-permute-done | bytes 262176 | tf_op jit(solution)/shard_map/ppermute | solution.py:313
  45.7 0.0 collective-permute-done.x1
  45.7 3.3 %stats.1 = (f32[32,1,128]{2,1,0:T(1,128)}, bf16[128,1024]{1,0:T(8,128)(2,1)S(1)}, f32[1,1024]{1,0:T(1,128)S(1)}, f32[1,1024]{1,0:T(1,128)S(1)}, bf16[2,1024,128]{2,1,0:T(8,128)(2,1)S(1)}) custom-call(s32[1]{0:T(128)} %bitcast.here_ref, f32[16]{0:T(128)S(1)} %copy-done.2, bf16[1024,128]{1,0:T(8,128)(2,1)S(1)} %compact.1.x0, ...), custom_call_target="tpu_custom_call" | custom-call | tf_op jit(solution)/shard_map/stats/pallas_call | solution.py:323
  49.0 1.3 %collective-permute-start.3 = (bf16[2,1024,128]{2,1,0:T(8,128)(2,1)S(1)}, bf16[2,1024,128]{2,1,0:T(8,128)(2,1)S(1)}, u32[]{:S(2)}, u32[]{:S(2)}) collective-permute-start(bf16[2,1024,128]{2,1,0:T(8,128)(2,1)S(1)} %get-tuple-element.20), channel_id=1, source_target_pairs={{0,1},{2,3},{4,5},{6,7},{8,9},{10,11},{12,13},{14,15},{16,17},{18,... | collective-permute-start | bytes 1572872 | tf_op jit(solution)/shard_map/ppermute | solution.py:338
  50.3 4.5 %all-to-all-start.1 = ((f32[32,1,128]{2,1,0:T(1,128)}), f32[32,1,128]{2,1,0:T(1,128)S(1)}, u32[]{:S(2)}, u32[]{:S(2)}) async-start(f32[32,1,128]{2,1,0:T(1,128)} %get-tuple-element.24), calls=%async_computation.1 | async-start | bytes 32768 | tf_op jit(solution)/shard_map/all_to_all | solution.py:356
  54.9 0.0 collective-permute-done.3.got
  54.9 2.8 %grads.1 = bf16[64,40,128]{2,1,0:T(8,128)(2,1)} custom-call(s32[64]{0:T(128)S(1)} %convert_reduce_fusion.before_ref, s32[1]{0:T(128)} %bitcast.here_ref, f32[16]{0:T(128)S(1)} %copy-done.2, bf16[1024,128]{1,0:T(8,128)(2,1)S(1)} %compact.1.x0, bf16[1024,128]{1,0:T(8,128)(2,1)S(1)} %collective-permute-done.x1, ...), custom_call_target="tpu_custom_call" | custom-call | tf_op jit(solution)/shard_map/grads/pallas_call | solution.py:339
  57.6 6.9 %all-to-all-done.1 = f32[32,1,128]{2,1,0:T(1,128)S(1)} async-done(((f32[32,1,128]{2,1,0:T(1,128)}), f32[32,1,128]{2,1,0:T(1,128)S(1)}, u32[]{:S(2)}, u32[]{:S(2)}) %all-to-all-start.1) | async-done | bytes 16416 | tf_op jit(solution)/shard_map/all_to_all | solution.py:356
  64.5 5.0 %all-to-all-start.2 = ((bf16[64,40,128]{2,1,0:T(8,128)(2,1)}), bf16[64,40,128]{2,1,0:T(8,128)(2,1)S(1)}, u32[]{:S(2)}, u32[]{:S(2)}) async-start(bf16[64,40,128]{2,1,0:T(8,128)(2,1)} %grads.1), calls=%async_computation.2 | async-start | bytes 1310720 | tf_op jit(solution)/shard_map/all_to_all | solution.py:365
  69.6 0.1 reduce_sum.21
  69.6 23.7 %psum.7 = f32[1,16]{1,0:T(1,128)} all-reduce(f32[1,16]{1,0:T(1,128)S(1)} %bitcast.19), channel_id=1, replica_groups=mesh['dp'=8,'ctx'=64] {'dp'}, use_global_device_ids=true, to_apply=%region_2.0 | all-reduce | flops 16 | bytes 128 | tf_op jit(solution)/shard_map/psum | solution.py:366
  93.3 0.0 all-to-all-done.2.in_ref
  93.3 2.2 %place.1 = (bf16[128,2048]{1,0:T(8,128)(2,1)}, bf16[128,2048]{1,0:T(8,128)(2,1)}, bf16[128,2048]{1,0:T(8,128)(2,1)}, bf16[128,2048]{1,0:T(8,128)(2,1)}, f32[1,128]{1,0:T(1,128)}) custom-call(s32[1]{0:T(128)} %bitcast.here_ref, s32[1,1024]{1,0:T(1,128)S(1)} %copy-done.1, f32[1,128]{1,0:T(1,128)S(1)} %copy-done.3, bf16[128,2048]{1,0:T(8,128)(2,1)S(1)} %bitcast.14, ...), custom_call_target="tpu_custom_call" | custom-call | tf_op jit(solution)/shard_map/place/pallas_call | solution.py:368
  (7 shorter events, 0.0 us)
Async XLA Ops:
  3.5 10.7 %copy-start.1 = (s32[1,1024]{1,0:T(1,128)S(1)}, s32[1,1024]{1,0:T(1,128)}, u32[]{:S(2)}) copy-start(s32[1,1024]{1,0:T(1,128)} %places_ref.1) | copy-start | bytes 12292
  3.5 31.0 %all-to-all-start = ((bf16[64,40,128]{2,1,0:T(8,128)(2,1)}), bf16[64,40,128]{2,1,0:T(8,128)(2,1)S(1)}, u32[]{:S(2)}, u32[]{:S(2)}) async-start(bf16[64,40,128]{2,1,0:T(8,128)(2,1)} %pack.1), calls=%async_computation | async-start | bytes 1310720 | tf_op jit(solution)/shard_map/all_to_all | solution.py:301
  14.4 31.3 %copy-start.2 = (f32[16]{0:T(128)S(1)}, f32[16]{0:T(128)}, u32[]{:S(2)}) copy-start(f32[16]{0:T(128)} %scale_ref.3) | copy-start | bytes 196
  35.2 8.6 %collective-permute-start.2 = (bf16[1024,128]{1,0:T(8,128)(2,1)S(1)}, bf16[1024,128]{1,0:T(8,128)(2,1)S(1)}, u32[]{:S(2)}, u32[]{:S(2)}) collective-permute-start(bf16[1024,128]{1,0:T(8,128)(2,1)S(1)} %compact.1.x0), channel_id=1, source_target_pairs={{1,2},{3,0},{5,6},{7,4},{9,10},{11,8},{13,14},{15,12},{17,18},{19,... | collective-permute-start | bytes 786440 | tf_op jit(solution)/shard_map/ppermute | solution.py:314
  36.5 9.2 %collective-permute-start.1 = (bf16[1024,128]{1,0:T(8,128)(2,1)S(1)}, bf16[1024,128]{1,0:T(8,128)(2,1)S(1)}, u32[]{:S(2)}, u32[]{:S(2)}) collective-permute-start(bf16[1024,128]{1,0:T(8,128)(2,1)S(1)} %compact.1.x0), channel_id=1, source_target_pairs={{0,2},{2,0},{4,6},{6,4},{8,10},{10,8},{12,14},{14,12},{16,18},{18,... | collective-permute-start | bytes 786440 | tf_op jit(solution)/shard_map/ppermute | solution.py:313
  39.0 6.7 %collective-permute-start = (bf16[1024,128]{1,0:T(8,128)(2,1)S(1)}, bf16[1024,128]{1,0:T(8,128)(2,1)S(1)}, u32[]{:S(2)}, u32[]{:S(2)}) collective-permute-start(bf16[1024,128]{1,0:T(8,128)(2,1)S(1)} %compact.1.x0), channel_id=1, source_target_pairs={{0,1},{1,0},{2,3},{3,2},{4,5},{5,4},{6,7},{7,6},{8,9},{9,8},{10,11... | collective-permute-start | bytes 786440 | tf_op jit(solution)/shard_map/ppermute | solution.py:315
  49.0 5.9 %collective-permute-start.3 = (bf16[2,1024,128]{2,1,0:T(8,128)(2,1)S(1)}, bf16[2,1024,128]{2,1,0:T(8,128)(2,1)S(1)}, u32[]{:S(2)}, u32[]{:S(2)}) collective-permute-start(bf16[2,1024,128]{2,1,0:T(8,128)(2,1)S(1)} %get-tuple-element.20), channel_id=1, source_target_pairs={{0,1},{2,3},{4,5},{6,7},{8,9},{10,11},{12,13},{14,15},{16,17},{18,... | collective-permute-start | bytes 1572872 | tf_op jit(solution)/shard_map/ppermute | solution.py:338
  50.3 14.2 %all-to-all-start.1 = ((f32[32,1,128]{2,1,0:T(1,128)}), f32[32,1,128]{2,1,0:T(1,128)S(1)}, u32[]{:S(2)}, u32[]{:S(2)}) async-start(f32[32,1,128]{2,1,0:T(1,128)} %get-tuple-element.24), calls=%async_computation.1 | async-start | bytes 32768 | tf_op jit(solution)/shard_map/all_to_all | solution.py:356
  57.6 35.7 %copy-start = (bf16[1,128,2048]{2,1,0:T(8,128)(2,1)S(1)}, bf16[1,128,2048]{2,1,0:T(8,128)(2,1)}, u32[]{:S(2)}) copy-start(bf16[1,128,2048]{2,1,0:T(8,128)(2,1)} %param.13) | copy-start | bytes 1572868
  64.5 28.8 %all-to-all-start.2 = ((bf16[64,40,128]{2,1,0:T(8,128)(2,1)}), bf16[64,40,128]{2,1,0:T(8,128)(2,1)S(1)}, u32[]{:S(2)}, u32[]{:S(2)}) async-start(bf16[64,40,128]{2,1,0:T(8,128)(2,1)} %grads.1), calls=%async_computation.2 | async-start | bytes 1310720 | tf_op jit(solution)/shard_map/all_to_all | solution.py:365
  69.6 23.7 %copy-start.3 = (f32[1,128]{1,0:T(1,128)S(1)}, f32[1,128]{1,0:T(1,128)}, u32[]{:S(2)}) copy-start(f32[1,128]{1,0:T(1,128)} %logit_ref.1) | copy-start | bytes 1540

commit v7 on v6

--- a/solution.py
+++ b/solution.py
@@ -174,7 +174,8 @@
 
 
 def grads_kernel(
-    before_ref, here_ref, scale_ref, x0, x1, x2, x3, got, att_ref, lse_ref, delta_ref, out_ref,
+    before_ref, here_ref, scale_ref, x0, x1, x2, x3, got, att_ref, lse_ref, delta_ref, places_ref, logit_ref,
+    out_ref, spread_ref, gate_ref, slope_ref,
     arr, res, pbuf, rbuf, gbuf, wbuf, att_own, lse_own, delta_own,
 ):
     shards, slots, hdim = out_ref.shape
@@ -188,6 +189,13 @@
     q_ref, k_ref, v_ref, g_ref = refs
     arr[role] = x0[...]
     arr[role ^ 1] = x1[...]
+    tok = spread_ref.shape[0]
+    col = slot_column(places_ref[...], here_ref[0] * tok, tok)
+    slot = lax.broadcasted_iota(jnp.int32, (tok, slots), 1).astype(F32) + 1.0
+    spread_ref[...] = (slot == col).astype(BF16)
+    row = sigmoid(logit_ref[...])
+    gate_ref[...] = jnp.broadcast_to(to_col(row, tok), gate_ref.shape)
+    slope_ref[...] = row * (1.0 - row)
 
     def fill(lse_of, delta_of):
         for lo in blocks:
@@ -243,15 +251,12 @@
 
 
 def place_kernel(
-    here_ref, places_ref, logit_ref, g_ref, in_ref, bo_ref, dq_ref, dk_ref, dv_ref, dl_ref
+    spread_ref, gate_ref, slope_ref, g_ref, in_ref, bo_ref, dq_ref, dk_ref, dv_ref, dl_ref
 ):
     tok, width = g_ref.shape
-    slots, hdim = in_ref.shape[1:]
-    col = slot_column(places_ref[...], here_ref[0] * tok, tok)
-    hit = lax.broadcasted_iota(jnp.int32, (tok, slots), 1).astype(F32) + 1.0 == col
-    spread = hit.astype(BF16)
-    gate_row = sigmoid(logit_ref[...])
-    gate = to_col(gate_row, tok)
+    hdim = in_ref.shape[2]
+    spread = spread_ref[...]
+    gate = gate_ref[...]
     acc = jnp.zeros((tok, 2 * hdim), F32)
     for head in range(0, width // hdim, 2):
         cols = slice(head * hdim, (head + 2) * hdim)
@@ -267,7 +272,7 @@
         dk_ref[:, cols] = home(2).astype(BF16)
         dv_ref[:, cols] = home(3).astype(BF16)
     dot = to_row(jnp.sum(acc, axis=1, keepdims=True), tok)
-    dl_ref[...] = gate_row * (1.0 - gate_row) * dot
+    dl_ref[...] = slope_ref[...] * dot
 
 
 def body(queries, keys, values, router_logit, head_scale, routed, grad_out):
@@ -336,11 +341,16 @@
         name="stats",
     )(here_vec, head_scale, *arrays)
     got_rest = lax.ppermute(rest, "ctx", [(i, i ^ 1) for i in even])
-    back = pl.pallas_call(
+    back, spread, gates, slope = pl.pallas_call(
         grads_kernel,
-        out_shape=jax.ShapeDtypeStruct((nctx, slots, hdim), BF16),
-        in_specs=[SM] * 3 + [VM] * 8,
-        out_specs=VM,
+        out_shape=(
+            jax.ShapeDtypeStruct((nctx, slots, hdim), BF16),
+            jax.ShapeDtypeStruct((tok, slots), BF16),
+            jax.ShapeDtypeStruct((tok, 2 * hdim), F32),
+            jax.ShapeDtypeStruct((1, tok), F32),
+        ),
+        in_specs=[SM] * 3 + [VM] * 10,
+        out_specs=(VM,) * 4,
         scratch_shapes=[table[0], pltpu.VMEM((total + slots, hdim), F32)]
         + table[1:]
         + [
@@ -351,7 +361,7 @@
         ],
         compiler_params=params,
         name="grads",
-    )(before, here_vec, head_scale, *arrays, got_rest, att, lse, delta)
+    )(before, here_vec, head_scale, *arrays, got_rest, att, lse, delta, routed, router_logit)
     groups = [[i for i in range(nctx) if i // 2 % 2 == j] for j in range(2)]
     dsc = lax.all_to_all(
         dsc,
@@ -369,11 +379,11 @@
         place_kernel,
         out_shape=tuple([jax.ShapeDtypeStruct((tok, width), BF16)] * 4)
         + (jax.ShapeDtypeStruct((1, tok), F32),),
-        in_specs=[SM] + [VM] * 4,
+        in_specs=[VM] * 5,
         out_specs=(VM,) * 5,
         compiler_params=params,
         name="place",
-    )(here_vec, routed, router_logit, grad_out[0], home)
+    )(spread, gates, slope, grad_out[0], home)
     block_out, d_q, d_k, d_v, d_logit = outs
     return block_out[None], d_q[None], d_k[None], d_v[None], d_logit, dsc[0]
 

time: 96 us -> 96.6 us (level)
  no operation moved by 1% of the time
where the time goes in v7:
time: 96.6 us; the launch traced here: 96.1 us
  waiting for transfers between devices  31 us (32%)
  starting transfers between devices  28 us (29%)
  blocking collectives  23.7 us (25%)
  Pallas kernels  11.7 us (12%)
    psum x1, blocking collectives, body(): dsc = lax.psum(jnp.sum(dsc, axis=0)[:, :heads], 'dp')  23.7 us
    all_to_all x1, waiting for transfers between devices, body(): got = lax.all_to_all(send, 'ctx', split_axis=0, concat_axis=0, tiled=True)  20.1 us
    all_to_all x1, starting transfers between devices, body(): got = lax.all_to_all(send, 'ctx', split_axis=0, concat_axis=0, tiled=True)  10.7 us
    all_to_all x1, waiting for transfers between devices, body(): lax.all_to_all(dsc, 'ctx', split_axis=0, concat_axis=0, axis_index_groups...  6.06 us
    all_to_all x1, starting transfers between devices, body(): home = lax.all_to_all(back, 'ctx', split_axis=0, concat_axis=0, tiled=True)  5.86 us
    all_to_all x1, starting transfers between devices, body(): lax.all_to_all(dsc, 'ctx', split_axis=0, concat_axis=0, axis_index_groups...  4.53 us
    pallas_call x1, Pallas kernels, body(): pl.pallas_call(stats_kernel, out_shape=(jax.ShapeDtypeStruct((nctx // 2,...  3.29 us
    pallas_call x1, Pallas kernels, body(): pl.pallas_call(grads_kernel, out_shape=(jax.ShapeDtypeStruct((nctx, slots...  2.93 us
  transfers between devices with their start and end apart: 7, of which 4 were waited for; matrix products, arithmetic and copies ran while one was open for 0% of the time, Pallas kernels for 3%

profile of v7, /device:TPU:2, one launch (start us, length us, event | category | flops | bytes accessed | tf_op | source)
XLA Modules:
  0.0 96.1 jit_solution(17338618258436101079)
XLA Ops:
  0.6 2.8 %pack.1 = bf16[64,40,128]{2,1,0:T(8,128)(2,1)} custom-call(s32[1]{0:T(128)} %bitcast.1.here_ref, s32[1,1024]{1,0:T(1,128)} %places_ref.1, f32[1,128]{1,0:T(1,128)} %logit_ref.1, bf16[128,2048]{1,0:T(8,128)(2,1)} %bitcast.16, bf16[128,2048]{1,0:T(8,128)(2,1)} %bitcast.17, bf16[128,2048]{1,0:T(8,128)(2,1)} %bitcast.18, bf16[128,2048]{1,0:T(8,128)(2,1)} %bitcast.13), custom_call_target="tpu_custom_call" | custom-call | tf_op jit(solution)/shard_map/pack/pallas_call | solution.py:292
  3.5 0.0 copy-start.1
  3.5 10.7 %all-to-all-start = ((bf16[64,40,128]{2,1,0:T(8,128)(2,1)}), bf16[64,40,128]{2,1,0:T(8,128)(2,1)S(1)}, u32[]{:S(2)}, u32[]{:S(2)}) async-start(bf16[64,40,128]{2,1,0:T(8,128)(2,1)} %pack.1), calls=%async_computation | async-start | bytes 1310720 | tf_op jit(solution)/shard_map/all_to_all | solution.py:306
  14.2 0.2 convert_reduce_fusion.before_ref
  14.4 0.0 copy-start.2
  14.4 20.1 %all-to-all-done.in_ref = bf16[64,40,128]{2,1,0:T(8,128)(2,1)S(1)} async-done(((bf16[64,40,128]{2,1,0:T(8,128)(2,1)}), bf16[64,40,128]{2,1,0:T(8,128)(2,1)S(1)}, u32[]{:S(2)}, u32[]{:S(2)}) %all-to-all-start) | async-done | bytes 655392 | tf_op jit(solution)/shard_map/all_to_all | solution.py:306
  34.5 0.7 compact.1.x0
  35.2 1.3 %collective-permute-start.2 = (bf16[1024,128]{1,0:T(8,128)(2,1)S(1)}, bf16[1024,128]{1,0:T(8,128)(2,1)S(1)}, u32[]{:S(2)}, u32[]{:S(2)}) collective-permute-start(bf16[1024,128]{1,0:T(8,128)(2,1)S(1)} %compact.1.x0), channel_id=1, source_target_pairs={{1,2},{3,0},{5,6},{7,4},{9,10},{11,8},{13,14},{15,12},{17,18},{19,... | collective-permute-start | bytes 786440 | tf_op jit(solution)/shard_map/ppermute | solution.py:319
  36.5 2.5 %collective-permute-start.1 = (bf16[1024,128]{1,0:T(8,128)(2,1)S(1)}, bf16[1024,128]{1,0:T(8,128)(2,1)S(1)}, u32[]{:S(2)}, u32[]{:S(2)}) collective-permute-start(bf16[1024,128]{1,0:T(8,128)(2,1)S(1)} %compact.1.x0), channel_id=1, source_target_pairs={{0,2},{2,0},{4,6},{6,4},{8,10},{10,8},{12,14},{14,12},{16,18},{18,... | collective-permute-start | bytes 786440 | tf_op jit(solution)/shard_map/ppermute | solution.py:318
  39.0 1.9 %collective-permute-start = (bf16[1024,128]{1,0:T(8,128)(2,1)S(1)}, bf16[1024,128]{1,0:T(8,128)(2,1)S(1)}, u32[]{:S(2)}, u32[]{:S(2)}) collective-permute-start(bf16[1024,128]{1,0:T(8,128)(2,1)S(1)} %compact.1.x0), channel_id=1, source_target_pairs={{0,1},{1,0},{2,3},{3,2},{4,5},{5,4},{6,7},{7,6},{8,9},{9,8},{10,11... | collective-permute-start | bytes 786440 | tf_op jit(solution)/shard_map/ppermute | solution.py:320
  40.9 2.9 %collective-permute-done.2.x3 = bf16[1024,128]{1,0:T(8,128)(2,1)S(1)} collective-permute-done((bf16[1024,128]{1,0:T(8,128)(2,1)S(1)}, bf16[1024,128]{1,0:T(8,128)(2,1)S(1)}, u32[]{:S(2)}, u32[]{:S(2)}) %collective-permute-start.2) | collective-permute-done | bytes 262176 | tf_op jit(solution)/shard_map/ppermute | solution.py:319
  43.8 1.9 %collective-permute-done.1.x2 = bf16[1024,128]{1,0:T(8,128)(2,1)S(1)} collective-permute-done((bf16[1024,128]{1,0:T(8,128)(2,1)S(1)}, bf16[1024,128]{1,0:T(8,128)(2,1)S(1)}, u32[]{:S(2)}, u32[]{:S(2)}) %collective-permute-start.1) | collective-permute-done | bytes 262176 | tf_op jit(solution)/shard_map/ppermute | solution.py:318
  45.7 0.0 collective-permute-done.x1
  45.7 3.3 %stats.1 = (f32[32,1,128]{2,1,0:T(1,128)}, bf16[128,1024]{1,0:T(8,128)(2,1)S(1)}, f32[1,1024]{1,0:T(1,128)S(1)}, f32[1,1024]{1,0:T(1,128)S(1)}, bf16[2,1024,128]{2,1,0:T(8,128)(2,1)S(1)}) custom-call(s32[1]{0:T(128)} %bitcast.1.here_ref, f32[16]{0:T(128)S(1)} %copy-done.2, bf16[1024,128]{1,0:T(8,128)(2,1)S(1)} %compact.1.x0, ...), custom_call_target="tpu_custom_call" | custom-call | tf_op jit(solution)/shard_map/stats/pallas_call | solution.py:328
  49.0 1.3 %collective-permute-start.3 = (bf16[2,1024,128]{2,1,0:T(8,128)(2,1)S(1)}, bf16[2,1024,128]{2,1,0:T(8,128)(2,1)S(1)}, u32[]{:S(2)}, u32[]{:S(2)}) collective-permute-start(bf16[2,1024,128]{2,1,0:T(8,128)(2,1)S(1)} %get-tuple-element.24), channel_id=1, source_target_pairs={{0,1},{2,3},{4,5},{6,7},{8,9},{10,11},{12,13},{14,15},{16,17},{18,... | collective-permute-start | bytes 1572872 | tf_op jit(solution)/shard_map/ppermute | solution.py:343
  50.3 4.5 %all-to-all-start.1 = ((f32[32,1,128]{2,1,0:T(1,128)}), f32[32,1,128]{2,1,0:T(1,128)S(1)}, u32[]{:S(2)}, u32[]{:S(2)}) async-start(f32[32,1,128]{2,1,0:T(1,128)} %get-tuple-element.32), calls=%async_computation.1 | async-start | bytes 32768 | tf_op jit(solution)/shard_map/all_to_all | solution.py:366
  54.9 0.0 copy-start.3
  54.9 0.6 copy-done.3
  55.5 2.9 %grads.1 = (bf16[64,40,128]{2,1,0:T(8,128)(2,1)}, bf16[128,40]{1,0:T(8,128)(2,1)S(1)}, f32[128,256]{1,0:T(8,128)S(1)}, f32[1,128]{1,0:T(1,128)S(1)}) custom-call(s32[64]{0:T(128)S(1)} %convert_reduce_fusion.before_ref, s32[1]{0:T(128)} %bitcast.1.here_ref, f32[16]{0:T(128)S(1)} %copy-done.2, bf16[1024,128]{1,0:T(8,128)(2,1)S(1)} %compact.1.x0, ...), custom_call_target="tpu_custom_call" | custom-call | tf_op jit(solution)/shard_map/grads/pallas_call | solution.py:344
  58.4 6.1 %all-to-all-done.1 = f32[32,1,128]{2,1,0:T(1,128)S(1)} async-done(((f32[32,1,128]{2,1,0:T(1,128)}), f32[32,1,128]{2,1,0:T(1,128)S(1)}, u32[]{:S(2)}, u32[]{:S(2)}) %all-to-all-start.1) | async-done | bytes 16416 | tf_op jit(solution)/shard_map/all_to_all | solution.py:366
  64.5 5.9 %all-to-all-start.2 = ((bf16[64,40,128]{2,1,0:T(8,128)(2,1)}), bf16[64,40,128]{2,1,0:T(8,128)(2,1)S(1)}, u32[]{:S(2)}, u32[]{:S(2)}) async-start(bf16[64,40,128]{2,1,0:T(8,128)(2,1)} %get-tuple-element.33), calls=%async_computation.2 | async-start | bytes 1310720 | tf_op jit(solution)/shard_map/all_to_all | solution.py:375
  70.4 0.1 reduce_sum.21
  70.4 23.7 %psum.7 = f32[1,16]{1,0:T(1,128)} all-reduce(f32[1,16]{1,0:T(1,128)S(1)} %bitcast.19), channel_id=1, replica_groups=mesh['dp'=8,'ctx'=64] {'dp'}, use_global_device_ids=true, to_apply=%region_2.0 | all-reduce | flops 16 | bytes 128 | tf_op jit(solution)/shard_map/psum | solution.py:376
  94.1 2.0 %place.1 = (bf16[128,2048]{1,0:T(8,128)(2,1)}, bf16[128,2048]{1,0:T(8,128)(2,1)}, bf16[128,2048]{1,0:T(8,128)(2,1)}, bf16[128,2048]{1,0:T(8,128)(2,1)}, f32[1,128]{1,0:T(1,128)}) custom-call(bf16[128,40]{1,0:T(8,128)(2,1)S(1)} %get-tuple-element.28.spread_ref, f32[128,256]{1,0:T(8,128)S(1)} %get-tuple-element.29.gate_ref, ...), custom_call_target="tpu_custom_call" | custom-call | tf_op jit(solution)/shard_map/place/pallas_call | solution.py:378
  (7 shorter events, 0.0 us)
Async XLA Ops:
  3.5 10.7 %copy-start.1 = (s32[1,1024]{1,0:T(1,128)S(1)}, s32[1,1024]{1,0:T(1,128)}, u32[]{:S(2)}) copy-start(s32[1,1024]{1,0:T(1,128)} %places_ref.1) | copy-start | bytes 12292
  3.5 31.0 %all-to-all-start = ((bf16[64,40,128]{2,1,0:T(8,128)(2,1)}), bf16[64,40,128]{2,1,0:T(8,128)(2,1)S(1)}, u32[]{:S(2)}, u32[]{:S(2)}) async-start(bf16[64,40,128]{2,1,0:T(8,128)(2,1)} %pack.1), calls=%async_computation | async-start | bytes 1310720 | tf_op jit(solution)/shard_map/all_to_all | solution.py:306
  14.4 31.3 %copy-start.2 = (f32[16]{0:T(128)S(1)}, f32[16]{0:T(128)}, u32[]{:S(2)}) copy-start(f32[16]{0:T(128)} %scale_ref.3) | copy-start | bytes 196
  35.2 8.6 %collective-permute-start.2 = (bf16[1024,128]{1,0:T(8,128)(2,1)S(1)}, bf16[1024,128]{1,0:T(8,128)(2,1)S(1)}, u32[]{:S(2)}, u32[]{:S(2)}) collective-permute-start(bf16[1024,128]{1,0:T(8,128)(2,1)S(1)} %compact.1.x0), channel_id=1, source_target_pairs={{1,2},{3,0},{5,6},{7,4},{9,10},{11,8},{13,14},{15,12},{17,18},{19,... | collective-permute-start | bytes 786440 | tf_op jit(solution)/shard_map/ppermute | solution.py:319
  36.5 9.2 %collective-permute-start.1 = (bf16[1024,128]{1,0:T(8,128)(2,1)S(1)}, bf16[1024,128]{1,0:T(8,128)(2,1)S(1)}, u32[]{:S(2)}, u32[]{:S(2)}) collective-permute-start(bf16[1024,128]{1,0:T(8,128)(2,1)S(1)} %compact.1.x0), channel_id=1, source_target_pairs={{0,2},{2,0},{4,6},{6,4},{8,10},{10,8},{12,14},{14,12},{16,18},{18,... | collective-permute-start | bytes 786440 | tf_op jit(solution)/shard_map/ppermute | solution.py:318
  39.0 6.7 %collective-permute-start = (bf16[1024,128]{1,0:T(8,128)(2,1)S(1)}, bf16[1024,128]{1,0:T(8,128)(2,1)S(1)}, u32[]{:S(2)}, u32[]{:S(2)}) collective-permute-start(bf16[1024,128]{1,0:T(8,128)(2,1)S(1)} %compact.1.x0), channel_id=1, source_target_pairs={{0,1},{1,0},{2,3},{3,2},{4,5},{5,4},{6,7},{7,6},{8,9},{9,8},{10,11... | collective-permute-start | bytes 786440 | tf_op jit(solution)/shard_map/ppermute | solution.py:320
  49.0 5.9 %collective-permute-start.3 = (bf16[2,1024,128]{2,1,0:T(8,128)(2,1)S(1)}, bf16[2,1024,128]{2,1,0:T(8,128)(2,1)S(1)}, u32[]{:S(2)}, u32[]{:S(2)}) collective-permute-start(bf16[2,1024,128]{2,1,0:T(8,128)(2,1)S(1)} %get-tuple-element.24), channel_id=1, source_target_pairs={{0,1},{2,3},{4,5},{6,7},{8,9},{10,11},{12,13},{14,15},{16,17},{18,... | collective-permute-start | bytes 1572872 | tf_op jit(solution)/shard_map/ppermute | solution.py:343
  50.3 14.2 %all-to-all-start.1 = ((f32[32,1,128]{2,1,0:T(1,128)}), f32[32,1,128]{2,1,0:T(1,128)S(1)}, u32[]{:S(2)}, u32[]{:S(2)}) async-start(f32[32,1,128]{2,1,0:T(1,128)} %get-tuple-element.32), calls=%async_computation.1 | async-start | bytes 32768 | tf_op jit(solution)/shard_map/all_to_all | solution.py:366
  54.9 0.7 copy-start.3
  64.5 29.6 %copy-start = (bf16[1,128,2048]{2,1,0:T(8,128)(2,1)S(1)}, bf16[1,128,2048]{2,1,0:T(8,128)(2,1)}, u32[]{:S(2)}) copy-start(bf16[1,128,2048]{2,1,0:T(8,128)(2,1)} %param.13) | copy-start | bytes 1572868
  64.5 29.6 %all-to-all-start.2 = ((bf16[64,40,128]{2,1,0:T(8,128)(2,1)}), bf16[64,40,128]{2,1,0:T(8,128)(2,1)S(1)}, u32[]{:S(2)}, u32[]{:S(2)}) async-start(bf16[64,40,128]{2,1,0:T(8,128)(2,1)} %get-tuple-element.33), calls=%async_computation.2 | async-start | bytes 1310720 | tf_op jit(solution)/shard_map/all_to_all | solution.py:375
